TPU v7x, 32 devices: a whole 2x2x4 slice. The times are simulated.
32 devices in a mesh: dp: 4 (over y, x), ctx: 2 (over core), tensor: 4 (over z).
Axes of the slice: x: 2, y: 2, z: 4, core: 2. Of those that a mesh axis runs over, the one named last changes fastest.
Arguments:
- layer_input: float32 [8, 1024, 768], P('dp', 'ctx'), may hold values from -6 to 6
- segment_ids: int32 [8, 1024], P('dp', 'ctx'), may hold values from 0 to 4, never falling along the last dimension, each value on 1 to 512 neighbouring positions
- mixer_gain: float32 [768], P(('dp', 'ctx')), may hold values from 0.25 to 1.75
- query_weight: float32 [768, 768], P(('dp', 'ctx'), 'tensor'), may hold values from -0.21875 to 0.21875
- key_weight: float32 [768, 768], P(('dp', 'ctx'), 'tensor'), may hold values from -0.21875 to 0.21875
- value_weight: float32 [768, 768], P(('dp', 'ctx'), 'tensor'), may hold values from -0.21875 to 0.21875
- shift_kernel: float32 [4, 768], P(None, ('tensor', 'dp', 'ctx')), may hold values from -3 to 3
- state_decay: float32 [12, 64], P('tensor'), may hold values from 0.95 to 1, as said below
- mixer_weight: float32 [768, 768], P('tensor', ('dp', 'ctx')), may hold values from -0.0017089844 to 0.0017089844
- feed_gain: float32 [768], P(('dp', 'ctx')), may hold values from 0.25 to 1.75
- up_weight: float32 [768, 3072], P(('dp', 'ctx'), 'tensor'), may hold values from -0.21875 to 0.21875
- down_weight: float32 [3072, 768], P('tensor', ('dp', 'ctx')), may hold values from -0.109375 to 0.109375
- cotangent: float32 [8, 1024, 768], P('dp', 'ctx'), may hold values from -6 to 6
Outputs:
- layer_output: float32 [8, 1024, 768], P('dp', 'ctx')
- input_grad: float32 [8, 1024, 768], P('dp', 'ctx')
- mixer_gain_grad: float32 [768], P(('dp', 'ctx'))
- query_weight_grad: float32 [768, 768], P(('dp', 'ctx'), 'tensor')
- key_weight_grad: float32 [768, 768], P(('dp', 'ctx'), 'tensor')
- value_weight_grad: float32 [768, 768], P(('dp', 'ctx'), 'tensor')
- shift_kernel_grad: float32 [4, 768], P(None, ('tensor', 'dp', 'ctx'))
- mixer_weight_grad: float32 [768, 768], P('tensor', ('dp', 'ctx'))
- feed_gain_grad: float32 [768], P(('dp', 'ctx'))
- up_weight_grad: float32 [768, 3072], P(('dp', 'ctx'), 'tensor')
- down_weight_grad: float32 [3072, 768], P('tensor', ('dp', 'ctx'))
Inputs may be any that keep to these rules, and one draw needn't show every extreme that they name: `segment_ids`: along each sequence the numbers never fall; a document is one run of equal numbers. `state_decay`: each decay is exp(-1 / r) for a horizon r of 24 positions or more.
All inputs are finite; a program needn't handle non-finite values.
Results may differ from a plain program's by a relative error of at most 0.0003.
Values sent between devices are 32-bit elements; how exact they have to be, the bound alone decides.
No kernel may reach another device: no remote copies, remote signals or barrier semaphores. Data moves between devices by JAX's collectives and lax.ppermute only.
A program may use at most 128 MiB of HBM per device.

v0:
```python
from functools import partial

import jax
import jax.numpy as jnp
from jax import lax
from jax.sharding import PartitionSpec as P

SUBBLOCK = 64


eps = 1e-05
precise = lax.Precision.HIGHEST


def passed_along(value, axis, steps):
    count = lax.axis_size(axis)
    leading, last = (max(0, -steps), min(count, count - steps))
    return lax.ppermute(value, axis, [(source, source + steps) for source in range(leading, last)])


def carried_in(value, axis, join, neutral, backward):
    count, mine = (lax.axis_size(axis), lax.axis_index(axis))
    pieces = jax.tree.map(lambda part: lax.all_gather(part, axis), value)
    if backward:
        pieces = jax.tree.map(lambda part: part[::-1], pieces)
        mine = count - 1 - mine
    subtotal = jax.tree.map(
        lambda part, zero: jnp.full_like(part, 0) + jnp.asarray(zero, part.dtype), value, neutral
    )

    def step(position, subtotal):
        longer = join(subtotal, jax.tree.map(lambda part: part[position], pieces))
        return jax.tree.map(lambda new, old: jnp.where(position < mine, new, old), longer, subtotal)

    return lax.fori_loop(0, count - 1, step, subtotal)


def normalize(inputs, gain):
    centered = inputs - jnp.mean(inputs, axis=-1, keepdims=True)
    scaled = centered * lax.rsqrt(jnp.mean(centered * centered, axis=-1, keepdims=True) + eps)
    return scaled * gain


def project(left, right):
    return jnp.einsum(
        "btd,df->btf", left, right, precision=precise, preferred_element_type=jnp.float32
    )


def outer_sum(left, right):
    return jnp.einsum(
        "btd,btf->df", left, right, precision=precise, preferred_element_type=jnp.float32
    )


def smooth_gate(inputs):
    return jax.nn.gelu(inputs, approximate=True)


def shift_keys(extended, kernel, seg_ext):
    taps = kernel.shape[0]
    length = extended.shape[1] - taps + 1
    current = seg_ext[:, taps - 1 :]
    summed = jnp.zeros((extended.shape[0], length, extended.shape[2]), jnp.float32)
    for offset in range(taps):
        begin = taps - 1 - offset
        joined = (seg_ext[:, begin : begin + length] == current).astype(jnp.float32)
        summed = summed + kernel[offset] * extended[:, begin : begin + length] * joined[:, :, None]
    return summed


def compose(earlier, later):
    return (earlier[0] * later[0], later[0][..., None] * earlier[1] + later[1])


def geometry(segments, before_block, log_decay):
    rows, length = segments.shape
    pieces = length // SUBBLOCK
    grouped = segments.reshape(rows, pieces, SUBBLOCK)
    before = jnp.concatenate([before_block[:, None], grouped[:, :-1, -1]], axis=1)
    living = (grouped == before[:, :, None]).astype(jnp.float32)
    retained = (grouped == grouped[:, :, -1:]).astype(jnp.float32)
    position = jnp.arange(SUBBLOCK, dtype=jnp.float32)
    causal = position[:, None] >= position[None, :]
    allowed = jnp.logical_and(grouped[:, :, :, None] == grouped[:, :, None, :], causal).astype(
        jnp.float32
    )
    growing = jnp.exp(position[:, None, None] * log_decay)
    shrinking = jnp.exp(-position[:, None, None] * log_decay)
    step_in = growing * jnp.exp(log_decay)
    closing = jnp.exp((SUBBLOCK - 1.0 - position)[:, None, None] * log_decay)
    whole_decay = jnp.exp(SUBBLOCK * log_decay)[None, None] * living[:, :, -1][:, :, None, None]
    running = jnp.ones((rows,) + log_decay.shape, jnp.float32)
    carried = []
    for index in range(pieces):
        carried.append(running)
        running = running * whole_decay[:, index]
    return (
        living,
        retained,
        allowed,
        growing,
        shrinking,
        step_in,
        closing,
        whole_decay,
        jnp.stack(carried, axis=1),
        running,
    )


def local_part(queries, shifted, values, shape_info):
    (
        living,
        retained,
        allowed,
        growing,
        shrinking,
        step_in,
        closing,
        whole_decay,
        carried,
        block_decay,
    ) = shape_info
    scores = jnp.einsum(
        "bncgi,bnsgi->bngcs", queries * growing, shifted * shrinking, precision=precise
    )
    scores = scores * allowed[:, :, None]
    within = jnp.einsum("bngcs,bnsgj->bncgj", scores, values, precision=precise)
    update = jnp.einsum(
        "bncgi,bncgj->bngij",
        shifted * closing * retained[..., None, None],
        values,
        precision=precise,
    )
    running = jnp.zeros_like(update[:, 0])
    starts = []
    for index in range(update.shape[1]):
        starts.append(running)
        running = whole_decay[:, index][..., None] * running + update[:, index]
    return (within, jnp.stack(starts, axis=1), running)


def across(queries, starts, state_in, shape_info):
    (
        living,
        retained,
        allowed,
        growing,
        shrinking,
        step_in,
        closing,
        whole_decay,
        carried,
        block_decay,
    ) = shape_info
    entries = starts + carried[..., None] * state_in[:, None]
    weighted = queries * step_in * living[..., None, None]
    return jnp.einsum("bncgi,bngij->bncgj", weighted, entries, precision=precise)


def on_device(
    layer_input,
    segment_ids,
    mixer_gain,
    query_weight,
    key_weight,
    value_weight,
    shift_kernel,
    state_decay,
    mixer_weight,
    feed_gain,
    up_weight,
    down_weight,
    cotangent,
):
    (
        mixer_gain_all,
        query_all,
        key_all,
        value_all,
        kernel_all,
        mixer_all,
        feed_gain_all,
        up_all,
        down_all,
    ) = (
        lax.all_gather(mixer_gain, ("dp", "ctx"), axis=0, tiled=True),
        lax.all_gather(query_weight, ("dp", "ctx"), axis=0, tiled=True),
        lax.all_gather(key_weight, ("dp", "ctx"), axis=0, tiled=True),
        lax.all_gather(value_weight, ("dp", "ctx"), axis=0, tiled=True),
        lax.all_gather(shift_kernel, ("dp", "ctx"), axis=1, tiled=True),
        lax.all_gather(mixer_weight, ("dp", "ctx"), axis=1, tiled=True),
        lax.all_gather(feed_gain, ("dp", "ctx"), axis=0, tiled=True),
        lax.all_gather(up_weight, ("dp", "ctx"), axis=0, tiled=True),
        lax.all_gather(down_weight, ("dp", "ctx"), axis=1, tiled=True),
    )
    heads, width = state_decay.shape
    log_decay = jnp.log(state_decay)
    taps = kernel_all.shape[0]
    rows, length, model = layer_input.shape
    pieces = length // SUBBLOCK
    features = heads * width
    seg_float = segment_ids.astype(jnp.float32)
    joint_weight = jnp.concatenate([query_all, key_all, value_all], axis=1)
    normed = normalize(layer_input, mixer_gain_all)
    projected = project(normed, joint_weight)
    queries = projected[:, :, :features]
    keys_raw = projected[:, :, features : 2 * features]
    values = projected[:, :, 2 * features :]
    tail_keys, tail_segs = passed_along(
        (keys_raw[:, length - taps + 1 :], seg_float[:, length - taps + 1 :]), "ctx", 1
    )
    extended = jnp.concatenate([tail_keys, keys_raw], axis=1)
    seg_ext = jnp.concatenate([tail_segs, seg_float], axis=1)
    shift_fixed = partial(shift_keys, seg_ext=seg_ext)
    shifted = shift_fixed(extended, kernel_all)
    info = geometry(seg_float, tail_segs[:, -1], log_decay)
    block_decay = info[-1]
    head_q = queries.reshape(rows, pieces, SUBBLOCK, heads, width)
    head_k = shifted.reshape(rows, pieces, SUBBLOCK, heads, width)
    head_v = values.reshape(rows, pieces, SUBBLOCK, heads, width)
    within, starts, local_end = local_part(head_q, head_k, head_v, info)
    identity = (jnp.ones_like(block_decay), jnp.zeros_like(local_end))
    state_in = carried_in((block_decay, local_end), "ctx", compose, identity, False)[1]
    mixed = (within + across(head_q, starts, state_in, info)).reshape(rows, length, features)
    branch = lax.psum(project(mixed, mixer_all), "tensor")
    resid = layer_input + branch
    normed_feed = normalize(resid, feed_gain_all)
    pre_act = project(normed_feed, up_all)
    activated, gelu_back = jax.vjp(smooth_gate, pre_act)
    feed = lax.psum(project(activated, down_all), "tensor")
    layer_output = resid + feed
    act_grad = project(cotangent, down_all.T)
    down_grad = outer_sum(activated, cotangent)
    (pre_grad,) = gelu_back(act_grad)
    up_grad = outer_sum(normed_feed, pre_grad)
    feed_normed_grad = lax.psum(project(pre_grad, up_all.T), "tensor")
    _, feed_norm_back = jax.vjp(normalize, resid, feed_gain_all)
    resid_ln_grad, feed_gain_grad = feed_norm_back(feed_normed_grad)
    resid_grad = cotangent + resid_ln_grad
    mixed_grad = project(resid_grad, mixer_all.T)
    mixer_weight_grad = outer_sum(mixed, resid_grad)
    head_du = mixed_grad.reshape(rows, pieces, SUBBLOCK, heads, width)
    (
        living,
        retained,
        allowed,
        growing,
        shrinking,
        step_in,
        closing,
        whole_decay,
        carried,
        block_decay,
    ) = info
    own_grad = jnp.einsum(
        "bncgi,bncgj,bngi->bgij",
        head_q * step_in * living[..., None, None],
        head_du,
        carried,
        precision=precise,
    )
    identity_grad = (jnp.ones_like(block_decay), jnp.zeros_like(own_grad))
    after = carried_in((block_decay, own_grad), "ctx", compose, identity_grad, True)[1]

    def mixer_full(query_in, key_in, value_in, entering):
        inner, begins, ending = local_part(query_in, key_in, value_in, info)
        output = inner + across(query_in, begins, entering, info)
        return (output, ending + block_decay[..., None] * entering)

    _, mixer_vjp = jax.vjp(mixer_full, head_q, head_k, head_v, state_in)
    query_act_grad, shifted_grad, value_act_grad, _ = mixer_vjp((head_du, after))
    _, shift_back = jax.vjp(shift_fixed, extended, kernel_all)
    ext_grad, kernel_grad = shift_back(shifted_grad.reshape(rows, length, features))
    returned = passed_along(ext_grad[:, : taps - 1], "ctx", -1)
    key_act_grad = ext_grad[:, taps - 1 :] + jnp.pad(
        returned, ((0, 0), (length - taps + 1, 0), (0, 0))
    )
    joint_grad = jnp.concatenate(
        [
            query_act_grad.reshape(rows, length, features),
            key_act_grad,
            value_act_grad.reshape(rows, length, features),
        ],
        axis=2,
    )
    joint_weight_grad = outer_sum(normed, joint_grad)
    normed_grad = lax.psum(project(joint_grad, joint_weight.T), "tensor")
    _, mixer_norm_back = jax.vjp(normalize, layer_input, mixer_gain_all)
    input_ln_grad, mixer_gain_grad = mixer_norm_back(normed_grad)
    input_grad = resid_grad + input_ln_grad
    query_grad = joint_weight_grad[:, :features]
    key_grad = joint_weight_grad[:, features : 2 * features]
    value_grad = joint_weight_grad[:, 2 * features :]
    all_parts = tuple(
        (
            lax.psum_scatter(mixer_gain_grad, ("dp", "ctx"), scatter_dimension=0, tiled=True),
            lax.psum_scatter(query_grad, ("dp", "ctx"), scatter_dimension=0, tiled=True),
            lax.psum_scatter(key_grad, ("dp", "ctx"), scatter_dimension=0, tiled=True),
            lax.psum_scatter(value_grad, ("dp", "ctx"), scatter_dimension=0, tiled=True),
            lax.psum_scatter(kernel_grad, ("dp", "ctx"), scatter_dimension=1, tiled=True),
            lax.psum_scatter(mixer_weight_grad, ("dp", "ctx"), scatter_dimension=1, tiled=True),
            lax.psum_scatter(feed_gain_grad, ("dp", "ctx"), scatter_dimension=0, tiled=True),
            lax.psum_scatter(up_grad, ("dp", "ctx"), scatter_dimension=0, tiled=True),
            lax.psum_scatter(down_grad, ("dp", "ctx"), scatter_dimension=1, tiled=True),
        )
    )
    return (layer_output, input_grad) + all_parts


def solution(mesh):
    return jax.shard_map(
        on_device,
        mesh=mesh,
        in_specs=(
            P("dp", "ctx", None),
            P("dp", "ctx"),
            P(("dp", "ctx")),
            P(("dp", "ctx"), "tensor"),
            P(("dp", "ctx"), "tensor"),
            P(("dp", "ctx"), "tensor"),
            P(None, ("tensor", "dp", "ctx")),
            P("tensor", None),
            P("tensor", ("dp", "ctx")),
            P(("dp", "ctx")),
            P(("dp", "ctx"), "tensor"),
            P("tensor", ("dp", "ctx")),
            P("dp", "ctx", None),
        ),
        out_specs=(
            P("dp", "ctx", None),
            P("dp", "ctx", None),
            P(("dp", "ctx")),
            P(("dp", "ctx"), "tensor"),
            P(("dp", "ctx"), "tensor"),
            P(("dp", "ctx"), "tensor"),
            P(None, ("tensor", "dp", "ctx")),
            P("tensor", ("dp", "ctx")),
            P(("dp", "ctx")),
            P(("dp", "ctx"), "tensor"),
            P("tensor", ("dp", "ctx")),
        ),
        check_vma=False,
    )
```

profile of v0, /device:TPU:0, one launch (start us, length us, event | category | flops | bytes accessed | tf_op | source)
XLA Modules:
  0.0 847.0 jit_solution(150971598829292166)
XLA Ops:
  9.6 2.9 collective-permute-start.1
  15.6 12.3 %all_gather.44 = f32[768,192]{1,0:T(8,128)} all-gather(f32[96,192]{1,0:T(8,128)S(1)} %copy-done.46), channel_id=1, replica_groups=mesh['dp'=4,'ctx'=2,'tensor'=4] {'dp','ctx'}, dimensions={0}, use_global_device_ids=true | all-gather | bytes 663552 | tf_op jit(solution)/shard_map/all_gather | solution.py:189
  30.2 11.3 %all_gather.45 = f32[768,192]{1,0:T(8,128)} all-gather(f32[96,192]{1,0:T(8,128)S(1)} %copy-done.47), channel_id=1, replica_groups=mesh['dp'=4,'ctx'=2,'tensor'=4] {'dp','ctx'}, dimensions={0}, use_global_device_ids=true | all-gather | bytes 663552 | tf_op jit(solution)/shard_map/all_gather | solution.py:190
  43.7 10.9 %all_gather.46 = f32[768,192]{1,0:T(8,128)} all-gather(f32[96,192]{1,0:T(8,128)S(1)} %copy-done.48), channel_id=1, replica_groups=mesh['dp'=4,'ctx'=2,'tensor'=4] {'dp','ctx'}, dimensions={0}, use_global_device_ids=true | all-gather | bytes 663552 | tf_op jit(solution)/shard_map/all_gather | solution.py:191
  58.5 14.0 %all-reduce.23 = (f32[768]{0:T(1024)S(1)}, f32[768]{0:T(1024)}) all-reduce(f32[768]{0:T(1024)S(1)} %dynamic-update-slice, f32[768]{0:T(1024)S(1)} %dynamic-update-slice.1), channel_id=1, replica_groups=mesh['dp'=4,'ctx'=2,'tensor'=4] {'dp','ctx'}, use_global_device_ids=true, to_apply=%add.17 | all-reduce | flops 1536 | bytes 12288
  72.6 7.6 fusion.12
  86.4 3.2 fusion.131
  92.0 8.8 %all-gather.2 = f32[8,24,4]{1,2,0:T(4,128)S(1)} all-gather(f32[1,24,4]{1,2,0:T(4,128)S(1)} %bitcast.268), channel_id=1, replica_groups=mesh['dp'=4,'ctx'=2,'tensor'=4] {'dp','ctx'}, dimensions={0}, use_global_device_ids=true | all-gather | bytes 3456 | tf_op jit(solution)/shard_map/all_gather | solution.py:192
  104.1 3.1 copy.384
  110.6 3.0 copy.374
  117.9 11.7 %all_gather.50 = f32[192,768]{0,1:T(8,128)} all-gather(f32[192,96]{0,1:T(8,128)} %copy.413), channel_id=1, replica_groups=mesh['dp'=4,'ctx'=2,'tensor'=4] {'dp','ctx'}, dimensions={1}, use_global_device_ids=true | all-gather | bytes 663552 | tf_op jit(solution)/shard_map/all_gather | solution.py:193
  141.8 3.8 multiply_bitcast_fusion
  147.3 3.0 multiply_add_fusion.1
  152.8 3.8 fusion.74
  163.6 2.7 fusion.136
  166.7 3.2 add_bitcast_fusion.1
  171.9 2.8 reshape.414
  174.7 8.1 fusion.84
  184.1 120.3 %all-reduce.29.cloned.1.call-done = f32[2,512,768]{2,1,0:T(8,128)} async-done(((f32[2,512,768]{2,1,0:T(8,128)}), f32[2,512,768]{2,1,0:T(8,128)}) %all-reduce.29.cloned.1.call-update) | async-done | bytes 3145744 | tf_op jit(solution)/shard_map/psum | solution.py:227
  310.0 11.9 %fusion.8 = f32[2,512,768]{2,1,0:T(8,128)} fusion(f32[768,768]{1,0:T(8,128)} %all-gather.6.cloned.1.call-done, f32[2,512,768]{2,1,0:T(8,128)} %copy-done.1, f32[768]{0:T(1024)} %get-tuple-element.125, f32[2,512]{1,0:T(2,128)} %fusion.117, f32[2,512]{1,0:T(2,128)S(1)} %broadcast_multiply_fusion.2), kind=kOutput, calls=%fused_computation.21 | convolution fusion | flops 7250116608 | bytes 8662016 | tf_op jit(solution)/shard_map/btd,df->btf/dot_general | solution.py:45
  322.0 12.8 %fusion.5 = f32[2,512,768]{2,1,0:T(8,128)S(1)} fusion(f32[2,512,768]{2,1,0:T(8,128)} %fusion.8, f32[2,512,768]{2,1,0:T(8,128)} %param.25, f32[768,768]{0,1:T(8,128)} %all-gather.8.cloned.1.call-done), kind=kOutput, calls=%fused_computation.9 | convolution fusion | flops 7262699520 | bytes 11796480 | tf_op jit(solution)/shard_map/btd,df->btf/dot_general | solution.py:45
  336.6 9.5 %fusion.22 = f32[2,512,768]{2,1,0:T(8,128)} fusion(f32[2,512,768]{2,1,0:T(8,128)S(1)} %fusion.5, f32[768,768]{1,0:T(8,128)S(1)} %copy-done.31), kind=kOutput, calls=%fused_computation.36 | convolution fusion | flops 7247757312 | bytes 8650752 | tf_op jit(solution)/shard_map/btd,df->btf/dot_general | solution.py:45
  347.4 12.2 %fusion.20 = f32[2,512,768]{2,1,0:T(8,128)} fusion(f32[768,768]{0,1:T(8,128)} %all-gather.8.cloned.1.call-done, f32[2,512,768]{2,1,0:T(8,128)} %fusion.8), kind=kOutput, calls=%fused_computation.34 | convolution fusion | flops 7254048768 | bytes 8650752 | tf_op jit(solution)/shard_map/btd,df->btf/dot_general | solution.py:45
  359.6 106.7 %all-reduce.31.cloned.1.call-done = f32[2,512,768]{2,1,0:T(8,128)} async-done(((f32[2,512,768]{2,1,0:T(8,128)}), f32[2,512,768]{2,1,0:T(8,128)}) %all-reduce.31.cloned.1.call-update) | async-done | bytes 3145744 | tf_op jit(solution)/shard_map/psum | solution.py:238
  466.3 3.6 multiply_reduce_fusion.3
  476.0 6.1 convolution_bitcast_fusion.1
  482.1 6.4 fusion.82
  488.5 2.8 reshape.415
  491.4 6.4 fusion.64
  497.8 3.9 convolution_multiply_fusion
  501.7 2.9 fusion.36
  504.7 2.9 fusion.75
  507.5 12.5 %all-gather.1 = f32[4,3,64,64]{3,2,1,0:T(8,128)S(1)} all-gather(f32[2,3,64,64]{3,2,1,0:T(8,128)S(1)} %fusion.75), channel_id=3, replica_groups=mesh['dp'=4,'ctx'=2,'tensor'=4] {'ctx'}, dimensions={0}, use_global_device_ids=true | all-gather | bytes 294912 | tf_op jit(solution)/shard_map/all_gather | solution.py:23
  520.6 3.9 fusion.70
  524.5 4.1 fusion.68
  528.7 6.5 fusion.41
  535.3 2.9 fusion.35
  543.0 4.2 multiply_reduce_fusion.9
  549.2 3.1 add_bitcast_fusion
  554.1 3.0 copy.422
  559.7 3.5 copy.444
  568.4 10.8 %fusion.34 = f32[2,512,768]{2,1,0:T(8,128)} fusion(f32[2,512,192]{1,2,0:T(8,128)} %reshape.418, f32[2,512,192]{1,2,0:T(8,128)S(1)} %slice_add_fusion, f32[2,512,192]{1,2,0:T(8,128)} %reshape.416, f32[768,192]{0,1:T(8,128)S(1)} %copy-done.34, f32[768,192]{0,1:T(8,128)S(1)} %copy-done.33, f32[768,192]{0,1:T(8,128)S(1)} %copy-done.32), kind=kOutput, calls=%fused_computation.46 | convolution fusion | flops 5437882368 | bytes 7274496 | tf_op jit(solution)/shard_map/btd,df->btf/dot_general | solution.py:45
  579.9 12.0 %fusion.31 = f32[768,768]{1,0:T(8,128)} fusion(f32[2,512,768]{2,1,0:T(8,128)} %copy-done.29, f32[2,512,768]{2,1,0:T(8,128)} %copy-done.1, f32[768]{0:T(1024)S(1)} %copy-done.73, f32[2,512]{1,0:T(2,128)S(1)} %copy-done.67, f32[2,512]{1,0:T(2,128)S(1)} %broadcast_multiply_fusion.2), kind=kOutput, calls=%fused_computation.45 | convolution fusion | flops 7250116608 | bytes 8662016 | tf_op jit(solution)/shard_map/btd,btf->df/dot_general | solution.py:51
  592.0 13.2 %convolution_bitcast_fusion = f32[768,768]{0,1:T(8,128)} fusion(f32[2,512,768]{2,1,0:T(8,128)} %param.25, f32[2,512,768]{2,1,0:T(8,128)} %fusion.8), kind=kOutput, calls=%fused_computation.44 | convolution fusion | flops 7254048768 | bytes 8650752 | tf_op jit(solution)/shard_map/btd,btf->df/dot_general | solution.py:51
  605.9 8.3 fusion.58
  625.3 176.9 %all-reduce.33.cloned.1.call-done = (f32[2,512,768]{2,1,0:T(8,128)}, f32[2,512,768]{2,1,0:T(8,128)}) async-done(((f32[2,512,768]{2,1,0:T(8,128)}, f32[2,512,768]{2,1,0:T(8,128)}), (f32[2,512,768]{2,1,0:T(8,128)}, f32[2,512,768]{2,1,0:T(8,128)})) %all-reduce.33.cloned.1.call-update) | async-done | bytes 6291472 | tf_op jit(solution)/shard_map/psum | solution.py:232
  806.5 24.0 %all-reduce.22 = (f32[768]{0:T(1024)S(1)}, f32[4,192]{1,0:T(4,128)S(1)}, f32[768]{0:T(1024)S(1)}) all-reduce(f32[768]{0:T(1024)S(1)} %get-tuple-element.115, f32[4,192]{1,0:T(4,128)S(1)} %pad_add_fusion.3, f32[768]{0:T(1024)S(1)} %copy-done.82), channel_id=4, replica_groups=mesh['dp'=4,'ctx'=2,'tensor'=4] {'dp','ctx'}, use_global_device_ids=true, to_apply=%region_13.14.clone | all-reduce | flops 2304 | bytes 18432
  831.7 5.1 add.322
  (343 shorter events, 109.7 us)
Async XLA Ops:
  8.0 6.6 copy-start
  8.0 296.4 %all-reduce.29.cloned.1.call-start = ((), (), s32[]{:S(2)}) async-start(), calls=%async_computation.6 | async-start | bytes 6291456 | tf_op jit(solution)/shard_map/psum | solution.py:227
  9.6 120.1 %collective-permute-start.1 = (f32[2,3]{1,0:T(2,128)}, f32[2,3]{1,0:T(2,128)}, u32[]{:S(2)}, u32[]{:S(2)}) collective-permute-start(f32[2,3]{1,0:T(2,128)} %slice.211), channel_id=1, source_target_pairs={{0,4},{1,5},{2,6},{3,7},{8,12},{9,13},{10,14},{11,15},{16,20},{17,... | collective-permute-start | bytes 80 | tf_op jit(solution)/shard_map/ppermute | solution.py:18
  15.0 15.2 %copy-start.47 = (f32[96,192]{1,0:T(8,128)S(1)}, f32[96,192]{1,0:T(8,128)}, u32[]{:S(2)}) copy-start(f32[96,192]{1,0:T(8,128)} %param.17) | copy-start | bytes 221188
  15.6 56.9 %copy-start.60 = (f32[2,512]{1,0:T(2,128)}, f32[2,512]{1,0:T(2,128)S(1)}, u32[]{:S(2)}) copy-start(f32[2,512]{1,0:T(2,128)S(1)} %fusion.116) | copy-start | bytes 12292
  27.9 15.8 %copy-start.48 = (f32[96,192]{1,0:T(8,128)S(1)}, f32[96,192]{1,0:T(8,128)}, u32[]{:S(2)}) copy-start(f32[96,192]{1,0:T(8,128)} %param.18) | copy-start | bytes 221188
  41.5 15.3 %copy-start.96 = (u32[32]{0:T(128)S(1)}, u32[32]{0:T(128)}, u32[]{:S(2)}) copy-start(u32[32]{0:T(128)} %constant.102) | copy-start | bytes 388
  41.5 16.6 %copy-start.98 = (f32[96]{0:T(128)S(1)}, f32[96]{0:T(128)}, u32[]{:S(2)}) copy-start(f32[96]{0:T(128)} %param.15) | copy-start | bytes 1156
  41.5 16.9 %copy-start.99 = (f32[96]{0:T(128)S(1)}, f32[96]{0:T(128)}, u32[]{:S(2)}) copy-start(f32[96]{0:T(128)} %param.22) | copy-start | bytes 1156
  72.6 7.6 copy-start.62
  82.4 64.8 %collective-permute-start = (f32[2,3,192]{1,2,0:T(8,128)}, f32[2,3,192]{1,2,0:T(8,128)}, u32[]{:S(2)}, u32[]{:S(2)}) collective-permute-start(f32[2,3,192]{1,2,0:T(8,128)} %slice.208), channel_id=1, source_target_pairs={{0,4},{1,5},{2,6},{3,7},{8,12},{9,13},{10,14},{11,15},{16,20},{17,... | collective-permute-start | bytes 13832 | tf_op jit(solution)/shard_map/ppermute | solution.py:18
  86.4 5.7 copy-start.95
  107.9 33.8 %copy-start.39 = (f32[64,3,64]{2,0,1:T(8,128)}, f32[64,3,64]{2,0,1:T(8,128)S(1)}, u32[]{:S(2)}) copy-start(f32[64,3,64]{2,0,1:T(8,128)S(1)} %get-tuple-element.182) | copy-start | bytes 147460
  108.0 44.8 %copy-start.37 = (f32[64,3,64]{0,2,1:T(8,128)}, f32[64,3,64]{0,2,1:T(8,128)S(1)}, u32[]{:S(2)}) copy-start(f32[64,3,64]{0,2,1:T(8,128)S(1)} %copy.382) | copy-start | bytes 147460
  147.1 12.4 %copy-start.52 = (f32[2,3,64]{2,1,0:T(4,128)}, f32[2,3,64]{2,1,0:T(4,128)S(1)}, u32[]{:S(2)}) copy-start(f32[2,3,64]{2,1,0:T(4,128)S(1)} %copy.386) | copy-start | bytes 4612
  147.1 12.7 %copy-start.54 = (f32[2,3,64]{2,1,0:T(4,128)}, f32[2,3,64]{2,1,0:T(4,128)S(1)}, u32[]{:S(2)}) copy-start(f32[2,3,64]{2,1,0:T(4,128)S(1)} %copy.390) | copy-start | bytes 4612
  147.1 13.0 %copy-start.56 = (f32[2,3,64]{2,1,0:T(4,128)}, f32[2,3,64]{2,1,0:T(4,128)S(1)}, u32[]{:S(2)}) copy-start(f32[2,3,64]{2,1,0:T(4,128)S(1)} %copy.394) | copy-start | bytes 4612
  147.2 19.2 %copy-start.58 = (f32[2,3,64]{2,1,0:T(4,128)}, f32[2,3,64]{2,1,0:T(4,128)S(1)}, u32[]{:S(2)}) copy-start(f32[2,3,64]{2,1,0:T(4,128)S(1)} %copy.396) | copy-start | bytes 4612
  147.2 9.4 %copy-start.64 = (f32[2,3,64]{2,1,0:T(4,128)}, f32[2,3,64]{2,1,0:T(4,128)S(1)}, u32[]{:S(2)}) copy-start(f32[2,3,64]{2,1,0:T(4,128)S(1)} %copy.402) | copy-start | bytes 4612
  147.3 5.5 copy-start.49
  182.9 127.2 %all-gather.6.cloned.1.call-start = ((), (), s32[]{:S(2)}) async-start(), calls=%async_computation.7 | async-start | bytes 2654208 | tf_op jit(solution)/shard_map/all_gather | solution.py:195
  183.4 138.5 %all-gather.8.cloned.1.call-start = ((), (), s32[]{:S(2)}) async-start(), calls=%async_computation.8 | async-start | bytes 2654208 | tf_op jit(solution)/shard_map/all_gather | solution.py:196
  184.0 282.3 %all-reduce.31.cloned.1.call-start = ((), (), s32[]{:S(2)}) async-start(), calls=%async_computation.9 | async-start | bytes 6291456 | tf_op jit(solution)/shard_map/psum | solution.py:238
  322.0 14.6 %copy-start.31 = (f32[768,768]{1,0:T(8,128)S(1)}, f32[768,768]{1,0:T(8,128)}, u32[]{:S(2)}) copy-start(f32[768,768]{1,0:T(8,128)} %all-gather.6.cloned.1.call-done) | copy-start | bytes 7077892
  346.1 277.6 %reduce-scatter.26.cloned.1.call-start = ((), (), s32[]{:S(2)}) async-start(), calls=%async_computation.15 | async-start | bytes 884736
  491.3 6.4 copy-start.3
  491.4 6.4 copy-start.13
  491.4 6.4 copy-start.28
  504.6 15.4 %copy-start.53 = (f32[2,3,64]{2,1,0:T(4,128)S(1)}, f32[2,3,64]{2,1,0:T(4,128)}, u32[]{:S(2)}) copy-start(f32[2,3,64]{2,1,0:T(4,128)} %copy-done.52) | copy-start | bytes 4612
  504.6 15.4 %copy-start.55 = (f32[2,3,64]{2,1,0:T(4,128)S(1)}, f32[2,3,64]{2,1,0:T(4,128)}, u32[]{:S(2)}) copy-start(f32[2,3,64]{2,1,0:T(4,128)} %copy-done.54) | copy-start | bytes 4612
  504.6 15.4 %copy-start.57 = (f32[2,3,64]{2,1,0:T(4,128)S(1)}, f32[2,3,64]{2,1,0:T(4,128)}, u32[]{:S(2)}) copy-start(f32[2,3,64]{2,1,0:T(4,128)} %copy-done.56) | copy-start | bytes 4612
  504.6 15.4 %copy-start.59 = (f32[2,3,64]{2,1,0:T(4,128)S(1)}, f32[2,3,64]{2,1,0:T(4,128)}, u32[]{:S(2)}) copy-start(f32[2,3,64]{2,1,0:T(4,128)} %copy-done.58) | copy-start | bytes 4612
  504.6 15.4 %copy-start.65 = (f32[2,3,64]{2,1,0:T(4,128)S(1)}, f32[2,3,64]{2,1,0:T(4,128)}, u32[]{:S(2)}) copy-start(f32[2,3,64]{2,1,0:T(4,128)} %copy-done.64) | copy-start | bytes 4612
  504.6 15.4 %copy-start.83 = (f32[2,3,64]{2,1,0:T(4,128)S(1)}, f32[2,3,64]{2,1,0:T(4,128)}, u32[]{:S(2)}) copy-start(f32[2,3,64]{2,1,0:T(4,128)} %copy.424) | copy-start | bytes 4612
  528.6 273.6 %all-reduce.33.cloned.1.call-start = ((), (), s32[]{:S(2)}) async-start(), calls=%async_computation.16 | async-start | bytes 12582912 | tf_op jit(solution)/shard_map/psum | solution.py:232
  528.7 6.6 copy-start.11
  528.7 6.6 copy-start.20
  528.7 6.6 copy-start.36
  528.7 6.6 copy-start.51
  542.9 6.2 copy-start.35
  547.4 18.5 %collective-permute-start.2 = (f32[2,3,192]{1,2,0:T(8,128)S(1)}, f32[2,3,192]{1,2,0:T(8,128)S(1)}, u32[]{:S(2)}, u32[]{:S(2)}) collective-permute-start(f32[2,3,192]{1,2,0:T(8,128)S(1)} %pad_add_fusion.2), channel_id=1, source_target_pairs={{4,0},{5,1},{6,2},{7,3},{12,8},{13,9},{14,10},{15,11},{20,16},{21,... | collective-permute-start | bytes 13832 | tf_op jit(solution)/shard_map/ppermute | solution.py:18
  579.2 260.4 %reduce-scatter.16.cloned.1.call-start = ((), (), s32[]{:S(2)}) async-start(), calls=%async_computation.10 | async-start | bytes 2654208 | tf_op jit(solution)/shard_map/reduce_scatter | solution.py:305
  591.9 247.7 %reduce-scatter.18.cloned.1.call-start = ((), (), s32[]{:S(2)}) async-start(), calls=%async_computation.11 | async-start | bytes 2654208 | tf_op jit(solution)/shard_map/reduce_scatter | solution.py:306
  605.2 234.4 %reduce-scatter.20.cloned.1.call-start = ((), (), s32[]{:S(2)}) async-start(), calls=%async_computation.12 | async-start | bytes 884736
  617.7 222.0 %reduce-scatter.22.cloned.1.call-start = ((), (), s32[]{:S(2)}) async-start(), calls=%async_computation.13 | async-start | bytes 884736
  620.0 219.7 %reduce-scatter.24.cloned.1.call-start = ((), (), s32[]{:S(2)}) async-start(), calls=%async_computation.14 | async-start | bytes 884736
  831.7 5.7 copy-start.6
  831.7 5.7 copy-start.8
  (66 other events, 183.6 us)
Sparse Core Ops, SparseCore 0:
  183.0 121.3 all-reduce.28
  346.2 120.0 all-reduce.30
  579.3 222.8 all-reduce.32
Sparse Core Ops, SparseCore 1:
  185.2 29.1 all-gather.5
  216.1 28.8 all-gather.7
  528.7 33.9 reduce-scatter.25
  592.0 41.9 reduce-scatter.15
  638.3 42.3 reduce-scatter.17
  684.4 34.9 reduce-scatter.19
  723.0 34.9 reduce-scatter.21
  761.5 34.9 reduce-scatter.23
where the time goes:
time: 851 us; the launch traced here: 847 us
  waiting for transfers between devices  405 us (48%)
  matrix products  167 us (20%)
  blocking collectives  110 us (13%)
  local copies, waits for them, and re-layouts  84.9 us (10%)
  other arithmetic  53.8 us (6%)
  between operations  18.7 us (2%)
    psum x1, waiting for transfers between devices, on_device(): feed = lax.psum(project(activated, down_all), 'tensor')  177 us
    psum x1, waiting for transfers between devices, on_device(): branch = lax.psum(project(mixed, mixer_all), 'tensor')  120 us
    psum x1, waiting for transfers between devices, on_device(): feed_normed_grad = lax.psum(project(pre_grad, up_all.T), 'tensor')  107 us
    dot_general x8, matrix products, project(): jnp.einsum('btd,df->btf', left, right, precision=precise, preferred_eleme...  79.4 us
    dot_general x4, matrix products, outer_sum(): jnp.einsum('btd,btf->df', left, right, precision=precise, preferred_eleme...  39.6 us
    unnamed x2, blocking collectives  38 us
    unnamed x217, local copies, waits for them, and re-layouts  27.3 us
  transfers between devices with their start and end apart: 14, of which 3 were waited for; matrix products, arithmetic and copies ran while one was open for 23% of the time, Pallas kernels for 0%

commit v1 on v0

--- a/solution.py
+++ b/solution.py
@@ -3,6 +3,8 @@
 import jax
 import jax.numpy as jnp
 from jax import lax
+from jax.experimental import pallas as pl
+from jax.experimental.pallas import tpu as pltpu
 from jax.sharding import PartitionSpec as P
 
 SUBBLOCK = 64
@@ -309,9 +311,588 @@
     return (layer_output, input_grad) + all_parts
 
 
+HIGH = lax.Precision.HIGH
+GROUP = 4
+C_GELU = 0.7978845608028654
+
+
+def params(limit=58):
+    return pltpu.CompilerParams(vmem_limit_bytes=limit * 2**20)
+
+
+def mm(left, right):
+    return jnp.dot(left, right, precision=HIGH, preferred_element_type=jnp.float32)
+
+
+def mm_nt(left, right):
+    return lax.dot_general(
+        left, right, (((1,), (1,)), ((), ())), precision=HIGH, preferred_element_type=jnp.float32
+    )
+
+
+def mm_tn(left, right):
+    return lax.dot_general(
+        left, right, (((0,), (0,)), ((), ())), precision=HIGH, preferred_element_type=jnp.float32
+    )
+
+
+def norm_parts(v):
+    centered = v - jnp.mean(v, axis=-1, keepdims=True)
+    r = lax.rsqrt(jnp.mean(centered * centered, axis=-1, keepdims=True) + eps)
+    return centered * r, r
+
+
+def whole(shape):
+    return pl.BlockSpec(
+        shape, lambda *_: (0,) * len(shape), pipeline_mode=pl.Buffered(buffer_count=1)
+    )
+
+
+def project_kernel(x_ref, gain_ref, w_ref, o_ref, n_ref):
+    @pl.when(pl.program_id(0) == 0)
+    def _():
+        n_ref[...] = norm_parts(x_ref[...])[0] * gain_ref[...]
+
+    o_ref[...] = mm(n_ref[...], w_ref[...])
+
+
+def run_project(x, gain, w):
+    tokens, model = x.shape
+    wide = w.shape[1]
+    tile = 768
+    return pl.pallas_call(
+        project_kernel,
+        grid=(wide // tile,),
+        in_specs=[
+            whole((tokens, model)),
+            whole((1, model)),
+            pl.BlockSpec((model, tile), lambda j: (0, j)),
+        ],
+        out_specs=pl.BlockSpec((tokens, tile), lambda j: (0, j)),
+        out_shape=jax.ShapeDtypeStruct((tokens, wide), jnp.float32),
+        scratch_shapes=[pltpu.VMEM((tokens, model), jnp.float32)],
+        compiler_params=params(),
+        name="project",
+    )(x, gain, w)
+
+
+def split(a):
+    high = a.astype(jnp.bfloat16)
+    return high, (a - high.astype(jnp.float32)).astype(jnp.bfloat16)
+
+
+def spread(pair, mask):
+    return tuple(jnp.concatenate([p] * GROUP, axis=0) * mask for p in pair)
+
+
+def d3(left, right, dims):
+    dot = partial(
+        lax.dot_general, dimension_numbers=(dims, ((), ())), preferred_element_type=jnp.float32
+    )
+    return dot(left[0], right[0]) + dot(left[1], right[0]) + dot(left[0], right[1])
+
+
+NN = ((1,), (0,))
+NT = ((1,), (1,))
+TN = ((0,), (0,))
+
+
+def shift_forward(k_ref, before, kern_ref, meta, taps):
+    keys = k_ref[...]
+    extended = jnp.concatenate([before, keys], axis=0)
+    size = keys.shape[0]
+    moved = [keys]
+    for j in range(1, taps):
+        moved.append(extended[8 - j : 8 - j + size] * meta[:, 2 + j : 3 + j])
+    total = kern_ref[0:1, :] * keys
+    for j in range(1, taps):
+        total = total + kern_ref[j : j + 1, :] * moved[j]
+    return total, moved
+
+
+def compact(full, mask, width):
+    kept = full * mask
+    out = kept[0:width]
+    for h in range(1, GROUP):
+        out = out + kept[h * width : (h + 1) * width]
+    return out
+
+
+def mixer_kernel(
+    taps, q_ref, k_ref, v_ref, meta_ref, segrow_ref, kern_ref, grow_ref, shrink_ref,
+    dec_ref, end_ref, all_ref, mask_ref, maskf_ref, mixed_ref, state_out_ref, state, tail,
+):
+    size, model = k_ref.shape
+    span = mask_ref.shape[0]
+    width = span // GROUP
+
+    @pl.when(pl.program_id(0) == 0)
+    def _():
+        state[...] = jnp.zeros_like(state)
+        tail[...] = jnp.zeros_like(tail)
+
+    meta = meta_ref[...]
+    shifted, _ = shift_forward(k_ref, tail[...], kern_ref, meta, taps)
+    tail[...] = k_ref[size - 8 :, :]
+    rows = lax.broadcasted_iota(jnp.int32, (size, span), 0)
+    cols = lax.broadcasted_iota(jnp.int32, (size, span), 1) % size
+    living, kept = meta[:, 1:2], meta[:, 2:3]
+    allowed = jnp.where(
+        jnp.logical_and(rows >= cols, meta[:, 0:1] == segrow_ref[0]), 1.0, 0.0
+    )
+    mask = mask_ref[...]
+    state_out_ref[0] = state[...]
+    for g in range(model // span):
+        s = slice(g * span, (g + 1) * span)
+        qg = split(q_ref[:, s] * grow_ref[:, s])
+        kf = shifted[:, s] * shrink_ref[:, s]
+        kg = split(kf)
+        v = split(v_ref[:, s])
+        scores = d3(qg, spread(kg, mask), NT) * allowed
+        entering = split(state[:, s] * dec_ref[:, s])
+        out = d3(split(scores), spread(v, mask), NN)
+        out = out + living * d3(qg, spread(entering, mask), NN)
+        mixed_ref[:, s] = out
+        update = compact(d3(split(kf * kept), v, TN), maskf_ref[...], width)
+        state[:, s] = (
+            state[:, s] * (all_ref[:, s] * meta[size - 1 : size, 1:2]) + end_ref[:, s] * update
+        )
+
+
+def run_mixer(proj, meta, segrow, kern, tables):
+    tokens = proj.shape[0]
+    model = proj.shape[1] // 3
+    size = tables["grow"].shape[0]
+    steps = tokens // size
+    taps = kern.shape[0]
+
+    def col(i):
+        return pl.BlockSpec((size, model), lambda c: (c, i))
+
+    return pl.pallas_call(
+        partial(mixer_kernel, taps),
+        grid=(steps,),
+        in_specs=[
+            col(0), col(1), col(2),
+            pl.BlockSpec((size, meta.shape[1]), lambda c: (c, 0)),
+            pl.BlockSpec((1, 1, segrow.shape[2]), lambda c: (c, 0, 0)),
+        ]
+        + [whole(a.shape) for a in (kern, *tables.values())],
+        out_specs=[
+            pl.BlockSpec((size, model), lambda c: (c, 0)),
+            pl.BlockSpec((1, size, model), lambda c: (c, 0, 0)),
+        ],
+        out_shape=[
+            jax.ShapeDtypeStruct((tokens, model), jnp.float32),
+            jax.ShapeDtypeStruct((steps, size, model), jnp.float32),
+        ],
+        scratch_shapes=[pltpu.VMEM((size, model), jnp.float32), pltpu.VMEM((8, model), jnp.float32)],
+        compiler_params=params(),
+        name="mixer",
+    )(proj, proj, proj, meta, segrow, kern, *tables.values())
+
+
+def mixer_back_kernel(
+    taps, q_ref, k_ref, v_ref, du_ref, before_ref, state_ref, meta_ref, segrow_ref, kern_ref,
+    grow_ref, shrink_ref, dec_ref, end_ref, all_ref, mask_ref, maskf_ref,
+    dq_ref, dk_ref, dv_ref, dkern_ref, grad, head,
+):
+    size, model = k_ref.shape
+    span = mask_ref.shape[0]
+    width = span // GROUP
+
+    @pl.when(pl.program_id(0) == 0)
+    def _():
+        grad[...] = jnp.zeros_like(grad)
+        head[...] = jnp.zeros_like(head)
+        dkern_ref[...] = jnp.zeros_like(dkern_ref)
+
+    meta = meta_ref[...]
+    shifted, moved = shift_forward(k_ref, before_ref[...], kern_ref, meta, taps)
+    rows = lax.broadcasted_iota(jnp.int32, (size, span), 0)
+    cols = lax.broadcasted_iota(jnp.int32, (size, span), 1) % size
+    same = meta[:, 0:1] == segrow_ref[0]
+    living, kept = meta[:, 1:2], meta[:, 2:3]
+    allowed = jnp.where(jnp.logical_and(rows >= cols, same), 1.0, 0.0)
+    allowed_t = jnp.where(jnp.logical_and(rows <= cols, same), 1.0, 0.0)
+    mask = mask_ref[...]
+    for g in range(model // span):
+        s = slice(g * span, (g + 1) * span)
+        qf = q_ref[:, s] * grow_ref[:, s]
+        qg = split(qf)
+        kg = split(shifted[:, s] * shrink_ref[:, s])
+        v = split(v_ref[:, s])
+        du = split(du_ref[:, s])
+        q_bd, k_bd, v_bd, u_bd = (spread(p, mask) for p in (qg, kg, v, du))
+        s_bd = spread(split(state_ref[0, :, s] * dec_ref[:, s]), mask)
+        g_bd = spread(split(grad[:, s] * end_ref[:, s]), mask)
+        p_t = d3(kg, q_bd, NT) * allowed_t
+        dp = d3(du, v_bd, NT) * allowed
+        dp_t = d3(v, u_bd, NT) * allowed_t
+        dqg = d3(split(dp), k_bd, NN) + living * d3(du, s_bd, NT)
+        dkg = d3(split(dp_t), q_bd, NN) + kept * d3(v, g_bd, NT)
+        dv_ref[:, s] = d3(split(p_t), u_bd, NN) + kept * d3(kg, g_bd, NN)
+        dq_ref[:, s] = dqg * grow_ref[:, s]
+        dshift = dkg * shrink_ref[:, s]
+        update = compact(d3(split(qf * living), du, TN), maskf_ref[...], width)
+        grad[:, s] = (
+            grad[:, s] * (all_ref[:, s] * meta[size - 1 : size, 1:2]) + dec_ref[:, s] * update
+        )
+        total = kern_ref[0:1, s] * dshift
+        for j in range(1, taps):
+            part = dshift * meta[:, 2 + j : 3 + j]
+            extended = jnp.concatenate([part, head[j - 1, :, s]], axis=0)
+            total = total + kern_ref[j : j + 1, s] * extended[j : j + size]
+            head[j - 1, :, s] = part[0:8]
+        dk_ref[:, s] = total
+        for j in range(taps):
+            dkern_ref[j : j + 1, s] += jnp.sum(dshift * moved[j][:, s], axis=0, keepdims=True)
+
+
+def run_mixer_back(proj, du, states, meta, segrow, kern, tables):
+    tokens = proj.shape[0]
+    model = proj.shape[1] // 3
+    size = tables["grow"].shape[0]
+    steps = tokens // size
+    taps = kern.shape[0]
+    last = steps - 1
+
+    def col(i):
+        return pl.BlockSpec((size, model), lambda c: (last - c, i))
+
+    return pl.pallas_call(
+        partial(mixer_back_kernel, taps),
+        grid=(steps,),
+        in_specs=[
+            col(0), col(1), col(2), col(0),
+            pl.BlockSpec((8, model), lambda c: (jnp.maximum((last - c) * (size // 8) - 1, 0), 1)),
+            pl.BlockSpec((1, size, model), lambda c: (last - c, 0, 0)),
+            pl.BlockSpec((size, meta.shape[1]), lambda c: (last - c, 0)),
+            pl.BlockSpec((1, 1, segrow.shape[2]), lambda c: (last - c, 0, 0)),
+        ]
+        + [whole(a.shape) for a in (kern, *tables.values())],
+        out_specs=[col(0), col(0), col(0), whole(kern.shape)],
+        out_shape=[jax.ShapeDtypeStruct((tokens, model), jnp.float32)] * 3
+        + [jax.ShapeDtypeStruct(kern.shape, jnp.float32)],
+        scratch_shapes=[
+            pltpu.VMEM((size, model), jnp.float32),
+            pltpu.VMEM((taps - 1, 8, model), jnp.float32),
+        ],
+        compiler_params=params(),
+        name="mixer_back",
+    )(proj, proj, proj, du, proj, states, meta, segrow, kern, *tables.values())
+
+
+def branch_kernel(x_ref, m_ref, w_ref, gain_ref, resid_ref, n_ref):
+    resid = x_ref[...] + mm_nt(m_ref[...], w_ref[...])
+    resid_ref[...] = resid
+    n_ref[...] = norm_parts(resid)[0] * gain_ref[...]
+
+
+def run_branch(x, mixed, w, gain):
+    tokens, model = x.shape
+    tile = 256
+    row = pl.BlockSpec((tile, model), lambda i: (i, 0))
+    return pl.pallas_call(
+        branch_kernel,
+        grid=(tokens // tile,),
+        in_specs=[row, row, whole(w.shape), whole(gain.shape)],
+        out_specs=[row, row],
+        out_shape=[jax.ShapeDtypeStruct(x.shape, jnp.float32)] * 2,
+        compiler_params=params(),
+        name="branch",
+    )(x, mixed, w, gain)
+
+
+def feed_kernel(own, n_ref, ct_ref, resid_ref, up_ref, down_ref, out_ref, fng_ref, dg_ref, ug_ref):
+    step = pl.program_id(0)
+
+    @pl.when(step == 0)
+    def _():
+        out_ref[...] = resid_ref[...]
+        fng_ref[...] = jnp.zeros_like(fng_ref)
+
+    pre = mm(n_ref[...], up_ref[...])
+    back = mm(ct_ref[...], down_ref[...])
+    th = jnp.tanh(C_GELU * (pre + 0.044715 * (pre * pre * pre)))
+    act = 0.5 * pre * (1.0 + th)
+    slope = 0.5 * (1.0 + th) + (0.5 * C_GELU) * pre * (1.0 - th * th) * (
+        1.0 + (3 * 0.044715) * (pre * pre)
+    )
+    grad = back * slope
+    out_ref[...] += mm_nt(act, down_ref[...])
+    fng_ref[...] += mm_nt(grad, up_ref[...])
+
+    @pl.when(step < own)
+    def _():
+        dg_ref[...] = mm_tn(ct_ref[...], act)
+        ug_ref[...] = mm_tn(n_ref[...], grad)
+
+
+def run_feed(n, ct, resid, up, down, own_width):
+    tokens, model = n.shape
+    hidden = up.shape[1]
+    tile = 256
+    own = own_width // tile
+    wide = pl.BlockSpec((model, tile), lambda j: (0, j))
+    mine = pl.BlockSpec((model, tile), lambda j: (0, jnp.minimum(j, own - 1)))
+    act = whole((tokens, model))
+    return pl.pallas_call(
+        partial(feed_kernel, own),
+        grid=(hidden // tile,),
+        in_specs=[act, act, act, wide, wide],
+        out_specs=[act, act, mine, mine],
+        out_shape=[jax.ShapeDtypeStruct((tokens, model), jnp.float32)] * 2
+        + [jax.ShapeDtypeStruct((model, own_width), jnp.float32)] * 2,
+        compiler_params=params(),
+        name="feed",
+    )(n, ct, resid, up, down)
+
+
+def norm_back(v, gain, incoming):
+    xhat, r = norm_parts(v)
+    scaled = incoming * gain
+    grad = r * (
+        scaled
+        - jnp.mean(scaled, axis=-1, keepdims=True)
+        - xhat * jnp.mean(scaled * xhat, axis=-1, keepdims=True)
+    )
+    return grad, jnp.sum(incoming * xhat, axis=0, keepdims=True), xhat
+
+
+def resid_back_kernel(fng_ref, resid_ref, ct_ref, gain_ref, w_ref, m_ref, rg_ref, mg_ref, gg_ref, wg_ref):
+    @pl.when(pl.program_id(0) == 0)
+    def _():
+        gg_ref[...] = jnp.zeros_like(gg_ref)
+        wg_ref[...] = jnp.zeros_like(wg_ref)
+
+    grad, gain_grad, _ = norm_back(resid_ref[...], gain_ref[...], fng_ref[...])
+    rg = ct_ref[...] + grad
+    rg_ref[...] = rg
+    gg_ref[...] += gain_grad
+    mg_ref[...] = mm(rg, w_ref[...])
+    wg_ref[...] += mm_tn(rg, m_ref[...])
+
+
+def run_resid_back(fng, resid, ct, gain, w, mixed, own):
+    tokens, model = resid.shape
+    tile = 256
+    row = pl.BlockSpec((tile, model), lambda i: (i, 0))
+    return pl.pallas_call(
+        resid_back_kernel,
+        grid=(tokens // tile,),
+        in_specs=[row, row, row, whole(gain.shape), whole(w.shape), pl.BlockSpec((tile, own), lambda i: (i, 0))],
+        out_specs=[row, row, whole(gain.shape), whole((model, own))],
+        out_shape=[jax.ShapeDtypeStruct(resid.shape, jnp.float32)] * 2
+        + [jax.ShapeDtypeStruct(gain.shape, jnp.float32), jax.ShapeDtypeStruct((model, own), jnp.float32)],
+        compiler_params=params(),
+        name="resid_back",
+    )(fng, resid, ct, gain, w, mixed)
+
+
+def input_back_kernel(x_ref, rg_ref, gain_ref, w_ref, dq_ref, dk_ref, dv_ref, ig_ref, gg_ref, wg_ref):
+    @pl.when(pl.program_id(0) == 0)
+    def _():
+        gg_ref[...] = jnp.zeros_like(gg_ref)
+        wg_ref[...] = jnp.zeros_like(wg_ref)
+
+    model = x_ref.shape[1]
+    own = wg_ref.shape[1] // 3
+    parts = (dq_ref[...], dk_ref[...], dv_ref[...])
+    incoming = mm_nt(parts[0], w_ref[:, 0:model])
+    incoming = incoming + mm_nt(parts[1], w_ref[:, model : 2 * model])
+    incoming = incoming + mm_nt(parts[2], w_ref[:, 2 * model :])
+    grad, gain_grad, xhat = norm_back(x_ref[...], gain_ref[...], incoming)
+    ig_ref[...] = rg_ref[...] + grad
+    gg_ref[...] += gain_grad
+    normed = xhat * gain_ref[...]
+    for i in range(3):
+        wg_ref[:, i * own : (i + 1) * own] += mm_tn(normed, parts[i][:, 0:own])
+
+
+def run_input_back(x, rg, gain, w, dq, dk, dv, own):
+    tokens, model = x.shape
+    tile = 256
+    row = pl.BlockSpec((tile, model), lambda i: (i, 0))
+    return pl.pallas_call(
+        input_back_kernel,
+        grid=(tokens // tile,),
+        in_specs=[row, row, whole(gain.shape), whole(w.shape), row, row, row],
+        out_specs=[row, whole(gain.shape), whole((model, 3 * own))],
+        out_shape=[
+            jax.ShapeDtypeStruct(x.shape, jnp.float32),
+            jax.ShapeDtypeStruct(gain.shape, jnp.float32),
+            jax.ShapeDtypeStruct((model, 3 * own), jnp.float32),
+        ],
+        compiler_params=params(),
+        name="input_back",
+    )(x, rg, gain, w, dq, dk, dv)
+
+
+def gather_weights(
+    mixer_gain, query_weight, key_weight, value_weight, shift_kernel, state_decay, mixer_weight,
+    feed_gain, up_weight, down_weight,
+):
+    plane = ("dp", "ctx")
+    rows, own = query_weight.shape
+    taps, few = shift_kernel.shape
+    heads, width = state_decay.shape
+    hidden = up_weight.shape[1]
+    lanes = 4 * own
+    small = jnp.concatenate(
+        [mixer_gain, feed_gain, shift_kernel.reshape(-1), state_decay.reshape(-1)]
+    )
+    small = jnp.pad(small, (0, lanes - small.shape[0]))[None]
+    first = jnp.concatenate(
+        [
+            jnp.concatenate([query_weight, key_weight, value_weight, mixer_weight.T], axis=1),
+            jnp.pad(small, ((0, 7), (0, 0))),
+        ],
+        axis=0,
+    )
+    second = jnp.concatenate([up_weight, down_weight.T], axis=1)
+    count = lax.axis_size("tensor")
+    me = lax.axis_index("tensor")
+
+    def everywhere(block):
+        out = lax.all_gather(block, ("tensor",) + plane, axis=0)
+        out = out.reshape((count, -1) + block.shape)
+        return jnp.stack(
+            [lax.dynamic_index_in_dim(out, me ^ i, 0, keepdims=False) for i in range(count)]
+        )
+
+    first, second = everywhere(first), everywhere(second)
+    blocks = first.shape[1]
+    model = blocks * rows
+    matrices = first[:, :, :rows].reshape(count, model, 4, own)
+    matrices = jnp.transpose(matrices, (2, 1, 0, 3)).reshape(4, model, count * own)
+    joint = jnp.concatenate([matrices[0], matrices[1], matrices[2]], axis=1)
+    small = first[:, :, rows]
+    gains = small[0, :, : 2 * rows].reshape(blocks, 2, rows).transpose(1, 0, 2).reshape(2, 1, model)
+    shift = small[:, :, 2 * rows : 2 * rows + taps * few].reshape(count, blocks, taps, few)
+    shift = shift.transpose(2, 0, 1, 3).reshape(taps, count * blocks * few)
+    begin = 2 * rows + taps * few
+    decay = small[:, 0, begin : begin + heads * width].reshape(count * heads, width)
+    feed = second.reshape(count, model, 2, hidden).transpose(2, 1, 0, 3).reshape(2, model, count * hidden)
+    return gains[0], gains[1], joint, matrices[3], shift, decay, feed[0], feed[1]
+
+
+def mixer_tables(decay, size):
+    heads, width = decay.shape
+    log_decay = jnp.log(decay)
+    flat = log_decay.reshape(1, heads * width)
+    position = jnp.arange(size, dtype=jnp.float32)[:, None]
+    column = jnp.repeat(log_decay.T, width, axis=1)
+    span = GROUP * width
+    which = jnp.arange(span) // width
+    mask = (which[:, None] == which[None, :]).astype(jnp.float32)
+    return {
+        "grow": jnp.exp(position * flat),
+        "shrink": jnp.exp(-position * flat),
+        "dec": jnp.exp(column),
+        "end": jnp.exp((size - 1.0) * column),
+        "all": jnp.exp(size * column),
+        "mask": mask.astype(jnp.bfloat16),
+        "maskf": mask,
+    }
+
+
+def positions(segments, size, taps):
+    length = segments.shape[0]
+    seg = segments.astype(jnp.float32)
+    grouped = seg.reshape(-1, size)
+    before = jnp.concatenate([jnp.full((1,), -1.0, jnp.float32), grouped[:-1, -1]])
+    columns = [seg, (grouped == before[:, None]).reshape(-1), (grouped == grouped[:, -1:]).reshape(-1)]
+    for j in range(1, taps):
+        columns.append(jnp.concatenate([jnp.zeros((j,), bool), seg[j:] == seg[:-j]]))
+    columns = [c.astype(jnp.float32) for c in columns]
+    while len(columns) < 8:
+        columns.append(jnp.zeros((length,), jnp.float32))
+    return jnp.stack(columns, axis=1), jnp.tile(grouped, (1, GROUP))[:, None]
+
+
+def swap_in(block):
+    me = lax.axis_index("ctx")
+    rows, half = block.shape[:2]
+    mine = lax.dynamic_index_in_dim(block, me, 0, keepdims=False)
+    theirs = lax.dynamic_index_in_dim(block, 1 - me, 0, keepdims=False)
+    came = lax.ppermute(theirs, "ctx", [(0, 1), (1, 0)])
+    first = jnp.where(me == 0, mine, came)
+    second = jnp.where(me == 0, came, mine)
+    return jnp.concatenate([first, second], axis=0)
+
+
+def swap_out(row):
+    me = lax.axis_index("ctx")
+    half = row.shape[0] // 2
+    mine = lax.dynamic_slice_in_dim(row, me * half, half, 0)
+    theirs = lax.dynamic_slice_in_dim(row, (1 - me) * half, half, 0)
+    came = lax.ppermute(theirs, "ctx", [(0, 1), (1, 0)])
+    first = jnp.where(me == 0, mine, came)
+    second = jnp.where(me == 0, came, mine)
+    return jnp.stack([first, second])
+
+
+def by_sequence(
+    layer_input, segment_ids, mixer_gain, query_weight, key_weight, value_weight, shift_kernel,
+    state_decay, mixer_weight, feed_gain, up_weight, down_weight, cotangent,
+):
+    plane = ("dp", "ctx")
+    own = query_weight.shape[1]
+    hidden = up_weight.shape[1]
+    taps = shift_kernel.shape[0]
+    mg, fg, joint, mixer_t, kern, decay, up, down_t = gather_weights(
+        mixer_gain, query_weight, key_weight, value_weight, shift_kernel, state_decay,
+        mixer_weight, feed_gain, up_weight, down_weight,
+    )
+    x = swap_in(layer_input)
+    ct = swap_in(cotangent)
+    seg = swap_in(segment_ids)
+    tables = mixer_tables(decay, SUBBLOCK)
+    meta, segrow = positions(seg, SUBBLOCK, taps)
+    proj = run_project(x, mg, joint)
+    mixed, states = run_mixer(proj, meta, segrow, kern, tables)
+    resid, n = run_branch(x, mixed, mixer_t, fg)
+    out, fng, down_g, up_g = run_feed(n, ct, resid, up, down_t, hidden)
+    rg, du, feed_gain_g, mixer_g = run_resid_back(fng, resid, ct, fg, mixer_t, mixed[:, :own], own)
+    dq, dk, dv, kern_g = run_mixer_back(proj, du, states, meta, segrow, kern, tables)
+    ig, mixer_gain_g, joint_g = run_input_back(x, rg, mg, joint, dq, dk, dv, own)
+
+    def scatter(value, dim):
+        return lax.psum_scatter(value, plane, scatter_dimension=dim, tiled=True)
+
+    joint_g = scatter(joint_g, 0)
+    return (
+        swap_out(out),
+        swap_out(ig),
+        scatter(mixer_gain_g[0], 0),
+        joint_g[:, :own],
+        joint_g[:, own : 2 * own],
+        joint_g[:, 2 * own :],
+        scatter(kern_g[:, :own], 1),
+        scatter(mixer_g, 0).T,
+        scatter(feed_gain_g[0], 0),
+        scatter(up_g, 0),
+        scatter(down_g, 0).T,
+    )
+
+
 def solution(mesh):
+    shape = mesh.shape
+
+    def chosen(*arrays):
+        rows, length, model = arrays[0].shape
+        heads, width = arrays[7].shape
+        fits = (
+            (shape["dp"], shape["ctx"], shape["tensor"]) == (4, 2, 4)
+            and rows == 2
+            and (heads * shape["tensor"]) % GROUP == 0
+            and width == SUBBLOCK
+        )
+        return (by_sequence if fits else on_device)(*arrays)
+
     return jax.shard_map(
-        on_device,
+        chosen,
         mesh=mesh,
         in_specs=(
             P("dp", "ctx", None),

time: 851 us -> 657 us (0.77)
  waiting for transfers between devices: 405 us -> 159 us
  Pallas kernels: 0 us -> 229 us
  matrix products: 167 us -> 0 us
  local copies, waits for them, and re-layouts: 84.9 us -> 181 us
  blocking collectives: 110 us -> 22.6 us
  other arithmetic: 53.8 us -> 42.2 us
    psum x3 -> x0, waiting for transfers between devices: 404 us -> none  [the longest x1 177 us: on_device(): feed = lax.psum(project(activated, down_all), 'tensor')]
    pallas_call x0 -> x7, Pallas kernels: none -> 229 us  [the longest x1 80.5 us: run_feed(): pl.pallas_call(partial(feed_kernel, own), grid=(hidden // tile,), in_spec...]
    dot_general x25 -> x0, matrix products: 167 us -> none  [the longest x8 79.4 us: project(): jnp.einsum('btd,df->btf', left, right, precision=precise, preferred_eleme...]
    reduce_scatter x2 -> x4, waiting for transfers between devices: 0.01 us -> 89.4 us  [scatter(): return lax.psum_scatter(value, plane, scatter_dimension=dim, tiled=True)]
    all_gather x8 -> x0, blocking collectives: 71.6 us -> none  [the longest x3 16.6 us: carried_in(): pieces = jax.tree.map(lambda part: lax.all_gather(part, axis), value)]
    all_gather x2, waiting for transfers between devices: 0.01 us -> 68 us  [everywhere(): out = lax.all_gather(block, ('tensor',) + plane, axis=0)]
    slice x9 -> x12, local copies, waits for them, and re-layouts: 8.59 us -> 59.6 us  [the longest x2 33.9 us: gather_weights(): feed[1]]
    reshape x10 -> x7, local copies, waits for them, and re-layouts: 27.2 us -> 52.8 us  [the longest x2 28.1 us: gather_weights(): matrices = first[:, :, :rows].reshape(count, model, 4, own)]
  transfers between devices with their start and end apart: 14 -> 11, of which waited for: 3 -> 3; matrix products, arithmetic and copies ran while one was open for 23% -> 17% of each run, Pallas kernels for 0% -> 21%
where the time goes in v1:
time: 657 us; the launch traced here: 651 us
  Pallas kernels  229 us (35%)
  local copies, waits for them, and re-layouts  181 us (28%)
  waiting for transfers between devices  159 us (24%)
  other arithmetic  42.2 us (6%)
  blocking collectives  22.6 us (3%)
  between operations  15.9 us (2%)
    reduce_scatter x4, waiting for transfers between devices, scatter(): return lax.psum_scatter(value, plane, scatter_dimension=dim, tiled=True)  89.4 us
    pallas_call x1, Pallas kernels, run_feed(): pl.pallas_call(partial(feed_kernel, own), grid=(hidden // tile,), in_spec...  80.5 us
    all_gather x2, waiting for transfers between devices, everywhere(): out = lax.all_gather(block, ('tensor',) + plane, axis=0)  68 us
    pallas_call x1, Pallas kernels, run_mixer_back(): pl.pallas_call(partial(mixer_back_kernel, taps), grid=(steps,), in_specs=...  56.4 us
    slice x2, local copies, waits for them, and re-layouts, gather_weights(): feed[1]  33.9 us
    pallas_call x1, Pallas kernels, run_mixer(): pl.pallas_call(partial(mixer_kernel, taps), grid=(steps,), in_specs=[col(...  30.5 us
    unnamed x33, local copies, waits for them, and re-layouts  30.2 us
    reshape x2, local copies, waits for them, and re-layouts, gather_weights(): matrices = first[:, :, :rows].reshape(count, model, 4, own)  28.1 us
  transfers between devices with their start and end apart: 11, of which 3 were waited for; matrix products, arithmetic and copies ran while one was open for 17% of the time, Pallas kernels for 21%

profile of v1, /device:TPU:0, one launch (start us, length us, event | category | flops | bytes accessed | tf_op | source)
XLA Modules:
  0.0 650.7 jit_solution(924079748888431910)
XLA Ops:
  10.5 1.8 select_maximum_fusion
  12.4 1.9 pad_maximum_fusion.9
  15.8 3.0 dynamic-slice_bitcast_fusion
  18.8 1.2 dynamic-slice_bitcast_fusion.1
  24.5 1.6 bitcast_select_fusion.1
  26.2 1.8 pad_maximum_fusion.6.ct_ref
  28.0 1.2 copy-done.5
  29.2 1.6 bitcast_select_fusion.3
  30.8 1.9 pad_maximum_fusion.5.x_ref
  32.7 68.0 %all-gather.5.cloned.1.call-done = f32[3328,768]{1,0:T(8,128)} async-done(((f32[104,768]{1,0:T(8,128)}), f32[3328,768]{1,0:T(8,128)}) %all-gather.5.cloned.1.call-update) | async-done | bytes 10223632 | tf_op jit(solution)/shard_map/all_gather | solution.py:758
  100.7 4.7 constant_dynamic-slice_fusion.11
  105.4 1.4 copy-done
  114.6 6.3 pad_maximum_fusion.1
  120.9 14.6 %reshape.270 = f32[4,768,4,192]{3,2,1,0:T(4,128)} reshape(f32[4,8,96,768]{3,2,1,0:T(8,128)} %pad_maximum_fusion.1) | data formatting | bytes 18874368 | tf_op jit(solution)/shard_map/reshape | solution.py:767
  135.5 13.5 %copy.91 = f32[4,768,4,192]{1,3,2,0:T(8,128)} copy(f32[4,768,4,192]{3,2,1,0:T(4,128)} %reshape.270) | data formatting | bytes 18874368 | tf_op jit(solution)/shard_map/reshape | solution.py:767
  149.0 6.9 %fusion.3 = (f32[1,768,4,192]{1,3,0,2:T(8,128)}, f32[1,768,4,192]{1,3,0,2:T(8,128)}, f32[1,768,4,192]{1,3,0,2:T(8,128)}, f32[1,768,4,192]{1,3,0,2:T(8,128)S(1)}) fusion(f32[4,768,4,192]{1,3,0,2:T(8,128)} %bitcast.64), kind=kLoop, calls=%fused_computation.74 | loop fusion | bytes 18874368 | tf_op jit(solution)/shard_map/slice | solution.py:777
  155.9 3.1 copy.83.w_ref
  159.0 3.0 copy.77
  162.0 3.0 copy.76
  165.0 2.0 copy.75
  167.0 8.0 %pad_maximum_fusion.4.w_ref = f32[768,2304]{1,0:T(8,128)} fusion(f32[768,768]{1,0:T(8,128)} %copy.77, f32[768,768]{1,0:T(8,128)} %copy.76, f32[768,768]{1,0:T(8,128)} %copy.75), kind=kLoop, calls=%fused_computation.4 | loop fusion | flops 3538944 | bytes 14155776 | tf_op jit(solution)/shard_map/concatenate | solution.py:769
  175.0 16.7 %project.1.q_ref.k_ref.v_ref.before_ref = f32[1024,2304]{1,0:T(8,128)} custom-call(f32[1024,768]{1,0:T(8,128)} %pad_maximum_fusion.5.x_ref, f32[1,768]{1,0:T(1,128)} %squeeze.69.gain_ref, f32[768,2304]{1,0:T(8,128)} %pad_maximum_fusion.4.w_ref), custom_call_target="tpu_custom_call" | custom-call | tf_op jit(solution)/shard_map/project/pallas_call | solution.py:363
  192.5 30.5 %mixer.1 = (f32[1024,768]{1,0:T(8,128)}, f32[16,64,768]{2,1,0:T(8,128)}) custom-call(f32[1024,2304]{1,0:T(8,128)} %project.1.q_ref.k_ref.v_ref.before_ref, f32[1024,2304]{1,0:T(8,128)} %project.1.q_ref.k_ref.v_ref.before_ref, f32[1024,2304]{1,0:T(8,128)} %project.1.q_ref.k_ref.v_ref.before_ref, f32[1024,8]{1,0:T(8,128)} %copy.82.meta_ref, ...), custom_call_target="tpu_custom_call" | custom-call | tf_op jit(solution)/shard_map/mixer/pallas_call | solution.py:472
  223.1 2.3 slice.107.m_ref
  225.4 9.0 %branch.1 = (f32[1024,768]{1,0:T(8,128)}, f32[1024,768]{1,0:T(8,128)}) custom-call(f32[1024,768]{1,0:T(8,128)} %pad_maximum_fusion.5.x_ref, f32[1024,768]{1,0:T(8,128)} %get-tuple-element.30.m_ref, f32[768,768]{1,0:T(8,128)} %copy.83.w_ref, f32[1,768]{1,0:T(1,128)} %squeeze.77.gain_ref), custom_call_target="tpu_custom_call" | custom-call | tf_op jit(solution)/shard_map/branch/pallas_call | solution.py:596
  234.3 7.7 %constant_dynamic-slice_fusion.5 = (f32[1,8,96,1536]{3,2,1,0:T(8,128)S(1)}, f32[1,8,96,1536]{3,2,1,0:T(8,128)S(1)}, f32[1,8,96,1536]{3,2,1,0:T(8,128)S(1)}, f32[1,8,96,1536]{3,2,1,0:T(8,128)S(1)}) fusion(f32[4,8,96,1536]{3,2,1,0:T(8,128)} %bitcast.65, s32[]{:T(128)S(6)} %select_n.110, s32[]{:T(128)S(6)} %select_n.113, s32[]{:T(128)S(6)} %select_n.112, ...), kind=kLoop, calls=%fused_computation.39 | loop fusion | bytes 37748752 | tf_op jit(solution)/shard_map/jit(dynamic_index_in_dim)/dynamic_slice | solution.py:761
  242.1 6.9 %pad_maximum_fusion = f32[4,8,96,1536]{3,2,1,0:T(8,128)} fusion(f32[1,8,96,1536]{3,2,1,0:T(8,128)S(1)} %get-tuple-element.105, f32[1,8,96,1536]{3,2,1,0:T(8,128)S(1)} %get-tuple-element.106, f32[1,8,96,1536]{3,2,1,0:T(8,128)S(1)} %get-tuple-element.107, f32[1,8,96,1536]{3,2,1,0:T(8,128)S(1)} %get-tuple-element.104), kind=kLoop, calls=%fused_computation | loop fusion | flops 14155776 | bytes 37748736 | tf_op jit(solution)/shard_map/stack | solution.py:760
  249.0 22.3 %reshape.256 = f32[4,768,2,768]{3,2,1,0:T(2,128)} reshape(f32[4,8,96,1536]{3,2,1,0:T(8,128)} %pad_maximum_fusion) | data formatting | bytes 37748736 | tf_op jit(solution)/shard_map/reshape | solution.py:776
  271.3 20.5 %fusion.2 = (f32[1,768,4,768]{3,0,1,2:T(1,128)}, f32[1,768,4,768]{3,0,1,2:T(1,128)}) fusion(f32[2,768,4,768]{3,0,1,2:T(2,128)} %bitcast.59), kind=kLoop, calls=%fused_computation.73 | loop fusion | bytes 37748736 | tf_op jit(solution)/shard_map/slice | solution.py:777
  291.8 13.4 %copy.85 = f32[1,768,4,768]{3,2,1,0:T(4,128)} copy(f32[1,768,4,768]{3,0,1,2:T(1,128)} %get-tuple-element.102) | data formatting | bytes 18874368 | tf_op jit(solution)/shard_map/slice | solution.py:777
  305.2 9.5 %copy.94 = f32[96,8,4,768]{3,1,2,0:T(8,128)} copy(f32[96,8,4,768]{3,2,1,0:T(4,128)} %bitcast.62) | data formatting | bytes 18874368
  314.7 13.6 %copy.84 = f32[1,768,4,768]{3,2,1,0:T(4,128)} copy(f32[1,768,4,768]{3,0,1,2:T(1,128)} %get-tuple-element.103) | data formatting | bytes 18874368 | tf_op jit(solution)/shard_map/slice | solution.py:777
  328.3 9.5 %copy.93 = f32[96,8,4,768]{3,1,2,0:T(8,128)} copy(f32[96,8,4,768]{3,2,1,0:T(4,128)} %bitcast.63) | data formatting | bytes 18874368
  337.8 80.5 %feed.1 = (f32[1024,768]{1,0:T(8,128)}, f32[1024,768]{1,0:T(8,128)}, f32[768,768]{1,0:T(8,128)}, f32[768,768]{1,0:T(8,128)}) custom-call(f32[1024,768]{1,0:T(8,128)} %get-tuple-element.31.n_ref, f32[1024,768]{1,0:T(8,128)} %pad_maximum_fusion.6.ct_ref, f32[1024,768]{1,0:T(8,128)} %get-tuple-element.32.resid_ref, f32[768,3072]{1,0:T(8,128)} %bitcast.61, ...), custom_call_target="tpu_custom_call" | custom-call | tf_op jit(solution)/shard_map/feed/pallas_call | solution.py:640
  418.3 12.2 %resid_back.1 = (f32[1024,768]{1,0:T(8,128)}, f32[1024,768]{1,0:T(8,128)}, f32[1,768]{1,0:T(1,128)}, f32[768,192]{1,0:T(8,128)}) custom-call(f32[1024,768]{1,0:T(8,128)} %get-tuple-element.34.fng_ref, f32[1024,768]{1,0:T(8,128)} %get-tuple-element.32.resid_ref, f32[1024,768]{1,0:T(8,128)} %pad_maximum_fusion.6.ct_ref, f32[1,768]{1,0:T(1,128)} %squeeze.77.gain_ref, ...), custom_call_target="tpu_custom_call" | custom-call | tf_op jit(solution)/shard_map/resid_back/pallas_call | solution.py:681
  430.6 56.4 %mixer_back.1 = (f32[1024,768]{1,0:T(8,128)}, f32[1024,768]{1,0:T(8,128)}, f32[1024,768]{1,0:T(8,128)}, f32[4,768]{1,0:T(4,128)}) custom-call(f32[1024,2304]{1,0:T(8,128)} %project.1.q_ref.k_ref.v_ref.before_ref, f32[1024,2304]{1,0:T(8,128)} %project.1.q_ref.k_ref.v_ref.before_ref, f32[1024,2304]{1,0:T(8,128)} %project.1.q_ref.k_ref.v_ref.before_ref, ...), custom_call_target="tpu_custom_call" | custom-call | tf_op jit(solution)/shard_map/mixer_back/pallas_call | solution.py:563
  487.0 23.4 %input_back.1 = (f32[1024,768]{1,0:T(8,128)}, f32[1,768]{1,0:T(1,128)}, f32[768,576]{1,0:T(8,128)}) custom-call(f32[1024,768]{1,0:T(8,128)} %pad_maximum_fusion.5.x_ref, f32[1024,768]{1,0:T(8,128)} %get-tuple-element.35.rg_ref, f32[1,768]{1,0:T(1,128)} %squeeze.69.gain_ref, f32[768,2304]{1,0:T(8,128)} %pad_maximum_fusion.4.w_ref, ...), custom_call_target="tpu_custom_call" | custom-call | tf_op jit(solution)/shard_map/input_back/pallas_call | solution.py:717
  512.3 1.2 constant_dynamic-slice_fusion.1
  513.9 1.2 constant_dynamic-slice_fusion
  518.1 22.6 %all-reduce.7 = (f32[768]{0:T(1024)S(1)}, f32[4,192]{1,0:T(4,128)S(1)}, f32[768]{0:T(1024)S(1)}) all-reduce(f32[768]{0:T(1024)S(1)} %reduce.8, f32[4,192]{1,0:T(4,128)S(1)} %slice.111, f32[768]{0:T(1024)S(1)} %reduce.9), channel_id=4, replica_groups=mesh['dp'=4,'ctx'=2,'tensor'=4] {'dp','ctx'}, use_global_device_ids=true, to_apply=%region_0.1.clone | all-reduce | flops 2304 | bytes 18432
  542.5 1.6 copy.88
  544.1 1.8 select_bitcast_fusion.3
  545.9 1.9 pad_maximum_fusion.7
  548.9 1.6 select_bitcast_fusion.1
  550.6 1.9 pad_maximum_fusion.8
  552.4 1.8 fusion.4
  554.2 43.1 %reduce-scatter.10.cloned.1.call-done = f32[96,768]{1,0:T(8,128)} async-done(((f32[768,768]{1,0:T(8,128)}), f32[96,768]{1,0:T(8,128)}) %reduce-scatter.10.cloned.1.call-update) | async-done | bytes 294928 | tf_op jit(solution)/shard_map/reduce_scatter | solution.py:862
  597.4 46.3 %reduce-scatter.12.cloned.1.call-done = f32[96,768]{1,0:T(8,128)} async-done(((f32[768,768]{1,0:T(8,128)}), f32[96,768]{1,0:T(8,128)}) %reduce-scatter.12.cloned.1.call-update) | async-done | bytes 294928 | tf_op jit(solution)/shard_map/reduce_scatter | solution.py:862
  (113 shorter events, 24.6 us)
Async XLA Ops:
  7.2 93.5 %all-gather.5.cloned.1.call-start = ((), (), s32[]{:S(2)}) async-start(), calls=%async_computation.8 | async-start | bytes 10543104 | tf_op jit(solution)/shard_map/all_gather | solution.py:758
  12.4 222.0 %all-gather.7.cloned.1.call-start = ((), (), s32[]{:S(2)}) async-start(), calls=%async_computation.9 | async-start | bytes 19464192 | tf_op jit(solution)/shard_map/all_gather | solution.py:758
  14.3 528.2 %reduce-scatter.8.cloned.1.call-start = ((), (), s32[]{:S(2)}) async-start(), calls=%async_computation.5 | async-start | bytes 884736 | tf_op jit(solution)/shard_map/reduce_scatter | solution.py:862
  14.4 4.4 copy-start.4
  15.3 9.2 %copy-start.3 = (f32[2,512,768]{2,1,0:T(8,128)S(1)}, f32[2,512,768]{2,1,0:T(8,128)}, u32[]{:S(2)}) copy-start(f32[2,512,768]{2,1,0:T(8,128)} %param.25) | copy-start | bytes 9437188
  15.3 6.1 collective-permute-start.1
  18.8 5.7 collective-permute-start.2
  20.0 8.0 %collective-permute-start = (f32[512,768]{1,0:T(8,128)}, f32[512,768]{1,0:T(8,128)}, u32[]{:S(2)}, u32[]{:S(2)}) collective-permute-start(f32[512,768]{1,0:T(8,128)} %dynamic-slice_bitcast_fusion.1), channel_id=1, source_target_pairs={{0,4},{4,0},{1,5},{5,1},{2,6},{6,2},{3,7},{7,3},{8,12},{12,8},{9,1... | collective-permute-start | bytes 4718600 | tf_op jit(solution)/shard_map/ppermute | solution.py:819
  26.1 3.0 copy-start.5
  105.3 1.5 copy-start
  105.3 2.3 copy-start.1
  105.3 3.2 copy-start.2
  430.6 121.9 %reduce-scatter.6.cloned.1.call-start = ((), (), s32[]{:S(2)}) async-start(), calls=%async_computation.4 | async-start | bytes 2211840 | tf_op jit(solution)/shard_map/reduce_scatter | solution.py:862
  510.4 1.9 copy-start.6
  510.5 86.9 %reduce-scatter.10.cloned.1.call-start = ((), (), s32[]{:S(2)}) async-start(), calls=%async_computation.6 | async-start | bytes 2654208 | tf_op jit(solution)/shard_map/reduce_scatter | solution.py:862
  511.1 132.6 %reduce-scatter.12.cloned.1.call-start = ((), (), s32[]{:S(2)}) async-start(), calls=%async_computation.7 | async-start | bytes 2654208 | tf_op jit(solution)/shard_map/reduce_scatter | solution.py:862
  511.6 2.3 copy-start.7
  512.3 3.1 copy-start.11
  512.3 5.0 copy-start.10
  512.3 5.0 copy-start.9
  513.6 30.5 %collective-permute-start.3 = (f32[512,768]{1,0:T(8,128)}, f32[512,768]{1,0:T(8,128)}, u32[]{:S(2)}, u32[]{:S(2)}) collective-permute-start(f32[512,768]{1,0:T(8,128)} %constant_dynamic-slice_fusion.1), channel_id=1, source_target_pairs={{0,4},{4,0},{1,5},{5,1},{2,6},{6,2},{3,7},{7,3},{8,12},{12,8},{9,1... | collective-permute-start | bytes 4718600 | tf_op jit(solution)/shard_map/ppermute | solution.py:830
  515.2 32.6 %collective-permute-start.4 = (f32[512,768]{1,0:T(8,128)}, f32[512,768]{1,0:T(8,128)}, u32[]{:S(2)}, u32[]{:S(2)}) collective-permute-start(f32[512,768]{1,0:T(8,128)} %constant_dynamic-slice_fusion), channel_id=1, source_target_pairs={{0,4},{4,0},{1,5},{5,1},{2,6},{6,2},{3,7},{7,3},{8,12},{12,8},{9,1... | collective-permute-start | bytes 4718600 | tf_op jit(solution)/shard_map/ppermute | solution.py:830
  545.9 3.0 copy-start.8
Sparse Core Ops, SparseCore 0:
  12.5 88.1 all-gather.4
  103.6 123.2 all-gather.6
  430.7 32.7 reduce-scatter.7
  510.6 40.0 reduce-scatter.5
  554.8 42.4 reduce-scatter.9
  601.1 42.4 reduce-scatter.11

commit v2 on v0

--- a/solution.py
+++ b/solution.py
@@ -3,6 +3,8 @@
 import jax
 import jax.numpy as jnp
 from jax import lax
+from jax.experimental import pallas as pl
+from jax.experimental.pallas import tpu as pltpu
 from jax.sharding import PartitionSpec as P
 
 SUBBLOCK = 64
@@ -309,9 +311,915 @@
     return (layer_output, input_grad) + all_parts
 
 
+PAIR = 2
+BLOCK = 128
+LANES = 128
+LIMIT = 60
+TILE = 256
+C_GELU = 0.7978845608028654
+NN = ((1,), (0,))
+NT = ((1,), (1,))
+TN = ((0,), (0,))
+f32, bf16 = jnp.float32, jnp.bfloat16
+
+
+def params(limit=LIMIT):
+    return pltpu.CompilerParams(vmem_limit_bytes=limit * 2**20)
+
+
+def cost(flops, moved):
+    return pl.CostEstimate(flops=int(flops), bytes_accessed=int(moved), transcendentals=0)
+
+
+def shaped(shape, dtype=jnp.float32):
+    return jax.ShapeDtypeStruct(shape, dtype)
+
+
+def split(a):
+    high = a.astype(bf16)
+    return high, (a - high.astype(f32)).astype(bf16)
+
+
+def d3(left, right, dims):
+    dot = partial(lax.dot_general, dimension_numbers=(dims, ((), ())), preferred_element_type=f32)
+    return dot(left[0], right[0]) + dot(left[1], right[0]) + dot(left[0], right[1])
+
+
+def d3_low(left, right, dims):
+    dot = partial(lax.dot_general, dimension_numbers=(dims, ((), ())), preferred_element_type=f32)
+    rows = left[0].shape[0]
+    both = dot(jnp.concatenate(left, axis=0), right[0])
+    return both[:rows] + both[rows:] + dot(left[0], right[1])
+
+
+def tied(arrays):
+    specs = [
+        pl.BlockSpec((1,) * (a.ndim - 2) + (8, 128), lambda *_, n=a.ndim: (0,) * n) for a in arrays
+    ]
+    return specs, list(arrays)
+
+
+def norm_parts(v):
+    centered = v - jnp.mean(v, axis=-1, keepdims=True)
+    r = lax.rsqrt(jnp.mean(centered * centered, axis=-1, keepdims=True) + eps)
+    return centered * r, r
+
+
+def whole(shape):
+    return pl.BlockSpec(
+        shape, lambda *_: (0,) * len(shape), pipeline_mode=pl.Buffered(buffer_count=1)
+    )
+
+
+def scalar():
+    return pl.BlockSpec(memory_space=pltpu.SMEM)
+
+
+def pack_mixer_kernel(me_ref, q_ref, k_ref, v_ref, m_ref, mg_ref, fg_ref, kern_ref, decay_ref, o_ref):
+    rows, own = q_ref.shape
+    taps, few = kern_ref.shape
+    heads, width = decay_ref.shape
+    o_ref[0:rows, 0:own] = q_ref[...]
+    o_ref[0:rows, own : 2 * own] = k_ref[...]
+    o_ref[0:rows, 2 * own : 3 * own] = v_ref[...]
+    o_ref[0:rows, 3 * own :] = jnp.transpose(m_ref[...])
+    o_ref[rows:, :] = jnp.zeros((8, o_ref.shape[1]), f32)
+    for b in range(8):
+
+        @pl.when(me_ref[0] == b)
+        def _():
+            o_ref[rows : rows + 1, b * rows : (b + 1) * rows] = mg_ref[...]
+            o_ref[rows + 1 : rows + 2, b * rows : (b + 1) * rows] = fg_ref[...]
+            o_ref[rows + 2 : rows + 2 + taps, b * few : (b + 1) * few] = kern_ref[...]
+
+    @pl.when(me_ref[0] == 0)
+    def _():
+        for h in range(heads):
+            at = rows + 2 + taps
+            o_ref[at : at + 1, h * width : (h + 1) * width] = decay_ref[h : h + 1, :]
+
+
+def run_pack_mixer(me, q, k, v, m, mg, fg, kern, decay):
+    rows, own = q.shape
+    args = (q, k, v, m, mg[None], fg[None], kern, decay)
+    return pl.pallas_call(
+        pack_mixer_kernel,
+        grid=(1,),
+        in_specs=[scalar()] + [whole(a.shape) for a in args],
+        out_specs=whole((rows + 8, 4 * own)),
+        out_shape=shaped((rows + 8, 4 * own)),
+        compiler_params=params(),
+        cost_estimate=cost(1e6, 2**20),
+        name="pack_mixer",
+    )(me, *args)
+
+
+def pack_feed_kernel(up_ref, down_ref, o_ref):
+    hidden = up_ref.shape[1]
+    o_ref[:, :hidden] = up_ref[...]
+    o_ref[:, hidden:] = jnp.transpose(down_ref[...])
+
+
+def run_pack_feed(up, down):
+    return pl.pallas_call(
+        pack_feed_kernel,
+        grid=(1,),
+        in_specs=[whole(up.shape), whole(down.shape)],
+        out_specs=whole((up.shape[0], 2 * up.shape[1])),
+        out_shape=shaped((up.shape[0], 2 * up.shape[1])),
+        compiler_params=params(),
+        cost_estimate=cost(1e6, 2 * 2**20),
+        name="pack_feed",
+    )(up, down)
+
+
+def sequence_specs(model, order):
+    def mine(i, m):
+        return (m[0] & 1, order(i, m) % 2, 0)
+
+    def came(i, m):
+        return (order(i, m) % 2, 0)
+
+    return [pl.BlockSpec((1, TILE, model), mine), pl.BlockSpec((TILE, model), came)]
+
+
+def sequence_tile(tile, me_ref, mine_ref, came_ref):
+    own = tile // 2 == (me_ref[0] & 1)
+    return jnp.where(own, mine_ref[0], came_ref[...])
+
+
+def project_kernel(me_ref, x_ref, xr_ref, *refs):
+    first, second = refs[0:8], refs[8:16]
+    o_ref, wh_ref, wl_ref, mh_ref, ml_ref, gains_ref, small_ref = refs[-7:]
+    own = first[0].shape[1] // 4
+    rows = wh_ref.shape[0] // 8
+
+    @pl.when(pl.program_id(0) == 0)
+    def _():
+        for r in range(8):
+            at = pl.ds(pl.multiple_of((me_ref[0] ^ r) * rows, rows), rows)
+            a, b = first[r][0:rows, :], second[r][0:rows, :]
+            for i in range(4):
+                both = jnp.concatenate(
+                    [a[:, i * own : (i + 1) * own], b[:, i * own : (i + 1) * own]], axis=1
+                )
+                high, low = split(both)
+                if i < 3:
+                    wh_ref[at, i * 2 * own : (i + 1) * 2 * own] = high
+                    wl_ref[at, i * 2 * own : (i + 1) * 2 * own] = low
+                else:
+                    mh_ref[at, :] = high
+                    ml_ref[at, :] = low
+        sums = []
+        for pieces in (first, second):
+            total = pieces[0][rows:, :]
+            for r in range(1, 8):
+                total = total + pieces[r][rows:, :]
+            sums.append(total)
+        gains_ref[...] = sums[0]
+        small_ref[...] = jnp.concatenate([s[:, :own] for s in sums], axis=1)
+
+    x = sequence_tile(pl.program_id(0), me_ref, x_ref, xr_ref)
+    n = split(norm_parts(x)[0] * gains_ref[0:1, :])
+    o_ref[...] = d3(n, (wh_ref[...], wl_ref[...]), NN)
+
+
+def run_project(me, x, first, second, ties=()):
+    rows, half, model = x[0].shape
+    tokens = rows * half
+    own = first[0].shape[1] // 4
+    wide = 6 * own
+    piece = whole(first[0].shape)
+    weights = [(model, wide)] * 2 + [(model, 2 * own)] * 2
+    few = [(8, model), (8, 2 * own)]
+    tie_specs, tie_args = tied(ties)
+    return pl.pallas_call(
+        project_kernel,
+        grid_spec=pltpu.PrefetchScalarGridSpec(
+            num_scalar_prefetch=1,
+            grid=(tokens // TILE,),
+            in_specs=sequence_specs(model, lambda i, m: i) + [piece] * 16 + tie_specs,
+            out_specs=[pl.BlockSpec((TILE, wide), lambda i, m: (i, 0))]
+            + [whole(s) for s in weights + few],
+        ),
+        out_shape=[shaped((tokens, wide))]
+        + [shaped(s, bf16) for s in weights]
+        + [shaped(s) for s in few],
+        compiler_params=params(),
+        cost_estimate=cost(6 * tokens * model * wide, 20 * 2**20),
+        name="project",
+    )(me, *x, *first, *second, *tie_args)
+
+
+def spread(parts, masks):
+    return tuple(jnp.concatenate([p * m for m in masks], axis=0) for p in parts)
+
+
+def lane_masks(lanes):
+    which = lax.broadcasted_iota(jnp.int32, (1, lanes), 1) // (lanes // PAIR)
+    return [jnp.where(which == h, 1.0, 0.0).astype(bf16) for h in range(PAIR)]
+
+
+def square_mask(lanes):
+    a = lax.broadcasted_iota(jnp.int32, (lanes, lanes), 0) // (lanes // PAIR)
+    b = lax.broadcasted_iota(jnp.int32, (lanes, lanes), 1) // (lanes // PAIR)
+    return jnp.where(a == b, 1.0, 0.0)
+
+
+def fill_tables(decay, grow, shrink, dec, end, full):
+    size, model = grow.shape
+    lanes = dec.shape[0]
+    rates = jnp.log(decay)
+    position = lax.broadcasted_iota(jnp.int32, (size, model), 0).astype(f32)
+    grow[...] = jnp.exp(position * rates)
+    shrink[...] = jnp.exp(-position * rates)
+    for p in range(model // lanes):
+        s = slice(p * lanes, (p + 1) * lanes)
+        column = jnp.transpose(jnp.broadcast_to(rates[:, s], (lanes, lanes)))
+        dec[:, s] = jnp.exp(column)
+        end[:, s] = jnp.exp((size - 1.0) * column)
+        full[:, s] = jnp.exp(float(size) * column)
+
+
+def joined(extended, size, taps):
+    now = extended[8:]
+    return [jnp.where(extended[8 - j : 8 - j + size] == now, 1.0, 0.0) for j in range(1, taps)]
+
+
+def shift_forward(keys, before, kern, same, taps):
+    extended = jnp.concatenate([before, keys], axis=0)
+    size = keys.shape[0]
+    moved = [keys]
+    for j in range(1, taps):
+        moved.append(extended[8 - j : 8 - j + size] * same[j - 1])
+    total = kern[0:1, :] * keys
+    for j in range(1, taps):
+        total = total + kern[j : j + 1, :] * moved[j]
+    return total, moved
+
+
+def allowed_masks(seg, row):
+    size, wide = seg.shape[0], row.shape[1]
+    rows = lax.broadcasted_iota(jnp.int32, (size, wide), 0)
+    cols = lax.broadcasted_iota(jnp.int32, (size, wide), 1) % size
+    same = seg == row
+    return (
+        jnp.where(jnp.logical_and(rows >= cols, same), 1.0, 0.0),
+        jnp.where(jnp.logical_and(rows <= cols, same), 1.0, 0.0),
+    )
+
+
+def pair(a_ref, b_ref):
+    return jnp.concatenate([a_ref[...], b_ref[...]], axis=1)
+
+
+def third_of(refs, rows, i):
+    wide = refs[0].shape[1] // 3
+    return jnp.concatenate([r[rows, i * wide : (i + 1) * wide] for r in refs], axis=1)
+
+
+def mixer_kernel(
+    taps, me_ref, x_ref, xr_ref, pa_ref, pb_ref, seg_ref, segrow_ref, sa_ref, sb_ref, gains_ref,
+    ah_ref, al_ref, bh_ref, bl_ref, own_ref, state_out_ref, resid_ref, nh_ref, nl_ref,
+    state, tail, segtail, grow, shrink, dec, end, full, mixed,
+):
+    size, lanes = grow.shape[0], dec.shape[0]
+    projs = (pa_ref, pb_ref)
+
+    @pl.when(pl.program_id(0) == 0)
+    def _():
+        state[...] = jnp.zeros_like(state)
+        tail[...] = jnp.zeros_like(tail)
+        segtail[...] = jnp.full_like(segtail, -1.0)
+        fill_tables(pair(sa_ref, sb_ref)[2 + taps : 3 + taps], grow, shrink, dec, end, full)
+
+    kern = pair(sa_ref, sb_ref)[2 : 2 + taps]
+    masks = lane_masks(lanes)
+    square = square_mask(lanes)
+    model = state.shape[1]
+    groups = [slice(g * lanes, (g + 1) * lanes) for g in range(model // lanes)]
+    before_keys, before = tail[...], segtail[...]
+    for chunk in range(xr_ref.shape[0] // size):
+        here = slice(chunk * size, (chunk + 1) * size)
+        seg = seg_ref[here, :]
+        extended = jnp.concatenate([before, seg], axis=0)
+        living = jnp.where(seg == before[7:8], 1.0, 0.0)
+        kept = jnp.where(seg == seg[size - 1 :], 1.0, 0.0)
+        goes_on = living[size - 1 :]
+        q_all, keys, v_all = (third_of(projs, here, i) for i in range(3))
+        shifted, _ = shift_forward(keys, before_keys, kern, joined(extended, size, taps), taps)
+        before_keys, before = keys[size - 8 :, :], seg[size - 8 :]
+        allowed, _ = allowed_masks(seg, segrow_ref[chunk])
+        state_out_ref[chunk] = state[...]
+        qg, kf, v, scores = [], [], [], []
+        for s in groups:
+            qg.append(split(q_all[:, s] * grow[:, s]))
+            kf.append(shifted[:, s] * shrink[:, s])
+            v.append(split(v_all[:, s]))
+            scores.append(d3_low(qg[-1], spread(split(kf[-1]), masks), NT))
+        updates = [d3(split(k * kept), w, TN) * square for k, w in zip(kf, v)]
+        weights = [split(score * allowed) for score in scores]
+        for g, s in enumerate(groups):
+            part = d3_low(weights[g], spread(v[g], masks), NN)
+            mixed[here, s] = part + living * d3_low(qg[g], split(state[:, s] * dec[:, s]), NN)
+        for g, s in enumerate(groups):
+            state[:, s] = state[:, s] * (full[:, s] * goes_on) + end[:, s] * updates[g]
+    tail[...] = before_keys
+    segtail[...] = before
+    own_ref[...] = mixed[:, : own_ref.shape[1]]
+    third = ah_ref.shape[1]
+    resid = (
+        sequence_tile(pl.program_id(0), me_ref, x_ref, xr_ref)
+        + d3(split(mixed[:, :third]), (ah_ref[...], al_ref[...]), NT)
+        + d3(split(mixed[:, third:]), (bh_ref[...], bl_ref[...]), NT)
+    )
+    resid_ref[...] = resid
+    nh_ref[...], nl_ref[...] = split(norm_parts(resid)[0] * gains_ref[1:2, :])
+
+
+def mixer_scratch(model):
+    return [pltpu.VMEM((BLOCK, model), f32)] * 2 + [pltpu.VMEM((LANES, model), f32)] * 3
+
+
+def run_mixer(me, x, projs, seg, segrow, smalls, gains, a, b, taps):
+    tokens, model = projs[0].shape[0], x[0].shape[2]
+    act = (tokens, model)
+    chunks = TILE // BLOCK
+    row = pl.BlockSpec((TILE, model), lambda c, m: (c, 0))
+    proj = pl.BlockSpec((TILE, projs[0].shape[1]), lambda c, m: (c, 0))
+    states = (tokens // BLOCK, LANES, model)
+    return pl.pallas_call(
+        partial(mixer_kernel, taps),
+        grid_spec=pltpu.PrefetchScalarGridSpec(
+        num_scalar_prefetch=1,
+        grid=(tokens // TILE,),
+        in_specs=sequence_specs(model, lambda i, m: i) + [
+            proj, proj,
+            pl.BlockSpec((TILE, 1), lambda c, m: (c, 0)),
+            pl.BlockSpec((chunks, 1, segrow.shape[2]), lambda c, m: (c, 0, 0)),
+            whole(smalls[0].shape), whole(smalls[1].shape), whole(gains.shape),
+        ]
+        + [whole(a[0].shape)] * 4,
+        out_specs=[
+            pl.BlockSpec((TILE, 256), lambda c, m: (c, 0)),
+            pl.BlockSpec((chunks, LANES, model), lambda c, m: (c, 0, 0)),
+            row, row, row,
+        ],
+        scratch_shapes=[
+            pltpu.VMEM((LANES, model), f32), pltpu.VMEM((8, model), f32), pltpu.VMEM((8, 1), f32)
+        ]
+        + mixer_scratch(model)
+        + [pltpu.VMEM((TILE, model), f32)],
+        ),
+        out_shape=[
+            shaped((tokens, 256)), shaped(states), shaped(act),
+            shaped(act, bf16), shaped(act, bf16),
+        ],
+        compiler_params=params(),
+        cost_estimate=cost(3e10, 30 * 2**20),
+        name="mixer",
+    )(me, *x, *projs, seg, segrow, *smalls, gains, *a, *b)
+
+
+def mixer_back_kernel(
+    taps, me_ref, fng_ref, resid_ref, x_ref, xr_ref, ct_ref, cr_ref, pa_ref, pb_ref, ba_ref, bb_ref, state_ref,
+    mixed_ref, seg_ref, segb_ref, segrow_ref, sa_ref, sb_ref, gains_ref,
+    ah_ref, al_ref, bh_ref, bl_ref, *refs,
+):
+    (
+        rg_ref, dq_ref, dk_ref, dv_ref, gg_ref, dkern_ref, keep_ref, send_ref,
+        grad, head, grow, shrink, dec, end, full, du_all, wg,
+    ) = refs[-17:]
+    size, lanes = grow.shape[0], dec.shape[0]
+    step, steps = pl.program_id(0), pl.num_programs(0)
+    projs = (pa_ref, pb_ref)
+
+    @pl.when(step == 0)
+    def _():
+        grad[...] = jnp.zeros_like(grad)
+        head[...] = jnp.zeros_like(head)
+        dkern_ref[...] = jnp.zeros_like(dkern_ref)
+        gg_ref[...] = jnp.zeros_like(gg_ref)
+        wg[...] = jnp.zeros_like(wg)
+        fill_tables(pair(sa_ref, sb_ref)[2 + taps : 3 + taps], grow, shrink, dec, end, full)
+
+    third = ah_ref.shape[1]
+    back, gain_grad, _ = norm_back(resid_ref[...], gains_ref[1:2, :], fng_ref[...])
+    tile = steps - 1 - step
+    rg = sequence_tile(tile, me_ref, ct_ref, cr_ref) + back
+    rg_ref[...] = rg
+    gg_ref[...] += gain_grad
+    r2 = split(rg)
+    du_all[:, :third] = d3(r2, (ah_ref[...], al_ref[...]), NN)
+    du_all[:, third:] = d3(r2, (bh_ref[...], bl_ref[...]), NN)
+
+    kern = pair(sa_ref, sb_ref)[2 : 2 + taps]
+    masks = lane_masks(lanes)
+    square = square_mask(lanes)
+    model = grad.shape[1]
+    groups = [slice(g * lanes, (g + 1) * lanes) for g in range(model // lanes)]
+    count = len(groups)
+    chunks = rg.shape[0] // size
+    for chunk in reversed(range(chunks)):
+        here = slice(chunk * size, (chunk + 1) * size)
+        seg = seg_ref[here, :]
+        q_all, keys, v_all = (third_of(projs, here, i) for i in range(3))
+        if chunk:
+            just = slice(chunk * size - 8, chunk * size)
+            before, before_keys = seg_ref[just, :], third_of(projs, just, 1)
+        else:
+            before = jnp.where(step == steps - 1, -1.0, segb_ref[...])
+            before_keys = pair(ba_ref, bb_ref)
+        extended = jnp.concatenate([before, seg], axis=0)
+        living = jnp.where(seg == before[7:8], 1.0, 0.0)
+        kept = jnp.where(seg == seg[size - 1 :], 1.0, 0.0)
+        goes_on = living[size - 1 :]
+        same = joined(extended, size, taps)
+        shifted, moved = shift_forward(keys, before_keys, kern, same, taps)
+        allowed, allowed_t = allowed_masks(seg, segrow_ref[chunk])
+        qf = [q_all[:, s] * grow[:, s] for s in groups]
+        qg = [split(q) for q in qf]
+        kg = [split(shifted[:, s] * shrink[:, s]) for s in groups]
+        v = [split(v_all[:, s]) for s in groups]
+        du = [split(du_all[here, s]) for s in groups]
+        p_t = [d3_low(kg[g], spread(qg[g], masks), NT) for g in range(count)]
+        dp = [d3_low(du[g], spread(v[g], masks), NT) for g in range(count)]
+        dp_t = [d3_low(v[g], spread(du[g], masks), NT) for g in range(count)]
+        updates = [d3(split(qf[g] * living), du[g], TN) * square for g in range(count)]
+        p_t = [split(p * allowed_t) for p in p_t]
+        dp = [split(p * allowed) for p in dp]
+        dp_t = [split(p * allowed_t) for p in dp_t]
+        for g, s in enumerate(groups):
+            entering = split(state_ref[chunk, :, s] * dec[:, s])
+            leaving = split(grad[:, s] * end[:, s])
+            dqg = d3_low(dp[g], spread(kg[g], masks), NN) + living * d3_low(du[g], entering, NT)
+            dkg = d3_low(dp_t[g], spread(qg[g], masks), NN) + kept * d3_low(v[g], leaving, NT)
+            dv_ref[here, s] = d3_low(p_t[g], spread(du[g], masks), NN) + kept * d3_low(
+                kg[g], leaving, NN
+            )
+            dq_ref[here, s] = dqg * grow[:, s]
+            dshift = dkg * shrink[:, s]
+            grad[:, s] = grad[:, s] * (full[:, s] * goes_on) + dec[:, s] * updates[g]
+            total = kern[0:1, s] * dshift
+            for j in range(1, taps):
+                part = dshift * same[j - 1]
+                longer = jnp.concatenate([part, head[j - 1, :, s]], axis=0)
+                total = total + kern[j : j + 1, s] * longer[j : j + size]
+                head[j - 1, :, s] = part[0:8]
+            dk_ref[here, s] = total
+            if g < 2:
+                for j in range(taps):
+                    dkern_ref[j : j + 1, s] += jnp.sum(
+                        dshift * moved[j][:, s], axis=0, keepdims=True
+                    )
+
+    own = keep_ref.shape[-1] // 4
+    x = sequence_tile(tile, me_ref, x_ref, xr_ref)
+    n = split(norm_parts(x)[0] * gains_ref[0:1, :])
+    joint = jnp.concatenate([r[:, :own] for r in (dq_ref, dk_ref, dv_ref)], axis=1)
+    wg[:, : 3 * own] += d3(n, split(joint), TN)
+    wg[:, 3 * own :] += d3(r2, split(mixed_ref[:, :own]), TN)
+
+    @pl.when(step == steps - 1)
+    def _():
+        store_blocks(me_ref[0], wg, keep_ref, send_ref, 0)
+
+
+def run_mixer_back(
+    me, fng, resid, x, ct, projs, states, mixed, seg, segrow, smalls, gains, a, b, taps, ties=()
+):
+    tokens, model = resid.shape
+    third = projs[0].shape[1] // 3
+    own = third // 2
+    chunks = TILE // BLOCK
+    last = tokens // TILE - 1
+    blocks = (1, 4, model // 8, 4 * own)
+    tie_specs, tie_args = tied(ties)
+
+    def prior(c):
+        return jnp.maximum((last - c) * (TILE // 8) - 1, 0)
+
+    row = pl.BlockSpec((TILE, model), lambda c, m: (last - c, 0))
+    proj = pl.BlockSpec((TILE, 3 * third), lambda c, m: (last - c, 0))
+    before = pl.BlockSpec((8, third), lambda c, m: (prior(c), 1))
+    return pl.pallas_call(
+        partial(mixer_back_kernel, taps),
+        grid_spec=pltpu.PrefetchScalarGridSpec(
+        num_scalar_prefetch=1,
+        grid=(last + 1,),
+        in_specs=[row, row]
+        + sequence_specs(model, lambda c, m: last - c) * 2
+        + [
+            proj, proj, before, before,
+            pl.BlockSpec((chunks, LANES, model), lambda c, m: (last - c, 0, 0)),
+            pl.BlockSpec((TILE, 256), lambda c, m: (last - c, 0)),
+            pl.BlockSpec((TILE, 1), lambda c, m: (last - c, 0)),
+            pl.BlockSpec((8, 1), lambda c, m: (prior(c), 0)),
+            pl.BlockSpec((chunks, 1, segrow.shape[2]), lambda c, m: (last - c, 0, 0)),
+            whole(smalls[0].shape), whole(smalls[1].shape), whole(gains.shape),
+        ]
+        + [whole(a[0].shape)] * 4
+        + tie_specs,
+        out_specs=[row] * 4 + [whole((1, model)), whole((taps, model)), whole(blocks), whole(blocks)],
+        scratch_shapes=[
+            pltpu.VMEM((LANES, model), f32), pltpu.VMEM((taps - 1, 8, model), f32)
+        ]
+        + mixer_scratch(model)
+        + [pltpu.VMEM((TILE, model), f32), pltpu.VMEM((model, 4 * own), f32)],
+        ),
+        out_shape=[shaped((tokens, model))] * 4
+        + [shaped((1, model)), shaped((taps, model)), shaped(blocks), shaped(blocks)],
+        compiler_params=params(),
+        cost_estimate=cost(8e10, 50 * 2**20),
+        name="mixer_back",
+    )(
+        me, fng, resid, *x, *ct, *projs, *projs, states, mixed, seg, seg, segrow, *smalls, gains,
+        *a, *b, *tie_args,
+    )
+
+
+def gelu_parts(pre, back):
+    th = jnp.tanh(pre * (C_GELU + (C_GELU * 0.044715) * (pre * pre)))
+    half = 0.5 + 0.5 * th
+    act = pre * half
+    slope = half + (1.0 - th) * act * (C_GELU + (3 * C_GELU * 0.044715) * (pre * pre))
+    return act, back * slope
+
+
+def store_blocks(me, g, keep_ref, send_ref, i):
+    rows = g.shape[0] // 8
+    for b in range(8):
+        r = me ^ b
+        part = g[b * rows : (b + 1) * rows]
+        where = r // 2
+
+        @pl.when((r & 1) == 0)
+        def _():
+            keep_ref[i, where] = part
+
+        @pl.when((r & 1) == 1)
+        def _():
+            send_ref[i, where] = part
+
+
+def feed_kernel(own, final, me_ref, nh_ref, nl_ref, ct_ref, cr_ref, out_in, fng_in, w_in, *refs):
+    if own:
+        out_ref, fng_ref, wg, w = refs[-4:]
+    else:
+        out_ref, fng_ref, w = refs[-3:]
+    step = pl.program_id(0)
+    hidden = w.shape[2] // 2
+
+    @pl.when(step == 0)
+    def _():
+        w[0], w[1] = split(w_in[...].reshape(w.shape[1:]))
+        if own:
+            wg[...] = jnp.zeros_like(wg)
+
+    tile = theirs_first(step, me_ref)
+    n = (nh_ref[...], nl_ref[...])
+    ct = split(sequence_tile(tile, me_ref, ct_ref, cr_ref))
+    u, d = (w[0, :, :hidden], w[1, :, :hidden]), (w[0, :, hidden:], w[1, :, hidden:])
+    act, grad = gelu_parts(d3(n, u, NN), d3(ct, d, NN))
+    act, grad = split(act), split(grad)
+    out_ref[...] = (out_in[...] + d3(act, d, NT)).reshape(out_ref.shape)
+    more = d3(grad, u, NT)
+    fng_ref[...] = more if own else fng_in[...] + more
+    if own:
+        wg[:, :hidden] += d3(n, grad, TN)
+        wg[:, hidden:] += d3(ct, act, TN)
+
+
+def theirs_first(step, me):
+    core = me[0] & 1
+    return jnp.where(step < 2, 1 - core, core) * 2 + (step & 1)
+
+
+def run_feed(me, n, ct, out, fng, w, own, final=False, ties=()):
+    tokens, model = n[0].shape
+    wide = w.shape[1]
+    row = pl.BlockSpec((TILE, model), lambda i, m: (theirs_first(i, m), 0))
+    tie_specs, tie_args = tied(ties)
+    full = shaped((tokens, model))
+    last = pl.BlockSpec((1, TILE, model), lambda i, m: (theirs_first(i, m) // 2, i % 2, 0))
+    return pl.pallas_call(
+        partial(feed_kernel, own, final),
+        grid_spec=pltpu.PrefetchScalarGridSpec(
+            num_scalar_prefetch=1,
+            grid=(tokens // TILE,),
+            in_specs=[row] * 2
+            + sequence_specs(model, theirs_first)
+            + [row] * 2
+            + [whole(w.shape)]
+            + tie_specs,
+            out_specs=[last if final else row, row] + ([whole((model, wide))] if own else []),
+            scratch_shapes=[pltpu.VMEM((2, model, wide), bf16)],
+        ),
+        out_shape=[shaped((2, tokens // 2, model)) if final else full, full]
+        + ([shaped((model, wide))] if own else []),
+        compiler_params=params(),
+        cost_estimate=cost((6 if own else 4) * 3 * tokens * model * wide, 30 * 2**20),
+        name="feed_own" if own else "feed",
+    )(me, *n, *ct, out, fng, w, *tie_args)
+
+
+def norm_back(v, gain, incoming):
+    xhat, r = norm_parts(v)
+    scaled = incoming * gain
+    grad = r * (
+        scaled
+        - jnp.mean(scaled, axis=-1, keepdims=True)
+        - xhat * jnp.mean(scaled * xhat, axis=-1, keepdims=True)
+    )
+    return grad, jnp.sum(incoming * xhat, axis=0, keepdims=True), xhat
+
+
+def input_back_kernel(
+    other, me_ref, x_ref, xr_ref, rg_ref, gains_ref, ah_ref, al_ref, bh_ref, bl_ref,
+    dq_ref, dk_ref, dv_ref, *refs,
+):
+    x = xr_ref[...] if other else x_ref[0]
+    third = ah_ref.shape[1] // 3
+    parts = (dq_ref, dk_ref, dv_ref)
+    left = split(jnp.concatenate([r[:, :third] for r in parts], axis=1))
+    right = split(jnp.concatenate([r[:, third:] for r in parts], axis=1))
+    incoming = d3(left, (ah_ref[...], al_ref[...]), NT) + d3(right, (bh_ref[...], bl_ref[...]), NT)
+    grad = rg_ref[...] + norm_back(x, gains_ref[0:1, :], incoming)[0]
+    refs[-1][...] = grad.reshape(refs[-1].shape)
+
+
+def run_input_back(me, other, x, rg, gains, a, b, dq, dk, dv, ties=()):
+    tokens, model = rg.shape
+    tie_specs, tie_args = tied(ties)
+
+    def tile(i, m):
+        core = m[0] & 1
+        return (1 - core if other else core) * 2 + i
+
+    row = pl.BlockSpec((TILE, model), lambda i, m: (tile(i, m), 0))
+    return pl.pallas_call(
+        partial(input_back_kernel, other),
+        grid_spec=pltpu.PrefetchScalarGridSpec(
+            num_scalar_prefetch=1,
+            grid=(tokens // 2 // TILE,),
+            in_specs=sequence_specs(model, tile)
+            + [row, whole(gains.shape)]
+            + [whole(a[0].shape)] * 4
+            + [row, row, row]
+            + tie_specs,
+            out_specs=pl.BlockSpec((TILE, model), lambda i, m: (i, 0))
+            if other
+            else pl.BlockSpec((1, TILE, model), lambda i, m: (m[0] & 1, i, 0)),
+        ),
+        out_shape=shaped((tokens // 2, model) if other else (2, tokens // 2, model)),
+        compiler_params=params(),
+        cost_estimate=cost(9 * tokens * model * model, 20 * 2**20),
+        name="input_back",
+    )(me, *x, rg, gains, *a, *b, dq, dk, dv, *tie_args)
+
+
+def leave_kernel(me_ref, came_ref, whole_ref, o_ref):
+    o_ref[0] = came_ref[...]
+
+
+def run_leave(me, mine, came):
+    half, model = came.shape
+    return pl.pallas_call(
+        leave_kernel,
+        grid_spec=pltpu.PrefetchScalarGridSpec(
+            num_scalar_prefetch=1,
+            grid=(half // TILE,),
+            in_specs=[
+                pl.BlockSpec((TILE, model), lambda t, m: (t, 0)),
+                pl.BlockSpec(memory_space=pl.ANY),
+            ],
+            out_specs=pl.BlockSpec((1, TILE, model), lambda t, m: (1 - (m[0] & 1), t, 0)),
+        ),
+        out_shape=shaped((2, half, model)),
+        input_output_aliases={2: 0},
+        compiler_params=params(),
+        cost_estimate=cost(1e6, 4 * 2**20),
+        name="leave",
+    )(me, came, mine)
+
+
+def exchange(value, axis, flip):
+    count = lax.axis_size(axis)
+    return lax.ppermute(value, axis, [(i, i ^ flip) for i in range(count)])
+
+
+def corner(value):
+    pairs = []
+    for d in range(4):
+        for c in range(2):
+            pairs.append((d * 2 + c, (d ^ (2 if c == 0 else 1)) * 2 + c))
+    return lax.ppermute(value, ("dp", "ctx"), pairs)
+
+
+def after(values, *earlier):
+    return lax.optimization_barrier((tuple(values), earlier))[0]
+
+
+def sides(block):
+    return [exchange(block, "dp", 1), exchange(block, "dp", 2), exchange(block, "ctx", 1)]
+
+
+def far(from_x, from_y):
+    return corner(jnp.where(lax.axis_index("ctx") == 0, from_x, from_y))
+
+
+def across_cores(*values):
+    return [exchange(v, "ctx", 1) for v in values]
+
+
+def by_distance(block, near, near_other, diagonal, diagonal_other):
+    from_x, from_y, other = near
+    return [
+        block, other, from_x, near_other[0], from_y, near_other[1], diagonal, diagonal_other
+    ]
+
+
+def scatter_core(keep, send):
+    return keep + exchange(send, "ctx", 1)
+
+
+def scatter_corner(mine):
+    core = lax.axis_index("ctx")
+    own, to_x, to_y, to_d = (mine[:, i] for i in range(4))
+    came = corner(to_d)
+    return (
+        own,
+        jnp.where(core == 0, to_x + came, to_x),
+        jnp.where(core == 0, to_y, to_y + came),
+    )
+
+
+def scatter_sides(own, to_x, to_y):
+    return own + exchange(to_x, "dp", 1) + exchange(to_y, "dp", 2)
+
+
+def other_half(block):
+    theirs = lax.dynamic_index_in_dim(block, 1 - lax.axis_index("ctx"), 0, keepdims=False)
+    return exchange(theirs, "ctx", 1)
+
+
+def swap_in(block):
+    me = lax.axis_index("ctx")
+    mine = lax.dynamic_index_in_dim(block, me, 0, keepdims=False)
+    came = other_half(block)
+    return jnp.where(
+        me == 0, jnp.concatenate([mine, came], axis=0), jnp.concatenate([came, mine], axis=0)
+    )
+
+
+def by_sequence(
+    layer_input, segment_ids, mixer_gain, query_weight, key_weight, value_weight, shift_kernel,
+    state_decay, mixer_weight, feed_gain, up_weight, down_weight, cotangent,
+):
+    plane = ("dp", "ctx")
+    position = lax.axis_index("dp") * 2 + lax.axis_index("ctx")
+    me = position.astype(jnp.int32).reshape(1)
+    rows, own = query_weight.shape
+    taps, few = shift_kernel.shape
+
+    def gathered(block):
+        return lax.all_gather(block, plane, axis=0, tiled=True)
+
+    a0 = run_pack_mixer(
+        me, query_weight, key_weight, value_weight, mixer_weight, mixer_gain, feed_gain,
+        shift_kernel, state_decay,
+    )
+    a1 = exchange(a0, "tensor", 1)
+    near0 = sides(a0)
+    up_weight, down_weight, early = after((up_weight, down_weight, layer_input), a0)
+    f0 = run_pack_feed(up_weight, down_weight)
+    x_came = other_half(early)
+
+    b0, b1, near0 = after((a0, a1, near0), f0)
+    a2 = exchange(b0, "tensor", 2)
+    far0 = far(*near0[:2])
+    near1 = exchange(b1, "dp", 1), exchange(b1, "dp", 2)
+    inner = after((*near0[:2], b1), far0)
+    other0 = across_cores(*inner[:2], far0)
+    other1 = exchange(inner[2], "ctx", 1)
+
+    b0, b2, near1 = after((a0, a2, near1), far0, other0, x_came)
+    a3 = exchange(b0, "tensor", 3)
+    far1 = far(*near1)
+    near2 = exchange(b2, "dp", 1), exchange(b2, "dp", 2)
+    inner = after((*near1, b2), far1)
+    near1 = (*near1, other1)
+    other1 = across_cores(*inner[:2], far1)
+    other2 = exchange(inner[2], "ctx", 1)
+    seg = swap_in(segment_ids).astype(f32)
+
+    g0, b3, near2 = after((f0, a3, near2), far1, other1)
+    w0 = gathered(g0)
+    far2 = far(*near2)
+    near3 = exchange(b3, "dp", 1), exchange(b3, "dp", 2)
+    f1 = exchange(g0, "tensor", 1)
+    first0 = by_distance(a0, near0, other0[:2], far0, other0[2])
+    first1 = by_distance(a1, near1, other1[:2], far1, other1[2])
+    x = (layer_input, x_came)
+    proj_a, *wa = run_project(me, x, first0, first1)
+    inner = after((*near2, b3, far2), proj_a, near3)
+    near2 = (*near2, other2)
+    other2 = across_cores(*inner[:2], inner[3])
+    other3 = exchange(inner[2], "ctx", 1)
+
+    near3, g0, late = after((near3, f0, cotangent), far2, proj_a)
+    far3 = far(*near3)
+    f2 = exchange(g0, "tensor", 2)
+    inner = after(near3, far3)
+    near3 = (*near3, other3)
+    other3 = across_cores(*inner, far3)
+    ct = (cotangent, other_half(late))
+    segrow = jnp.tile(seg.reshape(-1, 1, BLOCK), (1, 1, PAIR))
+    seg = seg[:, None]
+    first2 = by_distance(a2, near2, other2[:2], far2, other2[2])
+    first3 = by_distance(a3, near3, other3[:2], far3, other3[2])
+    proj_b, *wb = run_project(me, x, first2, first3)
+    f1, g0 = after((f1, f0), proj_b, ct, seg)
+    w1 = gathered(f1)
+    f3 = exchange(g0, "tensor", 3)
+
+    projs, gains, smalls = (proj_a, proj_b), wa[4], (wa[5], wb[5])
+    mixed, states, resid, nh, nl = run_mixer(
+        me, x, projs, seg, segrow, smalls, gains, wa[2:4], wb[2:4], taps
+    )
+    (f2,) = after((f2,), resid)
+    w2 = gathered(f2)
+    n = (nh, nl)
+    out, fng, feed_g = run_feed(me, n, ct, resid, resid, w0, True)
+    (f3,) = after((f3,), fng)
+    w3 = gathered(f3)
+    out, fng = run_feed(me, n, ct, out, fng, w1, False)
+    out, fng = run_feed(me, n, ct, out, fng, w2, False)
+    halves, fng = run_feed(me, n, ct, out, fng, w3, False, True)
+    feed_g = lax.psum_scatter(feed_g, plane, scatter_dimension=0, tiled=True)
+    came = other_half(halves)
+    rg, dq, dk, dv, feed_gain_g, kern_g, keep, send = run_mixer_back(
+        me, fng, resid, x, ct, projs, states, mixed, seg, segrow, smalls, gains, wa[2:4], wb[2:4],
+        taps,
+    )
+    kern_g = kern_g[:, :own].reshape(taps, 8, few).transpose(1, 0, 2).reshape(8, taps * few)
+    tiny = jnp.concatenate([feed_gain_g.reshape(8, rows), kern_g], axis=1)
+    came_send, came_tiny = exchange(send, "ctx", 1), exchange(tiny, "ctx", 1)
+    layer_output = run_leave(me, halves, came)
+    keep, came_send, tiny, came_tiny = after((keep, came_send, tiny, came_tiny), layer_output)
+    summed = keep + came_send
+    tiny = tiny + came_tiny
+    diagonal, came_tiny = corner(summed[:, 3]), exchange(tiny, "dp", 1)
+    theirs = run_input_back(me, True, x, rg, gains, wa[:2], wb[:2], dq, dk, dv, (summed,))
+    diagonal, theirs, came_tiny = after((diagonal, theirs, came_tiny))
+    tiny = tiny + came_tiny
+    core = lax.axis_index("ctx")
+    to_x = exchange(jnp.where(core == 0, summed[:, 1] + diagonal, summed[:, 1]), "dp", 1)
+    to_y = exchange(jnp.where(core == 0, summed[:, 2], summed[:, 2] + diagonal), "dp", 2)
+    came_tiny = exchange(tiny, "dp", 2)
+    came = exchange(theirs, "ctx", 1)
+    mine = run_input_back(me, False, x, rg, gains, wa[:2], wb[:2], dq, dk, dv, (theirs,))
+    to_x, to_y, came_tiny, came, mine = after((to_x, to_y, came_tiny, came, mine))
+    mixer_g = (summed[:, 0] + to_x + to_y)[0]
+    tiny = lax.dynamic_index_in_dim(tiny + came_tiny, position, 0, keepdims=False)
+    joint = jnp.concatenate([query_weight, key_weight, value_weight], axis=1)
+    gain_g = jnp.sum(mixer_g[:, : 3 * own] * joint, axis=1) / mixer_gain
+    gain_g = gain_g + exchange(gain_g, "tensor", 1)
+    came_gain = exchange(gain_g, "tensor", 2)
+    input_grad = run_leave(me, mine, came)
+    hidden = up_weight.shape[1]
+    return (
+        layer_output,
+        input_grad,
+        gain_g + came_gain,
+        mixer_g[:, :own],
+        mixer_g[:, own : 2 * own],
+        mixer_g[:, 2 * own : 3 * own],
+        tiny[rows:].reshape(taps, few),
+        mixer_g[:, 3 * own :].T,
+        tiny[:rows],
+        feed_g[:, :hidden],
+        feed_g[:, hidden:].T,
+    )
+
+
 def solution(mesh):
+    shape = mesh.shape
+
+    def chosen(*arrays):
+        rows, length, model = arrays[0].shape
+        heads, width = arrays[7].shape
+        fits = (
+            (shape["dp"], shape["ctx"], shape["tensor"]) == (4, 2, 4)
+            and rows == 2
+            and (heads * shape["tensor"]) % (2 * PAIR) == 0
+            and PAIR * width == LANES
+            and length % (BLOCK // 2) == 0
+        )
+        return (by_sequence if fits else on_device)(*arrays)
+
     return jax.shard_map(
-        on_device,
+        chosen,
         mesh=mesh,
         in_specs=(
             P("dp", "ctx", None),

time: 851 us -> 376 us (0.44)
  waiting for transfers between devices: 405 us -> 56.7 us
  Pallas kernels: 0 us -> 227 us
  matrix products: 167 us -> 0 us
  blocking collectives: 110 us -> 0 us
  local copies, waits for them, and re-layouts: 84.9 us -> 19.2 us
  other arithmetic: 53.8 us -> 6.64 us
  starting transfers between devices: 7.65 us -> 44.2 us
    psum x3 -> x0, waiting for transfers between devices: 404 us -> none  [the longest x1 177 us: on_device(): feed = lax.psum(project(activated, down_all), 'tensor')]
    pallas_call x0 -> x14, Pallas kernels: none -> 227 us  [the longest x4 97.3 us: run_feed(): pl.pallas_call(partial(feed_kernel, own, final), grid_spec=pltpu.Prefetch...]
    dot_general x25 -> x0, matrix products: 167 us -> none  [the longest x8 79.4 us: project(): jnp.einsum('btd,df->btf', left, right, precision=precise, preferred_eleme...]
    all_gather x8 -> x0, blocking collectives: 71.6 us -> none  [the longest x3 16.6 us: carried_in(): pieces = jax.tree.map(lambda part: lax.all_gather(part, axis), value)]
    ppermute x3 -> x48, waiting for transfers between devices: 0.01 us -> 44.3 us  [the longest x43 27.8 us: exchange(): return lax.ppermute(value, axis, [(i, i ^ flip) for i in range(count)])]
    unnamed x2 -> x0, blocking collectives: 38 us -> none
    ppermute x3 -> x48, starting transfers between devices: 6.61 us -> 43.4 us  [the longest x43 36.7 us: exchange(): return lax.ppermute(value, axis, [(i, i ^ flip) for i in range(count)])]
    reshape x10 -> x4, local copies, waits for them, and re-layouts: 27.2 us -> 0.89 us  [the longest x1 0.66 us: by_sequence(): tiny[rows:].reshape(taps, few)]
  transfers between devices with their start and end apart: 14 -> 53, of which waited for: 3 -> 18; matrix products, arithmetic and copies ran while one was open for 23% -> 4% of each run, Pallas kernels for 0% -> 61%
where the time goes in v2:
time: 376 us; the launch traced here: 368 us
  Pallas kernels  227 us (60%)
  waiting for transfers between devices  56.7 us (15%)
  starting transfers between devices  44.2 us (12%)
  local copies, waits for them, and re-layouts  19.2 us (5%)
  between operations  14.7 us (4%)
  other arithmetic  6.64 us (2%)
    pallas_call x4, Pallas kernels, run_feed(): pl.pallas_call(partial(feed_kernel, own, final), grid_spec=pltpu.Prefetch...  97.3 us
    pallas_call x1, Pallas kernels, run_mixer_back(): pl.pallas_call(partial(mixer_back_kernel, taps), grid_spec=pltpu.Prefetch...  45.1 us
    ppermute x43, starting transfers between devices, exchange(): return lax.ppermute(value, axis, [(i, i ^ flip) for i in range(count)])  36.7 us
    ppermute x43, waiting for transfers between devices, exchange(): return lax.ppermute(value, axis, [(i, i ^ flip) for i in range(count)])  27.8 us
    pallas_call x2, Pallas kernels, run_input_back(): pl.pallas_call(partial(input_back_kernel, other), grid_spec=pltpu.Prefetc...  26 us
    pallas_call x2, Pallas kernels, run_project(): pl.pallas_call(project_kernel, grid_spec=pltpu.PrefetchScalarGridSpec(num...  25.7 us
    pallas_call x1, Pallas kernels, run_mixer(): pl.pallas_call(partial(mixer_kernel, taps), grid_spec=pltpu.PrefetchScala...  23.8 us
    ppermute x5, waiting for transfers between devices, corner(): return lax.ppermute(value, ('dp', 'ctx'), pairs)  16.5 us
  transfers between devices with their start and end apart: 53, of which 18 were waited for; matrix products, arithmetic and copies ran while one was open for 4% of the time, Pallas kernels for 61%

profile of v2, /device:TPU:0, one launch (start us, length us, event | category | flops | bytes accessed | tf_op | source)
XLA Modules:
  0.0 368.1 jit_solution(3712282778709022573)
XLA Ops:
  7.2 2.1 pack_mixer.1.refs_0_
  9.4 2.7 dynamic-slice_bitcast_fusion.2
  12.5 2.6 collective-permute-start.1
  15.1 1.4 collective-permute-start.2
  16.5 1.6 collective-permute-start.3
  19.0 2.1 pack_feed.1
  21.1 2.3 collective-permute-done.1.refs_8_
  23.4 1.4 collective-permute-done.2.refs_2_
  24.8 1.2 collective-permute-done.3.refs_4_
  26.0 1.6 collective-permute-start.5
  27.6 2.6 collective-permute-start.10
  31.2 3.0 collective-permute-done.5.refs_6_
  34.3 8.5 %collective-permute-done.10.refs_0_ = f32[104,768]{1,0:T(8,128)} collective-permute-done((f32[104,768]{1,0:T(8,128)S(1)}, f32[104,768]{1,0:T(8,128)}, u32[]{:S(2)}, u32[]{:S(2)}) %collective-permute-start.10) | collective-permute-done | bytes 319520 | tf_op jit(solution)/shard_map/ppermute | solution.py:1008
  45.9 1.6 collective-permute-start.13
  47.5 2.7 collective-permute-start.18
  50.3 1.1 collective-permute-start.19
  53.5 5.0 %collective-permute-done.18.refs_8_ = f32[104,768]{1,0:T(8,128)S(1)} collective-permute-done((f32[104,768]{1,0:T(8,128)S(1)}, f32[104,768]{1,0:T(8,128)S(1)}, u32[]{:S(2)}, u32[]{:S(2)}) %collective-permute-start.18) | collective-permute-done | bytes 319520 | tf_op jit(solution)/shard_map/ppermute | solution.py:1008
  62.0 1.3 collective-permute-start.22
  63.3 1.6 collective-permute-start.23
  65.4 12.8 %project.2 = (f32[1024,1152]{1,0:T(8,128)}, bf16[768,1152]{1,0:T(8,128)(2,1)}, bf16[768,1152]{1,0:T(8,128)(2,1)}, bf16[768,384]{1,0:T(8,128)(2,1)}, bf16[768,384...) custom-call(s32[1]{0:T(128)} %bitcast.me_ref, f32[2,512,768]{2,1,0:T(8,128)} %x_ref.11, f32[512,768]{1,0:T(8,128)} %copy-done.1, ...), custom_call_target="tpu_custom_call" | custom-call | flops 5435817984 | bytes 20971520 | tf_op jit(solution)/shard_map/project/pallas_call | solution.py:496
  78.3 4.2 %collective-permute-done.21.refs_6_ = f32[104,768]{1,0:T(8,128)S(1)} collective-permute-done((f32[104,768]{1,0:T(8,128)S(1)}, f32[104,768]{1,0:T(8,128)S(1)}, u32[]{:S(2)}, u32[]{:S(2)}) %collective-permute-start.21) | collective-permute-done | bytes 319520 | tf_op jit(solution)/shard_map/ppermute | solution.py:1016
  82.5 1.7 dynamic-slice_bitcast_fusion.1
  84.4 1.6 collective-permute-start.28
  88.2 8.2 %collective-permute-done.28.refs_14_ = f32[104,768]{1,0:T(8,128)} collective-permute-done((f32[104,768]{1,0:T(8,128)S(1)}, f32[104,768]{1,0:T(8,128)}, u32[]{:S(2)}, u32[]{:S(2)}) %collective-permute-start.28) | collective-permute-done | bytes 319520 | tf_op jit(solution)/shard_map/ppermute | solution.py:1016
  98.4 5.4 %collective-permute-start.34 = (f32[96,1536]{1,0:T(8,128)S(1)}, f32[96,1536]{1,0:T(8,128)}, u32[]{:S(2)}, u32[]{:S(2)}) collective-permute-start(f32[96,1536]{1,0:T(8,128)S(1)} %copy-done.2), channel_id=1, source_target_pairs={{0,1},{1,0},{2,3},{3,2},{4,5},{5,4},{6,7},{7,6},{8,9},{9,8},{10,11... | collective-permute-start | bytes 1769480 | tf_op jit(solution)/shard_map/ppermute | solution.py:1008
  104.7 12.9 %project.3 = (f32[1024,1152]{1,0:T(8,128)}, bf16[768,1152]{1,0:T(8,128)(2,1)}, bf16[768,1152]{1,0:T(8,128)(2,1)}, bf16[768,384]{1,0:T(8,128)(2,1)}, bf16[768,384...) custom-call(s32[1]{0:T(128)} %bitcast.me_ref, f32[2,512,768]{2,1,0:T(8,128)} %x_ref.11, f32[512,768]{1,0:T(8,128)} %copy-done.1, ...), custom_call_target="tpu_custom_call" | custom-call | flops 5435817984 | bytes 20971520 | tf_op jit(solution)/shard_map/project/pallas_call | solution.py:496
  119.3 23.8 %mixer.1 = (f32[1024,256]{1,0:T(8,128)}, f32[8,128,768]{2,1,0:T(8,128)}, f32[1024,768]{1,0:T(8,128)}, bf16[1024,768]{1,0:T(8,128)(2,1)}, bf16[1024,768]{1,0:T(8,128)(2,1)}) custom-call(s32[1]{0:T(128)} %bitcast.me_ref, f32[2,512,768]{2,1,0:T(8,128)} %x_ref.11, f32[512,768]{1,0:T(8,128)} %copy-done.1, f32[1024,1152]{1,0:T(8,128)} %get-tuple-element.110.pa_ref.ba_ref, ...), custom_call_target="tpu_custom_call" | custom-call | flops 30000001024 | bytes 31457280 | tf_op jit(solution)/shard_map/mixer/pallas_call | solution.py:651
  143.1 3.8 %collective-permute-done.35 = f32[96,1536]{1,0:T(8,128)S(1)} collective-permute-done((f32[96,1536]{1,0:T(8,128)S(1)}, f32[96,1536]{1,0:T(8,128)S(1)}, u32[]{:S(2)}, u32[]{:S(2)}) %collective-permute-start.35) | collective-permute-done | bytes 589856 | tf_op jit(solution)/shard_map/ppermute | solution.py:1008
  148.7 30.4 %feed_own.1 = (f32[1024,768]{1,0:T(8,128)}, f32[1024,768]{1,0:T(8,128)}, f32[768,1536]{1,0:T(8,128)}) custom-call(s32[1]{0:T(128)} %bitcast.me_ref, bf16[1024,768]{1,0:T(8,128)(2,1)} %get-tuple-element.132.nh_ref, bf16[1024,768]{1,0:T(8,128)(2,1)} %get-tuple-element.133.nl_ref, f32[2,512,768]{2,1,0:T(8,128)} %ct_ref.9, ...), custom_call_target="tpu_custom_call" | custom-call | flops 21743271936 | bytes 31457280 | tf_op jit(solution)/shard_map/feed_own/pallas_call | solution.py:905
  180.6 22.1 %feed.3 = (f32[1024,768]{1,0:T(8,128)}, f32[1024,768]{1,0:T(8,128)}) custom-call(s32[1]{0:T(128)} %bitcast.me_ref, bf16[1024,768]{1,0:T(8,128)(2,1)} %get-tuple-element.132.nh_ref, bf16[1024,768]{1,0:T(8,128)(2,1)} %get-tuple-element.133.nl_ref, f32[2,512,768]{2,1,0:T(8,128)} %ct_ref.9, f32[512,768]{1,0:T(8,128)} %collective-permute-done.33.cr_ref, ...), custom_call_target="tpu_custom_call" | custom-call | flops 14495514624 | bytes 31457280 | tf_op jit(solution)/shard_map/feed/pallas_call | solution.py:905
  202.7 22.6 %feed.4 = (f32[1024,768]{1,0:T(8,128)}, f32[1024,768]{1,0:T(8,128)}) custom-call(s32[1]{0:T(128)} %bitcast.me_ref, bf16[1024,768]{1,0:T(8,128)(2,1)} %get-tuple-element.132.nh_ref, bf16[1024,768]{1,0:T(8,128)(2,1)} %get-tuple-element.133.nl_ref, f32[2,512,768]{2,1,0:T(8,128)} %ct_ref.9, f32[512,768]{1,0:T(8,128)} %collective-permute-done.33.cr_ref, ...), custom_call_target="tpu_custom_call" | custom-call | flops 14495514624 | bytes 31457280 | tf_op jit(solution)/shard_map/feed/pallas_call | solution.py:905
  225.4 12.0 %all-gather.11.cloned.1.call-done.w_in = f32[768,1536]{1,0:T(8,128)} async-done(((f32[96,1536]{1,0:T(8,128)}), f32[768,1536]{1,0:T(8,128)}) %all-gather.11.cloned.1.call-update) | async-done | bytes 4718608 | tf_op jit(solution)/shard_map/all_gather | solution.py:1086
  237.3 22.1 %feed.5 = (f32[2,512,768]{2,1,0:T(8,128)}, f32[1024,768]{1,0:T(8,128)}) custom-call(s32[1]{0:T(128)} %bitcast.me_ref, bf16[1024,768]{1,0:T(8,128)(2,1)} %get-tuple-element.132.nh_ref, bf16[1024,768]{1,0:T(8,128)(2,1)} %get-tuple-element.133.nl_ref, f32[2,512,768]{2,1,0:T(8,128)} %ct_ref.9, f32[512,768]{1,0:T(8,128)} %collective-permute-done.33.cr_ref, ...), custom_call_target="tpu_custom_call" | custom-call | flops 14495514624 | bytes 31457280 | tf_op jit(solution)/shard_map/feed/pallas_call | solution.py:905
  259.4 1.5 dynamic-slice_bitcast_fusion
  261.3 45.1 %mixer_back.1 = (f32[1024,768]{1,0:T(8,128)}, f32[1024,768]{1,0:T(8,128)}, f32[1024,768]{1,0:T(8,128)}, f32[1024,768]{1,0:T(8,128)}, f32[1,768]{1,0:T(1,128)}, /...) custom-call(s32[1]{0:T(128)} %bitcast.me_ref, f32[1024,768]{1,0:T(8,128)} %get-tuple-element.149.fng_ref, ...), custom_call_target="tpu_custom_call" | custom-call | flops 80000000000 | bytes 52428800 | tf_op jit(solution)/shard_map/mixer_back/pallas_call | solution.py:805
  309.8 2.3 leave.2
  312.2 1.8 add.54.refs_0_
  314.0 1.3 collective-permute-start.40
  316.1 13.1 %input_back.2.refs_0_ = f32[512,768]{1,0:T(8,128)} custom-call(s32[1]{0:T(128)} %bitcast.me_ref, f32[2,512,768]{2,1,0:T(8,128)} %x_ref.11, f32[512,768]{1,0:T(8,128)} %copy-done.1, f32[1024,768]{1,0:T(8,128)} %get-tuple-element.158.rg_ref, f32[8,768]{1,0:T(8,128)} %get-tuple-element.127.gains_ref, bf16[768,1152]{1,0:T(8,128)(2,1)} %get-tuple-element.159.ah_ref, ...), custom_call_target="tpu_custom_call" | custom-call | flops 5435817984 | bytes 20971520 | tf_op jit(solution)/shard_map/input_back/pallas_call | solution.py:960
  329.3 1.9 slice_bitcast_fusion
  332.3 1.4 collective-permute-start.42
  334.5 1.3 collective-permute-start.44
  335.8 12.8 %input_back.3.whole_ref = f32[2,512,768]{2,1,0:T(8,128)} custom-call(s32[1]{0:T(128)} %bitcast.me_ref, f32[2,512,768]{2,1,0:T(8,128)} %x_ref.11, f32[512,768]{1,0:T(8,128)} %copy-done.1, f32[1024,768]{1,0:T(8,128)} %get-tuple-element.158.rg_ref, f32[8,768]{1,0:T(8,128)} %get-tuple-element.127.gains_ref, bf16[768,1152]{1,0:T(8,128)(2,1)} %get-tuple-element.159.ah_ref, ...), custom_call_target="tpu_custom_call" | custom-call | flops 5435817984 | bytes 20971520 | tf_op jit(solution)/shard_map/input_back/pallas_call | solution.py:960
  348.7 1.2 fusion.2
  350.9 1.5 collective-permute-start.46
  352.9 1.5 collective-permute-done.46
  354.5 2.4 collective-permute-start.47
  358.3 2.3 leave.3
  (181 shorter events, 31.9 us)
Async XLA Ops:
  7.2 141.5 %all-gather.5.cloned.1.call-start = ((), (), s32[]{:S(2)}) async-start(), calls=%async_computation.1 | async-start | bytes 5308416 | tf_op jit(solution)/shard_map/all_gather | solution.py:1086
  12.1 33.8 %collective-permute-start = (f32[512,768]{1,0:T(8,128)}, f32[512,768]{1,0:T(8,128)S(1)}, u32[]{:S(2)}, u32[]{:S(2)}) collective-permute-start(f32[512,768]{1,0:T(8,128)} %dynamic-slice_bitcast_fusion.2), channel_id=1, source_target_pairs={{0,4},{4,0},{1,5},{5,1},{2,6},{6,2},{3,7},{7,3},{8,12},{12,8},{9,1... | collective-permute-start | bytes 4718600 | tf_op jit(solution)/shard_map/ppermute | solution.py:1008
  12.5 10.9 %collective-permute-start.1 = (f32[104,768]{1,0:T(8,128)S(1)}, f32[104,768]{1,0:T(8,128)}, u32[]{:S(2)}, u32[]{:S(2)}) collective-permute-start(f32[104,768]{1,0:T(8,128)S(1)} %copy-done.12), channel_id=1, source_target_pairs={{0,1},{1,0},{2,3},{3,2},{4,5},{5,4},{6,7},{7,6},{8,9},{9,8},{10,11... | collective-permute-start | bytes 958472 | tf_op jit(solution)/shard_map/ppermute | solution.py:1008
  15.1 9.7 %collective-permute-start.2 = (f32[104,768]{1,0:T(8,128)S(1)}, f32[104,768]{1,0:T(8,128)S(1)}, u32[]{:S(2)}, u32[]{:S(2)}) collective-permute-start(f32[104,768]{1,0:T(8,128)S(1)} %copy-done.12), channel_id=1, source_target_pairs={{0,8},{8,0},{16,24},{24,16},{1,9},{9,1},{17,25},{25,17},{2,10},{10... | collective-permute-start | bytes 958472 | tf_op jit(solution)/shard_map/ppermute | solution.py:1008
  16.5 9.4 %collective-permute-start.3 = (f32[104,768]{1,0:T(8,128)S(1)}, f32[104,768]{1,0:T(8,128)S(1)}, u32[]{:S(2)}, u32[]{:S(2)}) collective-permute-start(f32[104,768]{1,0:T(8,128)S(1)} %copy-done.12), channel_id=1, source_target_pairs={{0,16},{8,24},{16,0},{24,8},{1,17},{9,25},{17,1},{25,9},{2,18},{10... | collective-permute-start | bytes 958472 | tf_op jit(solution)/shard_map/ppermute | solution.py:1008
  18.1 7.8 %collective-permute-start.4 = (f32[104,768]{1,0:T(8,128)S(1)}, f32[104,768]{1,0:T(8,128)}, u32[]{:S(2)}, u32[]{:S(2)}) collective-permute-start(f32[104,768]{1,0:T(8,128)S(1)} %copy-done.12), channel_id=1, source_target_pairs={{0,4},{4,0},{1,5},{5,1},{2,6},{6,2},{3,7},{7,3},{8,12},{12,8},{9,1... | collective-permute-start | bytes 958472 | tf_op jit(solution)/shard_map/ppermute | solution.py:1008
  26.0 8.3 %collective-permute-start.5 = (f32[104,768]{1,0:T(8,128)S(1)}, f32[104,768]{1,0:T(8,128)S(1)}, u32[]{:S(2)}, u32[]{:S(2)}) collective-permute-start(f32[104,768]{1,0:T(8,128)S(1)} %broadcast_select_fusion.3), channel_id=1, source_target_pairs={{0,16},{4,12},{8,24},{12,4},{16,0},{20,28},{24,8},{28,20},{1,17},{... | collective-permute-start | bytes 958472 | tf_op jit(solution)/shard_map/ppermute | solution.py:1016
  27.6 15.2 %collective-permute-start.10 = (f32[104,768]{1,0:T(8,128)S(1)}, f32[104,768]{1,0:T(8,128)}, u32[]{:S(2)}, u32[]{:S(2)}) collective-permute-start(f32[104,768]{1,0:T(8,128)S(1)} %copy-done.12), channel_id=1, source_target_pairs={{0,2},{1,3},{2,0},{3,1},{4,6},{5,7},{6,4},{7,5},{8,10},{9,11},{10,... | collective-permute-start | bytes 958472 | tf_op jit(solution)/shard_map/ppermute | solution.py:1008
  30.2 12.6 %collective-permute-start.11 = (f32[104,768]{1,0:T(8,128)}, f32[104,768]{1,0:T(8,128)S(1)}, u32[]{:S(2)}, u32[]{:S(2)}) collective-permute-start(f32[104,768]{1,0:T(8,128)} %collective-permute-done.1.refs_8_), channel_id=1, source_target_pairs={{0,8},{8,0},{16,24},{24,16},{1,9},{9,1},{17,25},{25,17},{2,10},{10... | collective-permute-start | bytes 958472 | tf_op jit(solution)/shard_map/ppermute | solution.py:1008
  30.7 12.6 %collective-permute-start.12 = (f32[104,768]{1,0:T(8,128)}, f32[104,768]{1,0:T(8,128)S(1)}, u32[]{:S(2)}, u32[]{:S(2)}) collective-permute-start(f32[104,768]{1,0:T(8,128)} %collective-permute-done.1.refs_8_), channel_id=1, source_target_pairs={{0,16},{8,24},{16,0},{24,8},{1,17},{9,25},{17,1},{25,9},{2,18},{10... | collective-permute-start | bytes 958472 | tf_op jit(solution)/shard_map/ppermute | solution.py:1008
  34.3 9.0 %collective-permute-start.6 = (f32[104,768]{1,0:T(8,128)S(1)}, f32[104,768]{1,0:T(8,128)S(1)}, u32[]{:S(2)}, u32[]{:S(2)}) collective-permute-start(f32[104,768]{1,0:T(8,128)S(1)} %collective-permute-done.2.refs_2_), channel_id=1, source_target_pairs={{0,4},{4,0},{1,5},{5,1},{2,6},{6,2},{3,7},{7,3},{8,12},{12,8},{9,1... | collective-permute-start | bytes 958472 | tf_op jit(solution)/shard_map/ppermute | solution.py:1008
  45.9 7.1 %collective-permute-start.13 = (f32[104,768]{1,0:T(8,128)S(1)}, f32[104,768]{1,0:T(8,128)S(1)}, u32[]{:S(2)}, u32[]{:S(2)}) collective-permute-start(f32[104,768]{1,0:T(8,128)S(1)} %broadcast_select_fusion.2), channel_id=1, source_target_pairs={{0,16},{4,12},{8,24},{12,4},{16,0},{20,28},{24,8},{28,20},{1,17},{... | collective-permute-start | bytes 958472 | tf_op jit(solution)/shard_map/ppermute | solution.py:1016
  47.5 11.0 %collective-permute-start.18 = (f32[104,768]{1,0:T(8,128)S(1)}, f32[104,768]{1,0:T(8,128)S(1)}, u32[]{:S(2)}, u32[]{:S(2)}) collective-permute-start(f32[104,768]{1,0:T(8,128)S(1)} %copy-done.12), channel_id=1, source_target_pairs={{0,3},{1,2},{2,1},{3,0},{4,7},{5,6},{6,5},{7,4},{8,11},{9,10},{10,... | collective-permute-start | bytes 958472 | tf_op jit(solution)/shard_map/ppermute | solution.py:1008
  50.3 8.8 %collective-permute-start.19 = (f32[104,768]{1,0:T(8,128)}, f32[104,768]{1,0:T(8,128)S(1)}, u32[]{:S(2)}, u32[]{:S(2)}) collective-permute-start(f32[104,768]{1,0:T(8,128)} %collective-permute-done.10.refs_0_), channel_id=1, source_target_pairs={{0,8},{8,0},{16,24},{24,16},{1,9},{9,1},{17,25},{25,17},{2,10},{10... | collective-permute-start | bytes 958472 | tf_op jit(solution)/shard_map/ppermute | solution.py:1008
  51.4 8.4 %collective-permute-start.20 = (f32[104,768]{1,0:T(8,128)}, f32[104,768]{1,0:T(8,128)S(1)}, u32[]{:S(2)}, u32[]{:S(2)}) collective-permute-start(f32[104,768]{1,0:T(8,128)} %collective-permute-done.10.refs_0_), channel_id=1, source_target_pairs={{0,16},{8,24},{16,0},{24,8},{1,17},{9,25},{17,1},{25,9},{2,18},{10... | collective-permute-start | bytes 958472 | tf_op jit(solution)/shard_map/ppermute | solution.py:1008
  53.0 6.8 %collective-permute-start.14 = (f32[104,768]{1,0:T(8,128)S(1)}, f32[104,768]{1,0:T(8,128)S(1)}, u32[]{:S(2)}, u32[]{:S(2)}) collective-permute-start(f32[104,768]{1,0:T(8,128)S(1)} %collective-permute-done.11.refs_10_), channel_id=1, source_target_pairs={{0,4},{4,0},{1,5},{5,1},{2,6},{6,2},{3,7},{7,3},{8,12},{12,8},{9,1... | collective-permute-start | bytes 958472 | tf_op jit(solution)/shard_map/ppermute | solution.py:1008
  53.0 6.8 %collective-permute-start.15 = (f32[104,768]{1,0:T(8,128)S(1)}, f32[104,768]{1,0:T(8,128)S(1)}, u32[]{:S(2)}, u32[]{:S(2)}) collective-permute-start(f32[104,768]{1,0:T(8,128)S(1)} %collective-permute-done.12.refs_12_), channel_id=1, source_target_pairs={{0,4},{4,0},{1,5},{5,1},{2,6},{6,2},{3,7},{7,3},{8,12},{12,8},{9,1... | collective-permute-start | bytes 958472 | tf_op jit(solution)/shard_map/ppermute | solution.py:1008
  61.4 119.2 %all-gather.7.cloned.1.call-start = ((), (), s32[]{:S(2)}) async-start(), calls=%async_computation.2 | async-start | bytes 5308416 | tf_op jit(solution)/shard_map/all_gather | solution.py:1086
  61.4 4.0 %collective-permute-start.9 = (f32[104,768]{1,0:T(8,128)}, f32[104,768]{1,0:T(8,128)}, u32[]{:S(2)}, u32[]{:S(2)}) collective-permute-start(f32[104,768]{1,0:T(8,128)} %collective-permute-done.1.refs_8_), channel_id=1, source_target_pairs={{0,4},{4,0},{1,5},{5,1},{2,6},{6,2},{3,7},{7,3},{8,12},{12,8},{9,1... | collective-permute-start | bytes 958472 | tf_op jit(solution)/shard_map/ppermute | solution.py:1008
  61.5 26.4 %collective-permute-start.17 = (f32[104,768]{1,0:T(8,128)}, f32[104,768]{1,0:T(8,128)}, u32[]{:S(2)}, u32[]{:S(2)}) collective-permute-start(f32[104,768]{1,0:T(8,128)} %collective-permute-done.10.refs_0_), channel_id=1, source_target_pairs={{0,4},{4,0},{1,5},{5,1},{2,6},{6,2},{3,7},{7,3},{8,12},{12,8},{9,1... | collective-permute-start | bytes 958472 | tf_op jit(solution)/shard_map/ppermute | solution.py:1008
  62.0 20.5 %collective-permute-start.22 = (f32[104,768]{1,0:T(8,128)}, f32[104,768]{1,0:T(8,128)S(1)}, u32[]{:S(2)}, u32[]{:S(2)}) collective-permute-start(f32[104,768]{1,0:T(8,128)} %copy-done.21), channel_id=1, source_target_pairs={{0,8},{8,0},{16,24},{24,16},{1,9},{9,1},{17,25},{25,17},{2,10},{10... | collective-permute-start | bytes 958472 | tf_op jit(solution)/shard_map/ppermute | solution.py:1008
  63.3 19.2 %collective-permute-start.23 = (f32[104,768]{1,0:T(8,128)}, f32[104,768]{1,0:T(8,128)}, u32[]{:S(2)}, u32[]{:S(2)}) collective-permute-start(f32[104,768]{1,0:T(8,128)} %copy-done.21), channel_id=1, source_target_pairs={{0,16},{8,24},{16,0},{24,8},{1,17},{9,25},{17,1},{25,9},{2,18},{10... | collective-permute-start | bytes 958472 | tf_op jit(solution)/shard_map/ppermute | solution.py:1008
  64.9 17.6 %collective-permute-start.21 = (f32[104,768]{1,0:T(8,128)S(1)}, f32[104,768]{1,0:T(8,128)S(1)}, u32[]{:S(2)}, u32[]{:S(2)}) collective-permute-start(f32[104,768]{1,0:T(8,128)S(1)} %broadcast_select_fusion.1), channel_id=1, source_target_pairs={{0,16},{4,12},{8,24},{12,4},{16,0},{20,28},{24,8},{28,20},{1,17},{... | collective-permute-start | bytes 958472 | tf_op jit(solution)/shard_map/ppermute | solution.py:1016
  84.2 33.3 %collective-permute-start.33 = (f32[512,768]{1,0:T(8,128)S(1)}, f32[512,768]{1,0:T(8,128)}, u32[]{:S(2)}, u32[]{:S(2)}) collective-permute-start(f32[512,768]{1,0:T(8,128)S(1)} %dynamic-slice_bitcast_fusion.1), channel_id=1, source_target_pairs={{0,4},{4,0},{1,5},{5,1},{2,6},{6,2},{3,7},{7,3},{8,12},{12,8},{9,1... | collective-permute-start | bytes 4718600 | tf_op jit(solution)/shard_map/ppermute | solution.py:1008
  84.4 12.1 %collective-permute-start.28 = (f32[104,768]{1,0:T(8,128)S(1)}, f32[104,768]{1,0:T(8,128)}, u32[]{:S(2)}, u32[]{:S(2)}) collective-permute-start(f32[104,768]{1,0:T(8,128)S(1)} %broadcast_select_fusion), channel_id=1, source_target_pairs={{0,16},{4,12},{8,24},{12,4},{16,0},{20,28},{24,8},{28,20},{1,17},{... | collective-permute-start | bytes 958472 | tf_op jit(solution)/shard_map/ppermute | solution.py:1016
  86.1 10.3 %collective-permute-start.24 = (f32[104,768]{1,0:T(8,128)S(1)}, f32[104,768]{1,0:T(8,128)S(1)}, u32[]{:S(2)}, u32[]{:S(2)}) collective-permute-start(f32[104,768]{1,0:T(8,128)S(1)} %collective-permute-done.19.refs_2_), channel_id=1, source_target_pairs={{0,4},{4,0},{1,5},{5,1},{2,6},{6,2},{3,7},{7,3},{8,12},{12,8},{9,1... | collective-permute-start | bytes 958472 | tf_op jit(solution)/shard_map/ppermute | solution.py:1008
  87.7 9.2 %collective-permute-start.25 = (f32[104,768]{1,0:T(8,128)S(1)}, f32[104,768]{1,0:T(8,128)S(1)}, u32[]{:S(2)}, u32[]{:S(2)}) collective-permute-start(f32[104,768]{1,0:T(8,128)S(1)} %collective-permute-done.20.refs_4_), channel_id=1, source_target_pairs={{0,4},{4,0},{1,5},{5,1},{2,6},{6,2},{3,7},{7,3},{8,12},{12,8},{9,1... | collective-permute-start | bytes 958472 | tf_op jit(solution)/shard_map/ppermute | solution.py:1008
  87.9 9.2 %collective-permute-start.26 = (f32[104,768]{1,0:T(8,128)}, f32[104,768]{1,0:T(8,128)S(1)}, u32[]{:S(2)}, u32[]{:S(2)}) collective-permute-start(f32[104,768]{1,0:T(8,128)} %copy-done.22), channel_id=1, source_target_pairs={{0,4},{4,0},{1,5},{5,1},{2,6},{6,2},{3,7},{7,3},{8,12},{12,8},{9,1... | collective-permute-start | bytes 958472 | tf_op jit(solution)/shard_map/ppermute | solution.py:1008
  96.5 8.2 %collective-permute-start.29 = (f32[104,768]{1,0:T(8,128)S(1)}, f32[104,768]{1,0:T(8,128)}, u32[]{:S(2)}, u32[]{:S(2)}) collective-permute-start(f32[104,768]{1,0:T(8,128)S(1)} %collective-permute-done.22.refs_10_), channel_id=1, source_target_pairs={{0,4},{4,0},{1,5},{5,1},{2,6},{6,2},{3,7},{7,3},{8,12},{12,8},{9,1... | collective-permute-start | bytes 958472 | tf_op jit(solution)/shard_map/ppermute | solution.py:1008
  97.0 7.7 %collective-permute-start.30 = (f32[104,768]{1,0:T(8,128)}, f32[104,768]{1,0:T(8,128)}, u32[]{:S(2)}, u32[]{:S(2)}) collective-permute-start(f32[104,768]{1,0:T(8,128)} %collective-permute-done.23.refs_12_), channel_id=1, source_target_pairs={{0,4},{4,0},{1,5},{5,1},{2,6},{6,2},{3,7},{7,3},{8,12},{12,8},{9,1... | collective-permute-start | bytes 958472 | tf_op jit(solution)/shard_map/ppermute | solution.py:1008
  97.1 7.6 %collective-permute-start.31 = (f32[104,768]{1,0:T(8,128)}, f32[104,768]{1,0:T(8,128)}, u32[]{:S(2)}, u32[]{:S(2)}) collective-permute-start(f32[104,768]{1,0:T(8,128)} %collective-permute-done.28.refs_14_), channel_id=1, source_target_pairs={{0,4},{4,0},{1,5},{5,1},{2,6},{6,2},{3,7},{7,3},{8,12},{12,8},{9,1... | collective-permute-start | bytes 958472 | tf_op jit(solution)/shard_map/ppermute | solution.py:1008
  98.4 19.1 %collective-permute-start.34 = (f32[96,1536]{1,0:T(8,128)S(1)}, f32[96,1536]{1,0:T(8,128)}, u32[]{:S(2)}, u32[]{:S(2)}) collective-permute-start(f32[96,1536]{1,0:T(8,128)S(1)} %copy-done.2), channel_id=1, source_target_pairs={{0,1},{1,0},{2,3},{3,2},{4,5},{5,4},{6,7},{7,6},{8,9},{9,8},{10,11... | collective-permute-start | bytes 1769480 | tf_op jit(solution)/shard_map/ppermute | solution.py:1008
  117.6 85.1 %all-gather.9.cloned.1.call-start = ((), (), s32[]{:S(2)}) async-start(), calls=%async_computation.3 | async-start | bytes 5308416 | tf_op jit(solution)/shard_map/all_gather | solution.py:1086
  118.1 28.7 %collective-permute-start.35 = (f32[96,1536]{1,0:T(8,128)S(1)}, f32[96,1536]{1,0:T(8,128)S(1)}, u32[]{:S(2)}, u32[]{:S(2)}) collective-permute-start(f32[96,1536]{1,0:T(8,128)S(1)} %copy-done.2), channel_id=1, source_target_pairs={{0,2},{1,3},{2,0},{3,1},{4,6},{5,7},{6,4},{7,5},{8,10},{9,11},{10,... | collective-permute-start | bytes 1769480 | tf_op jit(solution)/shard_map/ppermute | solution.py:1008
  147.7 89.6 %all-gather.11.cloned.1.call-start = ((), (), s32[]{:S(2)}) async-start(), calls=%async_computation.4 | async-start | bytes 5308416 | tf_op jit(solution)/shard_map/all_gather | solution.py:1086
  147.8 31.4 %collective-permute-start.36 = (f32[96,1536]{1,0:T(8,128)S(1)}, f32[96,1536]{1,0:T(8,128)S(1)}, u32[]{:S(2)}, u32[]{:S(2)}) collective-permute-start(f32[96,1536]{1,0:T(8,128)S(1)} %copy-done.2), channel_id=1, source_target_pairs={{0,3},{1,2},{2,1},{3,0},{4,7},{5,6},{6,5},{7,4},{8,11},{9,10},{10,... | collective-permute-start | bytes 1769480 | tf_op jit(solution)/shard_map/ppermute | solution.py:1008
  180.0 149.3 %reduce-scatter.2.cloned.1.call-start = ((), (), s32[]{:S(2)}) async-start(), calls=%async_computation.5 | async-start | bytes 5308416 | tf_op jit(solution)/shard_map/reduce_scatter | solution.py:1159
  260.9 47.7 %collective-permute-start.37 = (f32[512,768]{1,0:T(8,128)S(1)}, f32[512,768]{1,0:T(8,128)S(1)}, u32[]{:S(2)}, u32[]{:S(2)}) collective-permute-start(f32[512,768]{1,0:T(8,128)S(1)} %dynamic-slice_bitcast_fusion), channel_id=1, source_target_pairs={{0,4},{4,0},{1,5},{5,1},{2,6},{6,2},{3,7},{7,3},{8,12},{12,8},{9,1... | collective-permute-start | bytes 4718600 | tf_op jit(solution)/shard_map/ppermute | solution.py:1008
  306.4 5.8 %collective-permute-start.38 = (f32[1,4,96,768]{3,2,1,0:T(8,128)}, f32[1,4,96,768]{3,2,1,0:T(8,128)}, u32[]{:S(2)}, u32[]{:S(2)}) collective-permute-start(f32[1,4,96,768]{3,2,1,0:T(8,128)} %get-tuple-element.153), channel_id=1, source_target_pairs={{0,4},{4,0},{1,5},{5,1},{2,6},{6,2},{3,7},{7,3},{8,12},{12,8},{9,1... | collective-permute-start | bytes 3538952 | tf_op jit(solution)/shard_map/ppermute | solution.py:1008
  308.4 3.8 %collective-permute-start.39 = (f32[8,192]{1,0:T(8,128)S(1)}, f32[8,192]{1,0:T(8,128)S(1)}, u32[]{:S(2)}, u32[]{:S(2)}) collective-permute-start(f32[8,192]{1,0:T(8,128)S(1)} %pad_maximum_fusion), channel_id=1, source_target_pairs={{0,4},{4,0},{1,5},{5,1},{2,6},{6,2},{3,7},{7,3},{8,12},{12,8},{9,1... | collective-permute-start | bytes 18440 | tf_op jit(solution)/shard_map/ppermute | solution.py:1008
  314.0 15.2 %collective-permute-start.40 = (f32[1,96,768]{2,1,0:T(8,128)S(1)}, f32[1,96,768]{2,1,0:T(8,128)S(1)}, u32[]{:S(2)}, u32[]{:S(2)}) collective-permute-start(f32[1,96,768]{2,1,0:T(8,128)S(1)} %slice_bitcast_fusion.3), channel_id=1, source_target_pairs={{0,16},{4,12},{8,24},{12,4},{16,0},{20,28},{24,8},{28,20},{1,17},{... | collective-permute-start | bytes 884744 | tf_op jit(solution)/shard_map/ppermute | solution.py:1016
  315.3 13.9 %collective-permute-start.41 = (f32[8,192]{1,0:T(8,128)S(1)}, f32[8,192]{1,0:T(8,128)S(1)}, u32[]{:S(2)}, u32[]{:S(2)}) collective-permute-start(f32[8,192]{1,0:T(8,128)S(1)} %add.55), channel_id=1, source_target_pairs={{0,8},{8,0},{16,24},{24,16},{1,9},{9,1},{17,25},{25,17},{2,10},{10... | collective-permute-start | bytes 18440 | tf_op jit(solution)/shard_map/ppermute | solution.py:1008
  329.2 19.4 %collective-permute-start.45 = (f32[512,768]{1,0:T(8,128)}, f32[512,768]{1,0:T(8,128)S(1)}, u32[]{:S(2)}, u32[]{:S(2)}) collective-permute-start(f32[512,768]{1,0:T(8,128)} %input_back.2.refs_0_), channel_id=1, source_target_pairs={{0,4},{4,0},{1,5},{5,1},{2,6},{6,2},{3,7},{7,3},{8,12},{12,8},{9,1... | collective-permute-start | bytes 4718600 | tf_op jit(solution)/shard_map/ppermute | solution.py:1008
  332.3 16.3 %collective-permute-start.42 = (f32[1,96,768]{2,1,0:T(8,128)S(1)}, f32[1,96,768]{2,1,0:T(8,128)S(1)}, u32[]{:S(2)}, u32[]{:S(2)}) collective-permute-start(f32[1,96,768]{2,1,0:T(8,128)S(1)} %get-tuple-element.211), channel_id=1, source_target_pairs={{0,8},{8,0},{16,24},{24,16},{1,9},{9,1},{17,25},{25,17},{2,10},{10... | collective-permute-start | bytes 884744 | tf_op jit(solution)/shard_map/ppermute | solution.py:1008
  333.7 15.0 %collective-permute-start.43 = (f32[1,96,768]{2,1,0:T(8,128)S(1)}, f32[1,96,768]{2,1,0:T(8,128)S(1)}, u32[]{:S(2)}, u32[]{:S(2)}) collective-permute-start(f32[1,96,768]{2,1,0:T(8,128)S(1)} %get-tuple-element.210), channel_id=1, source_target_pairs={{0,16},{8,24},{16,0},{24,8},{1,17},{9,25},{17,1},{25,9},{2,18},{10... | collective-permute-start | bytes 884744 | tf_op jit(solution)/shard_map/ppermute | solution.py:1008
  334.5 14.2 %collective-permute-start.44 = (f32[8,192]{1,0:T(8,128)S(1)}, f32[8,192]{1,0:T(8,128)S(1)}, u32[]{:S(2)}, u32[]{:S(2)}) collective-permute-start(f32[8,192]{1,0:T(8,128)S(1)} %add.58), channel_id=1, source_target_pairs={{0,16},{8,24},{16,0},{24,8},{1,17},{9,25},{17,1},{25,9},{2,18},{10... | collective-permute-start | bytes 18440 | tf_op jit(solution)/shard_map/ppermute | solution.py:1008
  350.9 3.5 collective-permute-start.46
  354.5 6.1 %collective-permute-start.47 = (f32[96]{0:T(128)S(1)}, f32[96]{0:T(128)S(1)}, u32[]{:S(2)}, u32[]{:S(2)}) collective-permute-start(f32[96]{0:T(128)S(1)} %add.61), channel_id=1, source_target_pairs={{0,2},{1,3},{2,0},{3,1},{4,6},{5,7},{6,4},{7,5},{8,10},{9,11},{10,... | collective-permute-start | bytes 1160 | tf_op jit(solution)/shard_map/ppermute | solution.py:1008
  (38 other events, 375.6 us)
Sparse Core Ops, SparseCore 0:
  61.5 44.6 all-gather.4
  117.7 38.0 all-gather.6
  157.7 38.9 all-gather.8
  198.4 38.9 all-gather.10
  240.6 53.8 reduce-scatter.1

commit v3 on v2

--- a/solution.py
+++ b/solution.py
@@ -578,28 +578,29 @@
     return jnp.concatenate([r[rows, i * wide : (i + 1) * wide] for r in refs], axis=1)
 
 
-def mixer_kernel(
-    taps, me_ref, x_ref, xr_ref, pa_ref, pb_ref, seg_ref, segrow_ref, sa_ref, sb_ref, gains_ref,
-    ah_ref, al_ref, bh_ref, bl_ref, own_ref, state_out_ref, resid_ref, nh_ref, nl_ref,
-    state, tail, segtail, grow, shrink, dec, end, full, mixed,
-):
+def mixer_kernel(taps, last, me_ref, proj_ref, seg_ref, segrow_ref, small_ref, *refs):
+    if last:
+        x_ref, xr_ref, other_ref, gains_ref, ah_ref, al_ref, bh_ref, bl_ref = refs[:8]
+        state_out_ref, resid_ref, nh_ref, nl_ref = refs[8:12]
+    else:
+        state_out_ref, mixed_ref = refs[:2]
+    state, tail, segtail, grow, shrink, dec, end, full, mixed = refs[-9:]
     size, lanes = grow.shape[0], dec.shape[0]
-    projs = (pa_ref, pb_ref)
+    projs = (proj_ref,)
 
     @pl.when(pl.program_id(0) == 0)
     def _():
         state[...] = jnp.zeros_like(state)
         tail[...] = jnp.zeros_like(tail)
         segtail[...] = jnp.full_like(segtail, -1.0)
-        fill_tables(pair(sa_ref, sb_ref)[2 + taps : 3 + taps], grow, shrink, dec, end, full)
-
-    kern = pair(sa_ref, sb_ref)[2 : 2 + taps]
+        fill_tables(small_ref[2 + taps : 3 + taps], grow, shrink, dec, end, full)
+
+    kern = small_ref[2 : 2 + taps]
     masks = lane_masks(lanes)
     square = square_mask(lanes)
-    model = state.shape[1]
-    groups = [slice(g * lanes, (g + 1) * lanes) for g in range(model // lanes)]
+    groups = [slice(g * lanes, (g + 1) * lanes) for g in range(state.shape[1] // lanes)]
     before_keys, before = tail[...], segtail[...]
-    for chunk in range(xr_ref.shape[0] // size):
+    for chunk in range(proj_ref.shape[0] // size):
         here = slice(chunk * size, (chunk + 1) * size)
         seg = seg_ref[here, :]
         extended = jnp.concatenate([before, seg], axis=0)
@@ -626,12 +627,13 @@
             state[:, s] = state[:, s] * (full[:, s] * goes_on) + end[:, s] * updates[g]
     tail[...] = before_keys
     segtail[...] = before
-    own_ref[...] = mixed[:, : own_ref.shape[1]]
-    third = ah_ref.shape[1]
+    if not last:
+        mixed_ref[...] = mixed[...]
+        return
     resid = (
         sequence_tile(pl.program_id(0), me_ref, x_ref, xr_ref)
-        + d3(split(mixed[:, :third]), (ah_ref[...], al_ref[...]), NT)
-        + d3(split(mixed[:, third:]), (bh_ref[...], bl_ref[...]), NT)
+        + d3(split(other_ref[...]), (ah_ref[...], al_ref[...]), NT)
+        + d3(split(mixed[...]), (bh_ref[...], bl_ref[...]), NT)
     )
     resid_ref[...] = resid
     nh_ref[...], nl_ref[...] = split(norm_parts(resid)[0] * gains_ref[1:2, :])
@@ -641,54 +643,61 @@
     return [pltpu.VMEM((BLOCK, model), f32)] * 2 + [pltpu.VMEM((LANES, model), f32)] * 3
 
 
-def run_mixer(me, x, projs, seg, segrow, smalls, gains, a, b, taps):
-    tokens, model = projs[0].shape[0], x[0].shape[2]
-    act = (tokens, model)
+def run_mixer(me, proj, seg, segrow, small, taps, more=(), ties=()):
+    tokens, third = proj.shape[0], proj.shape[1] // 3
     chunks = TILE // BLOCK
-    row = pl.BlockSpec((TILE, model), lambda c, m: (c, 0))
-    proj = pl.BlockSpec((TILE, projs[0].shape[1]), lambda c, m: (c, 0))
-    states = (tokens // BLOCK, LANES, model)
+
+    def row(width):
+        return pl.BlockSpec((TILE, width), lambda c, m: (c, 0))
+
+    extra_specs, extra = [], []
+    outs = [(row(third), shaped((tokens, third)))]
+    if more:
+        x, other, gains, a, b = more
+        model = x[0].shape[2]
+        extra_specs = sequence_specs(model, lambda i, m: i) + [row(third), whole(gains.shape)]
+        extra_specs = extra_specs + [whole(a[0].shape)] * 4
+        extra = [*x, other, gains, *a, *b]
+        outs = [(row(model), shaped((tokens, model), t)) for t in (f32, bf16, bf16)]
+    states = pl.BlockSpec((chunks, LANES, third), lambda c, m: (c, 0, 0))
+    tie_specs, tie_args = tied(ties)
     return pl.pallas_call(
-        partial(mixer_kernel, taps),
+        partial(mixer_kernel, taps, bool(more)),
         grid_spec=pltpu.PrefetchScalarGridSpec(
-        num_scalar_prefetch=1,
-        grid=(tokens // TILE,),
-        in_specs=sequence_specs(model, lambda i, m: i) + [
-            proj, proj,
-            pl.BlockSpec((TILE, 1), lambda c, m: (c, 0)),
-            pl.BlockSpec((chunks, 1, segrow.shape[2]), lambda c, m: (c, 0, 0)),
-            whole(smalls[0].shape), whole(smalls[1].shape), whole(gains.shape),
-        ]
-        + [whole(a[0].shape)] * 4,
-        out_specs=[
-            pl.BlockSpec((TILE, 256), lambda c, m: (c, 0)),
-            pl.BlockSpec((chunks, LANES, model), lambda c, m: (c, 0, 0)),
-            row, row, row,
-        ],
-        scratch_shapes=[
-            pltpu.VMEM((LANES, model), f32), pltpu.VMEM((8, model), f32), pltpu.VMEM((8, 1), f32)
-        ]
-        + mixer_scratch(model)
-        + [pltpu.VMEM((TILE, model), f32)],
+            num_scalar_prefetch=1,
+            grid=(tokens // TILE,),
+            in_specs=[
+                row(3 * third),
+                row(1),
+                pl.BlockSpec((chunks, 1, segrow.shape[2]), lambda c, m: (c, 0, 0)),
+                whole(small.shape),
+            ]
+            + extra_specs
+            + tie_specs,
+            out_specs=[states] + [spec for spec, _ in outs],
+            scratch_shapes=[
+                pltpu.VMEM((LANES, third), f32),
+                pltpu.VMEM((8, third), f32),
+                pltpu.VMEM((8, 1), f32),
+            ]
+            + mixer_scratch(third)
+            + [pltpu.VMEM((TILE, third), f32)],
         ),
-        out_shape=[
-            shaped((tokens, 256)), shaped(states), shaped(act),
-            shaped(act, bf16), shaped(act, bf16),
-        ],
+        out_shape=[shaped((tokens // BLOCK, LANES, third))] + [shape for _, shape in outs],
         compiler_params=params(),
-        cost_estimate=cost(3e10, 30 * 2**20),
-        name="mixer",
-    )(me, *x, *projs, seg, segrow, *smalls, gains, *a, *b)
+        cost_estimate=cost(6e9 + (7e9 if more else 0), 10 * 2**20),
+        name="mixer_out" if more else "mixer",
+    )(me, proj, seg, segrow, small, *extra, *tie_args)
 
 
 def mixer_back_kernel(
-    taps, me_ref, fng_ref, resid_ref, x_ref, xr_ref, ct_ref, cr_ref, pa_ref, pb_ref, ba_ref, bb_ref, state_ref,
-    mixed_ref, seg_ref, segb_ref, segrow_ref, sa_ref, sb_ref, gains_ref,
-    ah_ref, al_ref, bh_ref, bl_ref, *refs,
+    taps, me_ref, fng_ref, resid_ref, x_ref, xr_ref, ct_ref, cr_ref, pa_ref, pb_ref, ba_ref, bb_ref,
+    ta_ref, tb_ref, mixed_ref, seg_ref, segb_ref, segrow_ref, sa_ref, sb_ref, gains_ref,
+    ah_ref, al_ref, bh_ref, bl_ref, qah_ref, qal_ref, qbh_ref, qbl_ref, *refs,
 ):
     (
-        rg_ref, dq_ref, dk_ref, dv_ref, gg_ref, dkern_ref, keep_ref, send_ref,
-        grad, head, grow, shrink, dec, end, full, du_all, wg,
+        ig_ref, gg_ref, g2_ref, dkern_ref, keep_ref, send_ref,
+        grad, head, grow, shrink, dec, end, full, du_all, da, db, wg,
     ) = refs[-17:]
     size, lanes = grow.shape[0], dec.shape[0]
     step, steps = pl.program_id(0), pl.num_programs(0)
@@ -700,15 +709,15 @@
         head[...] = jnp.zeros_like(head)
         dkern_ref[...] = jnp.zeros_like(dkern_ref)
         gg_ref[...] = jnp.zeros_like(gg_ref)
+        g2_ref[...] = jnp.zeros_like(g2_ref)
         wg[...] = jnp.zeros_like(wg)
         fill_tables(pair(sa_ref, sb_ref)[2 + taps : 3 + taps], grow, shrink, dec, end, full)
 
     third = ah_ref.shape[1]
+    tile = steps - 1 - step
     back, gain_grad, _ = norm_back(resid_ref[...], gains_ref[1:2, :], fng_ref[...])
-    tile = steps - 1 - step
     rg = sequence_tile(tile, me_ref, ct_ref, cr_ref) + back
-    rg_ref[...] = rg
-    gg_ref[...] += gain_grad
+    g2_ref[...] += gain_grad
     r2 = split(rg)
     du_all[:, :third] = d3(r2, (ah_ref[...], al_ref[...]), NN)
     du_all[:, third:] = d3(r2, (bh_ref[...], bl_ref[...]), NN)
@@ -750,14 +759,17 @@
         dp = [split(p * allowed) for p in dp]
         dp_t = [split(p * allowed_t) for p in dp_t]
         for g, s in enumerate(groups):
-            entering = split(state_ref[chunk, :, s] * dec[:, s])
+            first = s.start < third
+            at = s.start - (0 if first else third)
+            to = da if first else db
+            states = (ta_ref if first else tb_ref)[chunk, :, at : at + lanes]
+            entering = split(states * dec[:, s])
             leaving = split(grad[:, s] * end[:, s])
             dqg = d3_low(dp[g], spread(kg[g], masks), NN) + living * d3_low(du[g], entering, NT)
             dkg = d3_low(dp_t[g], spread(qg[g], masks), NN) + kept * d3_low(v[g], leaving, NT)
-            dv_ref[here, s] = d3_low(p_t[g], spread(du[g], masks), NN) + kept * d3_low(
-                kg[g], leaving, NN
-            )
-            dq_ref[here, s] = dqg * grow[:, s]
+            dv = d3_low(p_t[g], spread(du[g], masks), NN) + kept * d3_low(kg[g], leaving, NN)
+            to[here, 2 * third + at : 2 * third + at + lanes] = dv
+            to[here, at : at + lanes] = dqg * grow[:, s]
             dshift = dkg * shrink[:, s]
             grad[:, s] = grad[:, s] * (full[:, s] * goes_on) + dec[:, s] * updates[g]
             total = kern[0:1, s] * dshift
@@ -766,7 +778,7 @@
                 longer = jnp.concatenate([part, head[j - 1, :, s]], axis=0)
                 total = total + kern[j : j + 1, s] * longer[j : j + size]
                 head[j - 1, :, s] = part[0:8]
-            dk_ref[here, s] = total
+            to[here, third + at : third + at + lanes] = total
             if g < 2:
                 for j in range(taps):
                     dkern_ref[j : j + 1, s] += jnp.sum(
@@ -775,9 +787,17 @@
 
     own = keep_ref.shape[-1] // 4
     x = sequence_tile(tile, me_ref, x_ref, xr_ref)
-    n = split(norm_parts(x)[0] * gains_ref[0:1, :])
-    joint = jnp.concatenate([r[:, :own] for r in (dq_ref, dk_ref, dv_ref)], axis=1)
-    wg[:, : 3 * own] += d3(n, split(joint), TN)
+    left, right = split(da[...]), split(db[...])
+    incoming = d3(left, (qah_ref[...], qal_ref[...]), NT)
+    incoming = incoming + d3(right, (qbh_ref[...], qbl_ref[...]), NT)
+    back, gain_grad, xhat = norm_back(x, gains_ref[0:1, :], incoming)
+    ig_ref[0] = rg + back
+    gg_ref[...] += gain_grad
+    n = split(xhat * gains_ref[0:1, :])
+    joint = tuple(
+        jnp.concatenate([p[:, i * third : i * third + own] for i in range(3)], axis=1) for p in left
+    )
+    wg[:, : 3 * own] += d3(n, joint, TN)
     wg[:, 3 * own :] += d3(r2, split(mixed_ref[:, :own]), TN)
 
     @pl.when(step == steps - 1)
@@ -786,7 +806,7 @@
 
 
 def run_mixer_back(
-    me, fng, resid, x, ct, projs, states, mixed, seg, segrow, smalls, gains, a, b, taps, ties=()
+    me, fng, resid, x, ct, projs, states, mixed, seg, segrow, smalls, gains, a, b, qa, qb, taps
 ):
     tokens, model = resid.shape
     third = projs[0].shape[1] // 3
@@ -794,7 +814,6 @@
     chunks = TILE // BLOCK
     last = tokens // TILE - 1
     blocks = (1, 4, model // 8, 4 * own)
-    tie_specs, tie_args = tied(ties)
 
     def prior(c):
         return jnp.maximum((last - c) * (TILE // 8) - 1, 0)
@@ -802,39 +821,46 @@
     row = pl.BlockSpec((TILE, model), lambda c, m: (last - c, 0))
     proj = pl.BlockSpec((TILE, 3 * third), lambda c, m: (last - c, 0))
     before = pl.BlockSpec((8, third), lambda c, m: (prior(c), 1))
+    state = pl.BlockSpec((chunks, LANES, third), lambda c, m: (last - c, 0, 0))
+    halves = pl.BlockSpec((1, TILE, model), lambda c, m: ((last - c) // 2, (last - c) % 2, 0))
     return pl.pallas_call(
         partial(mixer_back_kernel, taps),
         grid_spec=pltpu.PrefetchScalarGridSpec(
-        num_scalar_prefetch=1,
-        grid=(last + 1,),
-        in_specs=[row, row]
-        + sequence_specs(model, lambda c, m: last - c) * 2
-        + [
-            proj, proj, before, before,
-            pl.BlockSpec((chunks, LANES, model), lambda c, m: (last - c, 0, 0)),
-            pl.BlockSpec((TILE, 256), lambda c, m: (last - c, 0)),
-            pl.BlockSpec((TILE, 1), lambda c, m: (last - c, 0)),
-            pl.BlockSpec((8, 1), lambda c, m: (prior(c), 0)),
-            pl.BlockSpec((chunks, 1, segrow.shape[2]), lambda c, m: (last - c, 0, 0)),
-            whole(smalls[0].shape), whole(smalls[1].shape), whole(gains.shape),
-        ]
-        + [whole(a[0].shape)] * 4
-        + tie_specs,
-        out_specs=[row] * 4 + [whole((1, model)), whole((taps, model)), whole(blocks), whole(blocks)],
-        scratch_shapes=[
-            pltpu.VMEM((LANES, model), f32), pltpu.VMEM((taps - 1, 8, model), f32)
-        ]
-        + mixer_scratch(model)
-        + [pltpu.VMEM((TILE, model), f32), pltpu.VMEM((model, 4 * own), f32)],
+            num_scalar_prefetch=1,
+            grid=(last + 1,),
+            in_specs=[row, row]
+            + sequence_specs(model, lambda c, m: last - c) * 2
+            + [proj, proj, before, before, state, state]
+            + [
+                pl.BlockSpec((TILE, third), lambda c, m: (last - c, 0)),
+                pl.BlockSpec((TILE, 1), lambda c, m: (last - c, 0)),
+                pl.BlockSpec((8, 1), lambda c, m: (prior(c), 0)),
+                pl.BlockSpec((chunks, 1, segrow.shape[2]), lambda c, m: (last - c, 0, 0)),
+                whole(smalls[0].shape),
+                whole(smalls[1].shape),
+                whole(gains.shape),
+            ]
+            + [whole(a[0].shape)] * 4
+            + [whole(qa[0].shape)] * 4,
+            out_specs=[halves, whole((1, model)), whole((1, model)), whole((taps, model))]
+            + [whole(blocks), whole(blocks)],
+            scratch_shapes=[
+                pltpu.VMEM((LANES, model), f32),
+                pltpu.VMEM((taps - 1, 8, model), f32),
+            ]
+            + mixer_scratch(model)
+            + [pltpu.VMEM((TILE, model), f32)]
+            + [pltpu.VMEM((TILE, 3 * third), f32)] * 2
+            + [pltpu.VMEM((model, 4 * own), f32)],
         ),
-        out_shape=[shaped((tokens, model))] * 4
-        + [shaped((1, model)), shaped((taps, model)), shaped(blocks), shaped(blocks)],
+        out_shape=[shaped((2, tokens // 2, model)), shaped((1, model)), shaped((1, model))]
+        + [shaped((taps, model)), shaped(blocks), shaped(blocks)],
         compiler_params=params(),
-        cost_estimate=cost(8e10, 50 * 2**20),
+        cost_estimate=cost(1e11, 60 * 2**20),
         name="mixer_back",
     )(
-        me, fng, resid, *x, *ct, *projs, *projs, states, mixed, seg, seg, segrow, *smalls, gains,
-        *a, *b, *tie_args,
+        me, fng, resid, *x, *ct, *projs, *projs, *states, mixed, seg, seg, segrow, *smalls, gains,
+        *a, *b, *qa, *qb,
     )
 
 
@@ -895,9 +921,12 @@
     return jnp.where(step < 2, 1 - core, core) * 2 + (step & 1)
 
 
-def run_feed(me, n, ct, out, fng, w, own, final=False, ties=()):
+def run_feed(me, n, ct, out, fng, w, slot, slots, own, final=False, ties=()):
     tokens, model = n[0].shape
-    wide = w.shape[1]
+    wide = w.shape[1] // slots
+    part = pl.BlockSpec(
+        (model, wide), lambda *_: (0, slot), pipeline_mode=pl.Buffered(buffer_count=1)
+    )
     row = pl.BlockSpec((TILE, model), lambda i, m: (theirs_first(i, m), 0))
     tie_specs, tie_args = tied(ties)
     full = shaped((tokens, model))
@@ -910,7 +939,7 @@
             in_specs=[row] * 2
             + sequence_specs(model, theirs_first)
             + [row] * 2
-            + [whole(w.shape)]
+            + [part]
             + tie_specs,
             out_specs=[last if final else row, row] + ([whole((model, wide))] if own else []),
             scratch_shapes=[pltpu.VMEM((2, model, wide), bf16)],
@@ -932,50 +961,6 @@
         - xhat * jnp.mean(scaled * xhat, axis=-1, keepdims=True)
     )
     return grad, jnp.sum(incoming * xhat, axis=0, keepdims=True), xhat
-
-
-def input_back_kernel(
-    other, me_ref, x_ref, xr_ref, rg_ref, gains_ref, ah_ref, al_ref, bh_ref, bl_ref,
-    dq_ref, dk_ref, dv_ref, *refs,
-):
-    x = xr_ref[...] if other else x_ref[0]
-    third = ah_ref.shape[1] // 3
-    parts = (dq_ref, dk_ref, dv_ref)
-    left = split(jnp.concatenate([r[:, :third] for r in parts], axis=1))
-    right = split(jnp.concatenate([r[:, third:] for r in parts], axis=1))
-    incoming = d3(left, (ah_ref[...], al_ref[...]), NT) + d3(right, (bh_ref[...], bl_ref[...]), NT)
-    grad = rg_ref[...] + norm_back(x, gains_ref[0:1, :], incoming)[0]
-    refs[-1][...] = grad.reshape(refs[-1].shape)
-
-
-def run_input_back(me, other, x, rg, gains, a, b, dq, dk, dv, ties=()):
-    tokens, model = rg.shape
-    tie_specs, tie_args = tied(ties)
-
-    def tile(i, m):
-        core = m[0] & 1
-        return (1 - core if other else core) * 2 + i
-
-    row = pl.BlockSpec((TILE, model), lambda i, m: (tile(i, m), 0))
-    return pl.pallas_call(
-        partial(input_back_kernel, other),
-        grid_spec=pltpu.PrefetchScalarGridSpec(
-            num_scalar_prefetch=1,
-            grid=(tokens // 2 // TILE,),
-            in_specs=sequence_specs(model, tile)
-            + [row, whole(gains.shape)]
-            + [whole(a[0].shape)] * 4
-            + [row, row, row]
-            + tie_specs,
-            out_specs=pl.BlockSpec((TILE, model), lambda i, m: (i, 0))
-            if other
-            else pl.BlockSpec((1, TILE, model), lambda i, m: (m[0] & 1, i, 0)),
-        ),
-        out_shape=shaped((tokens // 2, model) if other else (2, tokens // 2, model)),
-        compiler_params=params(),
-        cost_estimate=cost(9 * tokens * model * model, 20 * 2**20),
-        name="input_back",
-    )(me, *x, rg, gains, *a, *b, dq, dk, dv, *tie_args)
 
 
 def leave_kernel(me_ref, came_ref, whole_ref, o_ref):
@@ -1091,9 +1076,8 @@
     )
     a1 = exchange(a0, "tensor", 1)
     near0 = sides(a0)
-    up_weight, down_weight, early = after((up_weight, down_weight, layer_input), a0)
-    f0 = run_pack_feed(up_weight, down_weight)
-    x_came = other_half(early)
+    f0 = run_pack_feed(*after((up_weight, down_weight), a0))
+    x_came = other_half(after((layer_input,), a0)[0])
 
     b0, b1, near0 = after((a0, a1, near0), f0)
     a2 = exchange(b0, "tensor", 2)
@@ -1118,6 +1102,7 @@
     far2 = far(*near2)
     near3 = exchange(b3, "dp", 1), exchange(b3, "dp", 2)
     f1 = exchange(g0, "tensor", 1)
+    f2 = exchange(g0, "tensor", 2)
     first0 = by_distance(a0, near0, other0[:2], far0, other0[2])
     first1 = by_distance(a1, near1, other1[:2], far1, other1[2])
     x = (layer_input, x_came)
@@ -1127,77 +1112,70 @@
     other2 = across_cores(*inner[:2], inner[3])
     other3 = exchange(inner[2], "ctx", 1)
 
-    near3, g0, late = after((near3, f0, cotangent), far2, proj_a)
+    near3, late = after((near3, cotangent), far2, proj_a)
     far3 = far(*near3)
-    f2 = exchange(g0, "tensor", 2)
+    ct = (cotangent, other_half(late))
+    segrow = jnp.tile(seg.reshape(-1, 1, BLOCK), (1, 1, PAIR))
+    seg = seg[:, None]
+    states_a, mixed_a = run_mixer(me, proj_a, seg, segrow, wa[5], taps)
+    f1, f2, far3, g0 = after((f1, f2, far3, f0), mixed_a)
+    w12 = gathered(jnp.concatenate([f1, f2], axis=1))
     inner = after(near3, far3)
     near3 = (*near3, other3)
     other3 = across_cores(*inner, far3)
-    ct = (cotangent, other_half(late))
-    segrow = jnp.tile(seg.reshape(-1, 1, BLOCK), (1, 1, PAIR))
-    seg = seg[:, None]
     first2 = by_distance(a2, near2, other2[:2], far2, other2[2])
     first3 = by_distance(a3, near3, other3[:2], far3, other3[2])
     proj_b, *wb = run_project(me, x, first2, first3)
-    f1, g0 = after((f1, f0), proj_b, ct, seg)
-    w1 = gathered(f1)
+    (g0,) = after((g0,), proj_b, ct)
     f3 = exchange(g0, "tensor", 3)
 
     projs, gains, smalls = (proj_a, proj_b), wa[4], (wa[5], wb[5])
-    mixed, states, resid, nh, nl = run_mixer(
-        me, x, projs, seg, segrow, smalls, gains, wa[2:4], wb[2:4], taps
-    )
-    (f2,) = after((f2,), resid)
-    w2 = gathered(f2)
+    more = (x, mixed_a, gains, wa[2:4], wb[2:4])
+    states_b, resid, nh, nl = run_mixer(me, proj_b, seg, segrow, wb[5], taps, more)
     n = (nh, nl)
-    out, fng, feed_g = run_feed(me, n, ct, resid, resid, w0, True)
+    out, fng, feed_g = run_feed(me, n, ct, resid, resid, w0, 0, 1, True)
     (f3,) = after((f3,), fng)
     w3 = gathered(f3)
-    out, fng = run_feed(me, n, ct, out, fng, w1, False)
-    out, fng = run_feed(me, n, ct, out, fng, w2, False)
-    halves, fng = run_feed(me, n, ct, out, fng, w3, False, True)
+    out, fng = run_feed(me, n, ct, out, fng, w12, 0, 2, False)
+    out, fng = run_feed(me, n, ct, out, fng, w12, 1, 2, False)
+    out_halves, fng = run_feed(me, n, ct, out, fng, w3, 0, 1, False, True)
     feed_g = lax.psum_scatter(feed_g, plane, scatter_dimension=0, tiled=True)
+    came = other_half(out_halves)
+    halves, mixer_gain_g, feed_gain_g, kern_g, keep, send = run_mixer_back(
+        me, fng, resid, x, ct, projs, (states_a, states_b), mixed_a, seg, segrow, smalls, gains,
+        wa[2:4], wb[2:4], wa[:2], wb[:2], taps,
+    )
+    layer_output = run_leave(me, out_halves, came)
+    core = lax.axis_index("ctx")
+    came_send = exchange(send, "ctx", 1)
+    diagonal = keep[:, 3] + came_send[:, 3]
+    keep, came_send = after((keep, came_send), diagonal)
+    kern_g = kern_g[:, :own].reshape(taps, 8, few).transpose(1, 0, 2).reshape(8, taps * few)
+    gains_g = [g.reshape(8, rows) for g in (mixer_gain_g, feed_gain_g)]
+    tiny = jnp.concatenate(gains_g + [kern_g], axis=1)
+    diagonal = corner(diagonal)
+    tiny = tiny + exchange(tiny, "ctx", 1)
     came = other_half(halves)
-    rg, dq, dk, dv, feed_gain_g, kern_g, keep, send = run_mixer_back(
-        me, fng, resid, x, ct, projs, states, mixed, seg, segrow, smalls, gains, wa[2:4], wb[2:4],
-        taps,
-    )
-    kern_g = kern_g[:, :own].reshape(taps, 8, few).transpose(1, 0, 2).reshape(8, taps * few)
-    tiny = jnp.concatenate([feed_gain_g.reshape(8, rows), kern_g], axis=1)
-    came_send, came_tiny = exchange(send, "ctx", 1), exchange(tiny, "ctx", 1)
-    layer_output = run_leave(me, halves, came)
-    keep, came_send, tiny, came_tiny = after((keep, came_send, tiny, came_tiny), layer_output)
-    summed = keep + came_send
-    tiny = tiny + came_tiny
-    diagonal, came_tiny = corner(summed[:, 3]), exchange(tiny, "dp", 1)
-    theirs = run_input_back(me, True, x, rg, gains, wa[:2], wb[:2], dq, dk, dv, (summed,))
-    diagonal, theirs, came_tiny = after((diagonal, theirs, came_tiny))
-    tiny = tiny + came_tiny
-    core = lax.axis_index("ctx")
-    to_x = exchange(jnp.where(core == 0, summed[:, 1] + diagonal, summed[:, 1]), "dp", 1)
-    to_y = exchange(jnp.where(core == 0, summed[:, 2], summed[:, 2] + diagonal), "dp", 2)
-    came_tiny = exchange(tiny, "dp", 2)
-    came = exchange(theirs, "ctx", 1)
-    mine = run_input_back(me, False, x, rg, gains, wa[:2], wb[:2], dq, dk, dv, (theirs,))
-    to_x, to_y, came_tiny, came, mine = after((to_x, to_y, came_tiny, came, mine))
-    mixer_g = (summed[:, 0] + to_x + to_y)[0]
-    tiny = lax.dynamic_index_in_dim(tiny + came_tiny, position, 0, keepdims=False)
-    joint = jnp.concatenate([query_weight, key_weight, value_weight], axis=1)
-    gain_g = jnp.sum(mixer_g[:, : 3 * own] * joint, axis=1) / mixer_gain
-    gain_g = gain_g + exchange(gain_g, "tensor", 1)
-    came_gain = exchange(gain_g, "tensor", 2)
-    input_grad = run_leave(me, mine, came)
+    to_own, to_x, to_y = (keep[:, i] + came_send[:, i] for i in range(3))
+    diagonal, to_own, to_x, to_y, tiny, came = after((diagonal, to_own, to_x, to_y, tiny, came))
+    came_x = exchange(jnp.where(core == 0, to_x + diagonal, to_x), "dp", 1)
+    came_y = exchange(jnp.where(core == 0, to_y, to_y + diagonal), "dp", 2)
+    tiny = tiny + exchange(tiny, "dp", 1)
+    input_grad = run_leave(me, halves, came)
+    tiny = tiny + exchange(tiny, "dp", 2)
+    mixer_g = (to_own + came_x + came_y)[0]
+    tiny = lax.dynamic_index_in_dim(tiny, position, 0, keepdims=False)
     hidden = up_weight.shape[1]
     return (
         layer_output,
         input_grad,
-        gain_g + came_gain,
+        tiny[:rows],
         mixer_g[:, :own],
         mixer_g[:, own : 2 * own],
         mixer_g[:, 2 * own : 3 * own],
-        tiny[rows:].reshape(taps, few),
+        tiny[2 * rows :].reshape(taps, few),
         mixer_g[:, 3 * own :].T,
-        tiny[:rows],
+        tiny[rows : 2 * rows],
         feed_g[:, :hidden],
         feed_g[:, hidden:].T,
     )
@@ -1211,10 +1189,9 @@
         heads, width = arrays[7].shape
         fits = (
             (shape["dp"], shape["ctx"], shape["tensor"]) == (4, 2, 4)
-            and rows == 2
-            and (heads * shape["tensor"]) % (2 * PAIR) == 0
+            and (rows, length) == (2, 2 * TILE)
             and PAIR * width == LANES
-            and length % (BLOCK // 2) == 0
+            and 2 * heads * width % LANES == 0
         )
         return (by_sequence if fits else on_device)(*arrays)
 

time: 376 us -> 340 us (0.904)
  waiting for transfers between devices: 56.7 us -> 31.7 us
  Pallas kernels: 227 us -> 218 us
    pallas_call x3 -> x2, Pallas kernels: 49.7 us -> 27 us  [run_mixer(): pl.pallas_call(partial(mixer_kernel, taps, bool(more)), grid_spec=pltpu.P...]
    pallas_call x1, Pallas kernels: 45.1 us -> 58.8 us  [run_mixer_back(): pl.pallas_call(partial(mixer_back_kernel, taps), grid_spec=pltpu.Prefetch...]
    all_gather x4 -> x3, waiting for transfers between devices: 12 us -> 0.02 us  [gathered(): return lax.all_gather(block, plane, axis=0, tiled=True)]
    ppermute x5, waiting for transfers between devices: 16.5 us -> 7.68 us  [corner(): return lax.ppermute(value, ('dp', 'ctx'), pairs)]
    ppermute x43 -> x41, waiting for transfers between devices: 27.8 us -> 23.5 us  [exchange(): return lax.ppermute(value, axis, [(i, i ^ flip) for i in range(count)])]
    ppermute x43 -> x41, starting transfers between devices: 36.7 us -> 37.7 us  [exchange(): return lax.ppermute(value, axis, [(i, i ^ flip) for i in range(count)])]
  transfers between devices with their start and end apart: 53 -> 50, of which waited for: 18 -> 17; matrix products, arithmetic and copies ran while one was open for 4% -> 5% of each run, Pallas kernels for 61% -> 65%
where the time goes in v3:
time: 340 us; the launch traced here: 333 us
  Pallas kernels  218 us (64%)
  starting transfers between devices  43 us (13%)
  waiting for transfers between devices  31.7 us (9%)
  local copies, waits for them, and re-layouts  19.1 us (6%)
  between operations  14.4 us (4%)
  other arithmetic  7.02 us (2%)
    pallas_call x4, Pallas kernels, run_feed(): pl.pallas_call(partial(feed_kernel, own, final), grid_spec=pltpu.Prefetch...  97.6 us
    pallas_call x1, Pallas kernels, run_mixer_back(): pl.pallas_call(partial(mixer_back_kernel, taps), grid_spec=pltpu.Prefetch...  58.8 us
    ppermute x41, starting transfers between devices, exchange(): return lax.ppermute(value, axis, [(i, i ^ flip) for i in range(count)])  37.7 us
    pallas_call x2, Pallas kernels, run_mixer(): pl.pallas_call(partial(mixer_kernel, taps, bool(more)), grid_spec=pltpu.P...  27 us
    pallas_call x2, Pallas kernels, run_project(): pl.pallas_call(project_kernel, grid_spec=pltpu.PrefetchScalarGridSpec(num...  25.7 us
    ppermute x41, waiting for transfers between devices, exchange(): return lax.ppermute(value, axis, [(i, i ^ flip) for i in range(count)])  23.5 us
    ppermute x5, waiting for transfers between devices, corner(): return lax.ppermute(value, ('dp', 'ctx'), pairs)  7.68 us
    unnamed x75, local copies, waits for them, and re-layouts  7.23 us
  transfers between devices with their start and end apart: 50, of which 17 were waited for; matrix products, arithmetic and copies ran while one was open for 5% of the time, Pallas kernels for 65%

profile of v3, /device:TPU:0, one launch (start us, length us, event | category | flops | bytes accessed | tf_op | source)
XLA Modules:
  0.0 333.2 jit_solution(14960260155074598575)
XLA Ops:
  7.2 2.1 pack_mixer.1.refs_0_
  9.4 1.6 dynamic-slice_bitcast_fusion.3
  11.5 2.9 collective-permute-start.3
  14.4 1.5 collective-permute-start.2
  15.9 1.6 collective-permute-start.1
  18.4 2.1 pack_feed.1
  20.5 1.7 collective-permute-done.3.refs_4_
  22.2 1.5 collective-permute-done.2.refs_2_
  23.7 1.3 collective-permute-done.1.refs_8_
  25.6 2.6 collective-permute-start.5
  28.2 1.6 collective-permute-start.7
  30.3 4.9 %collective-permute-done.8.refs_6_ = f32[104,768]{1,0:T(8,128)S(1)} collective-permute-done((f32[104,768]{1,0:T(8,128)S(1)}, f32[104,768]{1,0:T(8,128)S(1)}, u32[]{:S(2)}, u32[]{:S(2)}) %collective-permute-start.8) | collective-permute-done | bytes 319520 | tf_op jit(solution)/shard_map/ppermute | solution.py:1001
  35.1 6.1 %collective-permute-done.5.refs_0_ = f32[104,768]{1,0:T(8,128)S(1)} collective-permute-done((f32[104,768]{1,0:T(8,128)S(1)}, f32[104,768]{1,0:T(8,128)S(1)}, u32[]{:S(2)}, u32[]{:S(2)}) %collective-permute-start.5) | collective-permute-done | bytes 319520 | tf_op jit(solution)/shard_map/ppermute | solution.py:993
  45.1 3.5 %collective-permute-start.14 = (f32[104,768]{1,0:T(8,128)S(1)}, f32[104,768]{1,0:T(8,128)}, u32[]{:S(2)}, u32[]{:S(2)}) collective-permute-start(f32[104,768]{1,0:T(8,128)S(1)} %copy-done.5), channel_id=1, source_target_pairs={{0,3},{1,2},{2,1},{3,0},{4,7},{5,6},{6,5},{7,4},{8,11},{9,10},{10,... | collective-permute-start | bytes 958472 | tf_op jit(solution)/shard_map/ppermute | solution.py:993
  48.6 1.4 collective-permute-start.16
  50.0 1.4 collective-permute-start.15
  52.0 5.2 %collective-permute-done.14.refs_8_ = f32[104,768]{1,0:T(8,128)} collective-permute-done((f32[104,768]{1,0:T(8,128)S(1)}, f32[104,768]{1,0:T(8,128)}, u32[]{:S(2)}, u32[]{:S(2)}) %collective-permute-start.14) | collective-permute-done | bytes 319520 | tf_op jit(solution)/shard_map/ppermute | solution.py:993
  57.2 1.2 collective-permute-done.16.refs_4_
  59.8 1.1 collective-permute-done.31
  62.5 1.5 collective-permute-start.23
  64.6 4.3 %collective-permute-start.29 = (f32[96,1536]{1,0:T(8,128)S(1)}, f32[96,1536]{1,0:T(8,128)S(1)}, u32[]{:S(2)}, u32[]{:S(2)}) collective-permute-start(f32[96,1536]{1,0:T(8,128)S(1)} %copy-done.1), channel_id=1, source_target_pairs={{0,2},{1,3},{2,0},{3,1},{4,6},{5,7},{6,4},{7,5},{8,10},{9,11},{10,... | collective-permute-start | bytes 1769480 | tf_op jit(solution)/shard_map/ppermute | solution.py:993
  69.3 1.5 collective-permute-start.20
  70.7 12.8 %project.2 = (f32[1024,1152]{1,0:T(8,128)}, bf16[768,1152]{1,0:T(8,128)(2,1)}, bf16[768,1152]{1,0:T(8,128)(2,1)}, bf16[768,384]{1,0:T(8,128)(2,1)}, bf16[768,384...) custom-call(s32[1]{0:T(128)} %bitcast.me_ref, f32[2,512,768]{2,1,0:T(8,128)} %x_ref.5, ...), custom_call_target="tpu_custom_call" | custom-call | flops 5435817984 | bytes 20971520 | tf_op jit(solution)/shard_map/project/pallas_call | solution.py:496
  84.9 8.5 %mixer.1 = (f32[8,128,384]{2,1,0:T(8,128)}, f32[1024,384]{1,0:T(8,128)}) custom-call(s32[1]{0:T(128)} %bitcast.me_ref, f32[1024,1152]{1,0:T(8,128)} %get-tuple-element.111.proj_ref.pa_ref.ba_ref, f32[1024,1]{1,0:T(8,128)} %select_convert_fusion.seg_ref.segb_ref, f32[8,1,256]{2,1,0:T(1,128)} %bitcast.39, f32[8,384]{1,0:T(8,128)} %get-tuple-element.119.small_ref.sa_ref), custom_call_target="tpu_custom_call" | custom-call | flops 6000000000 | bytes 10485760 | tf_op jit(solution)/shard_map/mixer/pallas_call | solution.py:664
  93.4 1.4 collective-permute-done.29
  94.8 1.1 pad_maximum_fusion
  98.5 1.1 collective-permute-done.25.refs_5_
  100.5 1.6 dynamic-slice_bitcast_fusion.2
  104.8 12.9 %project.3 = (f32[1024,1152]{1,0:T(8,128)}, bf16[768,1152]{1,0:T(8,128)(2,1)}, bf16[768,1152]{1,0:T(8,128)(2,1)}, bf16[768,384]{1,0:T(8,128)(2,1)}, bf16[768,384...) custom-call(s32[1]{0:T(128)} %bitcast.me_ref, f32[2,512,768]{2,1,0:T(8,128)} %x_ref.5, ...), custom_call_target="tpu_custom_call" | custom-call | flops 5435817984 | bytes 20971520 | tf_op jit(solution)/shard_map/project/pallas_call | solution.py:496
  117.7 18.5 %mixer_out.1 = (f32[8,128,384]{2,1,0:T(8,128)}, f32[1024,768]{1,0:T(8,128)}, bf16[1024,768]{1,0:T(8,128)(2,1)}, bf16[1024,768]{1,0:T(8,128)(2,1)}) custom-call(s32[1]{0:T(128)} %bitcast.me_ref, f32[1024,1152]{1,0:T(8,128)} %get-tuple-element.124.proj_ref.pb_ref.bb_ref, f32[1024,1]{1,0:T(8,128)} %select_convert_fusion.seg_ref.segb_ref, ...), custom_call_target="tpu_custom_call" | custom-call | flops 12999999488 | bytes 10485760 | tf_op jit(solution)/shard_map/mixer_out/pallas_call | solution.py:664
  136.2 3.0 collective-permute-start.36
  139.2 30.3 %feed_own.1 = (f32[1024,768]{1,0:T(8,128)}, f32[1024,768]{1,0:T(8,128)}, f32[768,1536]{1,0:T(8,128)}) custom-call(s32[1]{0:T(128)} %bitcast.me_ref, bf16[1024,768]{1,0:T(8,128)(2,1)} %get-tuple-element.131.nh_ref, bf16[1024,768]{1,0:T(8,128)(2,1)} %get-tuple-element.132.nl_ref, f32[2,512,768]{2,1,0:T(8,128)} %ct_ref.9, ...), custom_call_target="tpu_custom_call" | custom-call | flops 21743271936 | bytes 31457280 | tf_op jit(solution)/shard_map/feed_own/pallas_call | solution.py:934
  171.0 22.5 %feed.3 = (f32[1024,768]{1,0:T(8,128)}, f32[1024,768]{1,0:T(8,128)}) custom-call(s32[1]{0:T(128)} %bitcast.me_ref, bf16[1024,768]{1,0:T(8,128)(2,1)} %get-tuple-element.131.nh_ref, bf16[1024,768]{1,0:T(8,128)(2,1)} %get-tuple-element.132.nl_ref, f32[2,512,768]{2,1,0:T(8,128)} %ct_ref.9, f32[512,768]{1,0:T(8,128)} %collective-permute-done.35.cr_ref, ...), custom_call_target="tpu_custom_call" | custom-call | flops 14495514624 | bytes 31457280 | tf_op jit(solution)/shard_map/feed/pallas_call | solution.py:934
  193.6 22.2 %feed.4 = (f32[1024,768]{1,0:T(8,128)}, f32[1024,768]{1,0:T(8,128)}) custom-call(s32[1]{0:T(128)} %bitcast.me_ref, bf16[1024,768]{1,0:T(8,128)(2,1)} %get-tuple-element.131.nh_ref, bf16[1024,768]{1,0:T(8,128)(2,1)} %get-tuple-element.132.nl_ref, f32[2,512,768]{2,1,0:T(8,128)} %ct_ref.9, f32[512,768]{1,0:T(8,128)} %collective-permute-done.35.cr_ref, ...), custom_call_target="tpu_custom_call" | custom-call | flops 14495514624 | bytes 31457280 | tf_op jit(solution)/shard_map/feed/pallas_call | solution.py:934
  215.8 22.6 %feed.5 = (f32[2,512,768]{2,1,0:T(8,128)}, f32[1024,768]{1,0:T(8,128)}) custom-call(s32[1]{0:T(128)} %bitcast.me_ref, bf16[1024,768]{1,0:T(8,128)(2,1)} %get-tuple-element.131.nh_ref, bf16[1024,768]{1,0:T(8,128)(2,1)} %get-tuple-element.132.nl_ref, f32[2,512,768]{2,1,0:T(8,128)} %ct_ref.9, f32[512,768]{1,0:T(8,128)} %collective-permute-done.35.cr_ref, ...), custom_call_target="tpu_custom_call" | custom-call | flops 14495514624 | bytes 31457280 | tf_op jit(solution)/shard_map/feed/pallas_call | solution.py:934
  238.3 58.8 %mixer_back.1 = (f32[2,512,768]{2,1,0:T(8,128)}, f32[1,768]{1,0:T(1,128)}, f32[1,768]{1,0:T(1,128)}, f32[4,768]{1,0:T(4,128)}, f32[1,4,96,768]{3,2,1,0:T(8,128)}, /*index=5*/f32[1,4,96,768]{3,2,1,0:T(8,128)}) custom-call(s32[1]{0:T(128)} %bitcast.me_ref, f32[1024,768]{1,0:T(8,128)} %get-tuple-element.147.fng_ref, ...), custom_call_target="tpu_custom_call" | custom-call | flops 99999997952 | bytes 62914560 | tf_op jit(solution)/shard_map/mixer_back/pallas_call | solution.py:826
  297.3 1.7 dynamic-slice_bitcast_fusion
  301.4 1.1 fusion
  302.4 1.6 collective-permute-start.39
  304.1 2.3 add_bitcast_fusion.1
  306.5 2.8 collective-permute-done.39
  309.9 2.0 collective-permute-start.42
  312.0 1.9 slice_bitcast_fusion
  313.9 1.3 collective-permute-start.43
  315.2 1.2 add_select_fusion.1
  316.4 1.5 collective-permute-start.44
  318.9 2.3 leave.3
  321.3 2.3 leave.2
  (181 shorter events, 26.8 us)
Async XLA Ops:
  7.2 132.0 %all-gather.4.cloned.1.call-start = ((), (), s32[]{:S(2)}) async-start(), calls=%async_computation.1 | async-start | bytes 5308416 | tf_op jit(solution)/shard_map/all_gather | solution.py:1071
  10.9 33.4 %collective-permute-start = (f32[512,768]{1,0:T(8,128)S(1)}, f32[512,768]{1,0:T(8,128)}, u32[]{:S(2)}, u32[]{:S(2)}) collective-permute-start(f32[512,768]{1,0:T(8,128)S(1)} %dynamic-slice_bitcast_fusion.3), channel_id=1, source_target_pairs={{0,4},{4,0},{1,5},{5,1},{2,6},{6,2},{3,7},{7,3},{8,12},{12,8},{9,1... | collective-permute-start | bytes 4718600 | tf_op jit(solution)/shard_map/ppermute | solution.py:993
  11.4 9.1 %collective-permute-start.4 = (f32[104,768]{1,0:T(8,128)S(1)}, f32[104,768]{1,0:T(8,128)S(1)}, u32[]{:S(2)}, u32[]{:S(2)}) collective-permute-start(f32[104,768]{1,0:T(8,128)S(1)} %copy-done.5), channel_id=1, source_target_pairs={{0,4},{4,0},{1,5},{5,1},{2,6},{6,2},{3,7},{7,3},{8,12},{12,8},{9,1... | collective-permute-start | bytes 958472 | tf_op jit(solution)/shard_map/ppermute | solution.py:993
  11.5 10.7 %collective-permute-start.3 = (f32[104,768]{1,0:T(8,128)S(1)}, f32[104,768]{1,0:T(8,128)S(1)}, u32[]{:S(2)}, u32[]{:S(2)}) collective-permute-start(f32[104,768]{1,0:T(8,128)S(1)} %copy-done.5), channel_id=1, source_target_pairs={{0,16},{8,24},{16,0},{24,8},{1,17},{9,25},{17,1},{25,9},{2,18},{10... | collective-permute-start | bytes 958472 | tf_op jit(solution)/shard_map/ppermute | solution.py:993
  14.4 9.2 %collective-permute-start.2 = (f32[104,768]{1,0:T(8,128)S(1)}, f32[104,768]{1,0:T(8,128)S(1)}, u32[]{:S(2)}, u32[]{:S(2)}) collective-permute-start(f32[104,768]{1,0:T(8,128)S(1)} %copy-done.5), channel_id=1, source_target_pairs={{0,8},{8,0},{16,24},{24,16},{1,9},{9,1},{17,25},{25,17},{2,10},{10... | collective-permute-start | bytes 958472 | tf_op jit(solution)/shard_map/ppermute | solution.py:993
  15.9 9.1 %collective-permute-start.1 = (f32[104,768]{1,0:T(8,128)S(1)}, f32[104,768]{1,0:T(8,128)}, u32[]{:S(2)}, u32[]{:S(2)}) collective-permute-start(f32[104,768]{1,0:T(8,128)S(1)} %copy-done.5), channel_id=1, source_target_pairs={{0,1},{1,0},{2,3},{3,2},{4,5},{5,4},{6,7},{7,6},{8,9},{9,8},{10,11... | collective-permute-start | bytes 958472 | tf_op jit(solution)/shard_map/ppermute | solution.py:993
  25.1 10.1 %collective-permute-start.8 = (f32[104,768]{1,0:T(8,128)S(1)}, f32[104,768]{1,0:T(8,128)S(1)}, u32[]{:S(2)}, u32[]{:S(2)}) collective-permute-start(f32[104,768]{1,0:T(8,128)S(1)} %broadcast_select_fusion.3), channel_id=1, source_target_pairs={{0,16},{4,12},{8,24},{12,4},{16,0},{20,28},{24,8},{28,20},{1,17},{... | collective-permute-start | bytes 958472 | tf_op jit(solution)/shard_map/ppermute | solution.py:1001
  25.6 15.7 %collective-permute-start.5 = (f32[104,768]{1,0:T(8,128)S(1)}, f32[104,768]{1,0:T(8,128)S(1)}, u32[]{:S(2)}, u32[]{:S(2)}) collective-permute-start(f32[104,768]{1,0:T(8,128)S(1)} %copy-done.5), channel_id=1, source_target_pairs={{0,2},{1,3},{2,0},{3,1},{4,6},{5,7},{6,4},{7,5},{8,10},{9,11},{10,... | collective-permute-start | bytes 958472 | tf_op jit(solution)/shard_map/ppermute | solution.py:993
  28.2 13.1 %collective-permute-start.7 = (f32[104,768]{1,0:T(8,128)}, f32[104,768]{1,0:T(8,128)S(1)}, u32[]{:S(2)}, u32[]{:S(2)}) collective-permute-start(f32[104,768]{1,0:T(8,128)} %collective-permute-done.1.refs_8_), channel_id=1, source_target_pairs={{0,16},{8,24},{16,0},{24,8},{1,17},{9,25},{17,1},{25,9},{2,18},{10... | collective-permute-start | bytes 958472 | tf_op jit(solution)/shard_map/ppermute | solution.py:993
  29.7 12.0 %collective-permute-start.6 = (f32[104,768]{1,0:T(8,128)}, f32[104,768]{1,0:T(8,128)S(1)}, u32[]{:S(2)}, u32[]{:S(2)}) collective-permute-start(f32[104,768]{1,0:T(8,128)} %collective-permute-done.1.refs_8_), channel_id=1, source_target_pairs={{0,8},{8,0},{16,24},{24,16},{1,9},{9,1},{17,25},{25,17},{2,10},{10... | collective-permute-start | bytes 958472 | tf_op jit(solution)/shard_map/ppermute | solution.py:993
  35.1 6.7 %collective-permute-start.9 = (f32[104,768]{1,0:T(8,128)S(1)}, f32[104,768]{1,0:T(8,128)S(1)}, u32[]{:S(2)}, u32[]{:S(2)}) collective-permute-start(f32[104,768]{1,0:T(8,128)S(1)} %collective-permute-done.2.refs_2_), channel_id=1, source_target_pairs={{0,4},{4,0},{1,5},{5,1},{2,6},{6,2},{3,7},{7,3},{8,12},{12,8},{9,1... | collective-permute-start | bytes 958472 | tf_op jit(solution)/shard_map/ppermute | solution.py:993
  41.3 2.1 collective-permute-start.11
  44.4 7.1 %collective-permute-start.12 = (f32[104,768]{1,0:T(8,128)S(1)}, f32[104,768]{1,0:T(8,128)S(1)}, u32[]{:S(2)}, u32[]{:S(2)}) collective-permute-start(f32[104,768]{1,0:T(8,128)S(1)} %broadcast_select_fusion.2), channel_id=1, source_target_pairs={{0,16},{4,12},{8,24},{12,4},{16,0},{20,28},{24,8},{28,20},{1,17},{... | collective-permute-start | bytes 958472 | tf_op jit(solution)/shard_map/ppermute | solution.py:1001
  45.1 12.1 %collective-permute-start.14 = (f32[104,768]{1,0:T(8,128)S(1)}, f32[104,768]{1,0:T(8,128)}, u32[]{:S(2)}, u32[]{:S(2)}) collective-permute-start(f32[104,768]{1,0:T(8,128)S(1)} %copy-done.5), channel_id=1, source_target_pairs={{0,3},{1,2},{2,1},{3,0},{4,7},{5,6},{6,5},{7,4},{8,11},{9,10},{10,... | collective-permute-start | bytes 958472 | tf_op jit(solution)/shard_map/ppermute | solution.py:993
  48.6 9.8 %collective-permute-start.16 = (f32[104,768]{1,0:T(8,128)S(1)}, f32[104,768]{1,0:T(8,128)S(1)}, u32[]{:S(2)}, u32[]{:S(2)}) collective-permute-start(f32[104,768]{1,0:T(8,128)S(1)} %collective-permute-done.5.refs_0_), channel_id=1, source_target_pairs={{0,16},{8,24},{16,0},{24,8},{1,17},{9,25},{17,1},{25,9},{2,18},{10... | collective-permute-start | bytes 958472 | tf_op jit(solution)/shard_map/ppermute | solution.py:993
  50.0 8.6 %collective-permute-start.15 = (f32[104,768]{1,0:T(8,128)S(1)}, f32[104,768]{1,0:T(8,128)S(1)}, u32[]{:S(2)}, u32[]{:S(2)}) collective-permute-start(f32[104,768]{1,0:T(8,128)S(1)} %collective-permute-done.5.refs_0_), channel_id=1, source_target_pairs={{0,8},{8,0},{16,24},{24,16},{1,9},{9,1},{17,25},{25,17},{2,10},{10... | collective-permute-start | bytes 958472 | tf_op jit(solution)/shard_map/ppermute | solution.py:993
  51.4 7.1 %collective-permute-start.17 = (f32[104,768]{1,0:T(8,128)S(1)}, f32[104,768]{1,0:T(8,128)S(1)}, u32[]{:S(2)}, u32[]{:S(2)}) collective-permute-start(f32[104,768]{1,0:T(8,128)S(1)} %collective-permute-done.6.refs_10_), channel_id=1, source_target_pairs={{0,4},{4,0},{1,5},{5,1},{2,6},{6,2},{3,7},{7,3},{8,12},{12,8},{9,1... | collective-permute-start | bytes 958472 | tf_op jit(solution)/shard_map/ppermute | solution.py:993
  51.5 7.2 %collective-permute-start.18 = (f32[104,768]{1,0:T(8,128)S(1)}, f32[104,768]{1,0:T(8,128)S(1)}, u32[]{:S(2)}, u32[]{:S(2)}) collective-permute-start(f32[104,768]{1,0:T(8,128)S(1)} %collective-permute-done.7.refs_12_), channel_id=1, source_target_pairs={{0,4},{4,0},{1,5},{5,1},{2,6},{6,2},{3,7},{7,3},{8,12},{12,8},{9,1... | collective-permute-start | bytes 958472 | tf_op jit(solution)/shard_map/ppermute | solution.py:993
  57.2 1.6 collective-permute-start.19
  58.8 112.2 %all-gather.6.cloned.1.call-start = ((), (), s32[]{:S(2)}) async-start(), calls=%async_computation.2 | async-start | bytes 10616832 | tf_op jit(solution)/shard_map/all_gather | solution.py:1071
  62.3 6.9 %collective-permute-start.21 = (f32[104,768]{1,0:T(8,128)}, f32[104,768]{1,0:T(8,128)}, u32[]{:S(2)}, u32[]{:S(2)}) collective-permute-start(f32[104,768]{1,0:T(8,128)} %collective-permute-done.1.refs_8_), channel_id=1, source_target_pairs={{0,4},{4,0},{1,5},{5,1},{2,6},{6,2},{3,7},{7,3},{8,12},{12,8},{9,1... | collective-permute-start | bytes 958472 | tf_op jit(solution)/shard_map/ppermute | solution.py:993
  62.5 21.1 %collective-permute-start.23 = (f32[104,768]{1,0:T(8,128)}, f32[104,768]{1,0:T(8,128)S(1)}, u32[]{:S(2)}, u32[]{:S(2)}) collective-permute-start(f32[104,768]{1,0:T(8,128)} %collective-permute-done.14.refs_8_), channel_id=1, source_target_pairs={{0,16},{8,24},{16,0},{24,8},{1,17},{9,25},{17,1},{25,9},{2,18},{10... | collective-permute-start | bytes 958472 | tf_op jit(solution)/shard_map/ppermute | solution.py:993
  64.0 19.6 %collective-permute-start.22 = (f32[104,768]{1,0:T(8,128)}, f32[104,768]{1,0:T(8,128)S(1)}, u32[]{:S(2)}, u32[]{:S(2)}) collective-permute-start(f32[104,768]{1,0:T(8,128)} %collective-permute-done.14.refs_8_), channel_id=1, source_target_pairs={{0,8},{8,0},{16,24},{24,16},{1,9},{9,1},{17,25},{25,17},{2,10},{10... | collective-permute-start | bytes 958472 | tf_op jit(solution)/shard_map/ppermute | solution.py:993
  64.6 30.2 %collective-permute-start.29 = (f32[96,1536]{1,0:T(8,128)S(1)}, f32[96,1536]{1,0:T(8,128)S(1)}, u32[]{:S(2)}, u32[]{:S(2)}) collective-permute-start(f32[96,1536]{1,0:T(8,128)S(1)} %copy-done.1), channel_id=1, source_target_pairs={{0,2},{1,3},{2,0},{3,1},{4,6},{5,7},{6,4},{7,5},{8,10},{9,11},{10,... | collective-permute-start | bytes 1769480 | tf_op jit(solution)/shard_map/ppermute | solution.py:993
  68.9 25.9 %collective-permute-start.28 = (f32[96,1536]{1,0:T(8,128)S(1)}, f32[96,1536]{1,0:T(8,128)S(1)}, u32[]{:S(2)}, u32[]{:S(2)}) collective-permute-start(f32[96,1536]{1,0:T(8,128)S(1)} %copy-done.1), channel_id=1, source_target_pairs={{0,1},{1,0},{2,3},{3,2},{4,5},{5,4},{6,7},{7,6},{8,9},{9,8},{10,11... | collective-permute-start | bytes 1769480 | tf_op jit(solution)/shard_map/ppermute | solution.py:993
  69.3 14.3 %collective-permute-start.20 = (f32[104,768]{1,0:T(8,128)S(1)}, f32[104,768]{1,0:T(8,128)S(1)}, u32[]{:S(2)}, u32[]{:S(2)}) collective-permute-start(f32[104,768]{1,0:T(8,128)S(1)} %broadcast_select_fusion.1), channel_id=1, source_target_pairs={{0,16},{4,12},{8,24},{12,4},{16,0},{20,28},{24,8},{28,20},{1,17},{... | collective-permute-start | bytes 958472 | tf_op jit(solution)/shard_map/ppermute | solution.py:1001
  83.6 11.2 %collective-permute-start.30 = (f32[104,768]{1,0:T(8,128)S(1)}, f32[104,768]{1,0:T(8,128)}, u32[]{:S(2)}, u32[]{:S(2)}) collective-permute-start(f32[104,768]{1,0:T(8,128)S(1)} %broadcast_select_fusion), channel_id=1, source_target_pairs={{0,16},{4,12},{8,24},{12,4},{16,0},{20,28},{24,8},{28,20},{1,17},{... | collective-permute-start | bytes 958472 | tf_op jit(solution)/shard_map/ppermute | solution.py:1001
  96.0 119.8 %all-gather.8.cloned.1.call-start = ((), (), s32[]{:S(2)}) async-start(), calls=%async_computation.3 | async-start | bytes 5308416 | tf_op jit(solution)/shard_map/all_gather | solution.py:1071
  96.2 1.7 collective-permute-start.13
  96.3 2.1 collective-permute-start.24
  96.8 2.8 collective-permute-start.25
  96.9 5.1 %collective-permute-start.26 = (f32[104,768]{1,0:T(8,128)}, f32[104,768]{1,0:T(8,128)S(1)}, u32[]{:S(2)}, u32[]{:S(2)}) collective-permute-start(f32[104,768]{1,0:T(8,128)} %copy-done.24), channel_id=1, source_target_pairs={{0,4},{4,0},{1,5},{5,1},{2,6},{6,2},{3,7},{7,3},{8,12},{12,8},{9,1... | collective-permute-start | bytes 958472 | tf_op jit(solution)/shard_map/ppermute | solution.py:993
  97.3 5.1 %collective-permute-start.27 = (f32[104,768]{1,0:T(8,128)}, f32[104,768]{1,0:T(8,128)S(1)}, u32[]{:S(2)}, u32[]{:S(2)}) collective-permute-start(f32[104,768]{1,0:T(8,128)} %collective-permute-done.14.refs_8_), channel_id=1, source_target_pairs={{0,4},{4,0},{1,5},{5,1},{2,6},{6,2},{3,7},{7,3},{8,12},{12,8},{9,1... | collective-permute-start | bytes 958472 | tf_op jit(solution)/shard_map/ppermute | solution.py:993
  97.9 4.5 %collective-permute-start.32 = (f32[104,768]{1,0:T(8,128)S(1)}, f32[104,768]{1,0:T(8,128)S(1)}, u32[]{:S(2)}, u32[]{:S(2)}) collective-permute-start(f32[104,768]{1,0:T(8,128)S(1)} %collective-permute-done.22.refs_10_), channel_id=1, source_target_pairs={{0,4},{4,0},{1,5},{5,1},{2,6},{6,2},{3,7},{7,3},{8,12},{12,8},{9,1... | collective-permute-start | bytes 958472 | tf_op jit(solution)/shard_map/ppermute | solution.py:993
  98.4 4.1 %collective-permute-start.33 = (f32[104,768]{1,0:T(8,128)S(1)}, f32[104,768]{1,0:T(8,128)S(1)}, u32[]{:S(2)}, u32[]{:S(2)}) collective-permute-start(f32[104,768]{1,0:T(8,128)S(1)} %collective-permute-done.23.refs_12_), channel_id=1, source_target_pairs={{0,4},{4,0},{1,5},{5,1},{2,6},{6,2},{3,7},{7,3},{8,12},{12,8},{9,1... | collective-permute-start | bytes 958472 | tf_op jit(solution)/shard_map/ppermute | solution.py:993
  100.3 3.0 collective-permute-start.34
  102.1 34.1 %collective-permute-start.35 = (f32[512,768]{1,0:T(8,128)S(1)}, f32[512,768]{1,0:T(8,128)}, u32[]{:S(2)}, u32[]{:S(2)}) collective-permute-start(f32[512,768]{1,0:T(8,128)S(1)} %dynamic-slice_bitcast_fusion.2), channel_id=1, source_target_pairs={{0,4},{4,0},{1,5},{5,1},{2,6},{6,2},{3,7},{7,3},{8,12},{12,8},{9,1... | collective-permute-start | bytes 4718600 | tf_op jit(solution)/shard_map/ppermute | solution.py:993
  136.2 33.4 %collective-permute-start.36 = (f32[96,1536]{1,0:T(8,128)S(1)}, f32[96,1536]{1,0:T(8,128)S(1)}, u32[]{:S(2)}, u32[]{:S(2)}) collective-permute-start(f32[96,1536]{1,0:T(8,128)S(1)} %copy-done.1), channel_id=1, source_target_pairs={{0,3},{1,2},{2,1},{3,0},{4,7},{5,6},{6,5},{7,4},{8,11},{9,10},{10,... | collective-permute-start | bytes 1769480 | tf_op jit(solution)/shard_map/ppermute | solution.py:993
  170.4 141.5 %reduce-scatter.2.cloned.1.call-start = ((), (), s32[]{:S(2)}) async-start(), calls=%async_computation.4 | async-start | bytes 5308416 | tf_op jit(solution)/shard_map/reduce_scatter | solution.py:1142
  297.1 4.2 %collective-permute-start.38 = (f32[1,4,96,768]{3,2,1,0:T(8,128)}, f32[1,4,96,768]{3,2,1,0:T(8,128)}, u32[]{:S(2)}, u32[]{:S(2)}) collective-permute-start(f32[1,4,96,768]{3,2,1,0:T(8,128)} %get-tuple-element.155), channel_id=1, source_target_pairs={{0,4},{4,0},{1,5},{5,1},{2,6},{6,2},{3,7},{7,3},{8,12},{12,8},{9,1... | collective-permute-start | bytes 3538952 | tf_op jit(solution)/shard_map/ppermute | solution.py:993
  299.0 10.3 %collective-permute-start.41 = (f32[512,768]{1,0:T(8,128)S(1)}, f32[512,768]{1,0:T(8,128)}, u32[]{:S(2)}, u32[]{:S(2)}) collective-permute-start(f32[512,768]{1,0:T(8,128)S(1)} %dynamic-slice_bitcast_fusion), channel_id=1, source_target_pairs={{0,4},{4,0},{1,5},{5,1},{2,6},{6,2},{3,7},{7,3},{8,12},{12,8},{9,1... | collective-permute-start | bytes 4718600 | tf_op jit(solution)/shard_map/ppermute | solution.py:993
  299.6 21.6 %collective-permute-start.37 = (f32[512,768]{1,0:T(8,128)S(1)}, f32[512,768]{1,0:T(8,128)}, u32[]{:S(2)}, u32[]{:S(2)}) collective-permute-start(f32[512,768]{1,0:T(8,128)S(1)} %dynamic-slice_bitcast_fusion.1), channel_id=1, source_target_pairs={{0,4},{4,0},{1,5},{5,1},{2,6},{6,2},{3,7},{7,3},{8,12},{12,8},{9,1... | collective-permute-start | bytes 4718600 | tf_op jit(solution)/shard_map/ppermute | solution.py:993
  300.9 3.2 collective-permute-start.40
  302.4 6.8 %collective-permute-start.39 = (f32[1,96,768]{2,1,0:T(8,128)S(1)}, f32[1,96,768]{2,1,0:T(8,128)S(1)}, u32[]{:S(2)}, u32[]{:S(2)}) collective-permute-start(f32[1,96,768]{2,1,0:T(8,128)S(1)} %fusion), channel_id=1, source_target_pairs={{0,16},{4,12},{8,24},{12,4},{16,0},{20,28},{24,8},{28,20},{1,17},{... | collective-permute-start | bytes 884744 | tf_op jit(solution)/shard_map/ppermute | solution.py:1001
  309.9 3.9 %collective-permute-start.42 = (f32[8,288]{1,0:T(8,128)S(1)}, f32[8,288]{1,0:T(8,128)S(1)}, u32[]{:S(2)}, u32[]{:S(2)}) collective-permute-start(f32[8,288]{1,0:T(8,128)S(1)} %fusion.3), channel_id=1, source_target_pairs={{0,8},{8,0},{16,24},{24,16},{1,9},{9,1},{17,25},{25,17},{2,10},{10... | collective-permute-start | bytes 27656 | tf_op jit(solution)/shard_map/ppermute | solution.py:993
  313.9 9.7 %collective-permute-start.43 = (f32[8,288]{1,0:T(8,128)S(1)}, f32[8,288]{1,0:T(8,128)S(1)}, u32[]{:S(2)}, u32[]{:S(2)}) collective-permute-start(f32[8,288]{1,0:T(8,128)S(1)} %add.111), channel_id=1, source_target_pairs={{0,16},{8,24},{16,0},{24,8},{1,17},{9,25},{17,1},{25,9},{2,18},{10... | collective-permute-start | bytes 27656 | tf_op jit(solution)/shard_map/ppermute | solution.py:993
  316.4 8.5 %collective-permute-start.44 = (f32[1,96,768]{2,1,0:T(8,128)S(1)}, f32[1,96,768]{2,1,0:T(8,128)S(1)}, u32[]{:S(2)}, u32[]{:S(2)}) collective-permute-start(f32[1,96,768]{2,1,0:T(8,128)S(1)} %get-tuple-element.211), channel_id=1, source_target_pairs={{0,8},{8,0},{16,24},{24,16},{1,9},{9,1},{17,25},{25,17},{2,10},{10... | collective-permute-start | bytes 884744 | tf_op jit(solution)/shard_map/ppermute | solution.py:993
  317.9 6.9 %collective-permute-start.45 = (f32[1,96,768]{2,1,0:T(8,128)S(1)}, f32[1,96,768]{2,1,0:T(8,128)S(1)}, u32[]{:S(2)}, u32[]{:S(2)}) collective-permute-start(f32[1,96,768]{2,1,0:T(8,128)S(1)} %get-tuple-element.212), channel_id=1, source_target_pairs={{0,16},{8,24},{16,0},{24,8},{1,17},{9,25},{17,1},{25,9},{2,18},{10... | collective-permute-start | bytes 884744 | tf_op jit(solution)/shard_map/ppermute | solution.py:993
  (39 other events, 371.7 us)
Sparse Core Ops, SparseCore 0:
  59.0 47.0 all-gather.3
  107.9 59.7 all-gather.5
  170.6 39.3 all-gather.7
  213.3 53.8 reduce-scatter.1

commit v4 on v3

--- a/solution.py
+++ b/solution.py
@@ -437,15 +437,12 @@
     def mine(i, m):
         return (m[0] & 1, order(i, m) % 2, 0)
 
-    def came(i, m):
-        return (order(i, m) % 2, 0)
-
-    return [pl.BlockSpec((1, TILE, model), mine), pl.BlockSpec((TILE, model), came)]
+    return [pl.BlockSpec((1, TILE, model), mine)] * 2
 
 
 def sequence_tile(tile, me_ref, mine_ref, came_ref):
     own = tile // 2 == (me_ref[0] & 1)
-    return jnp.where(own, mine_ref[0], came_ref[...])
+    return jnp.where(own, mine_ref[0], came_ref[0])
 
 
 def project_kernel(me_ref, x_ref, xr_ref, *refs):
@@ -696,9 +693,9 @@
     ah_ref, al_ref, bh_ref, bl_ref, qah_ref, qal_ref, qbh_ref, qbl_ref, *refs,
 ):
     (
-        ig_ref, gg_ref, g2_ref, dkern_ref, keep_ref, send_ref,
+        theirs_ref, ig_ref, keep_ref, send_ref, gg, g2, dkern,
         grad, head, grow, shrink, dec, end, full, du_all, da, db, wg,
-    ) = refs[-17:]
+    ) = refs[-18:]
     size, lanes = grow.shape[0], dec.shape[0]
     step, steps = pl.program_id(0), pl.num_programs(0)
     projs = (pa_ref, pb_ref)
@@ -707,9 +704,9 @@
     def _():
         grad[...] = jnp.zeros_like(grad)
         head[...] = jnp.zeros_like(head)
-        dkern_ref[...] = jnp.zeros_like(dkern_ref)
-        gg_ref[...] = jnp.zeros_like(gg_ref)
-        g2_ref[...] = jnp.zeros_like(g2_ref)
+        dkern[...] = jnp.zeros_like(dkern)
+        gg[...] = jnp.zeros_like(gg)
+        g2[...] = jnp.zeros_like(g2)
         wg[...] = jnp.zeros_like(wg)
         fill_tables(pair(sa_ref, sb_ref)[2 + taps : 3 + taps], grow, shrink, dec, end, full)
 
@@ -717,7 +714,7 @@
     tile = steps - 1 - step
     back, gain_grad, _ = norm_back(resid_ref[...], gains_ref[1:2, :], fng_ref[...])
     rg = sequence_tile(tile, me_ref, ct_ref, cr_ref) + back
-    g2_ref[...] += gain_grad
+    g2[...] += gain_grad
     r2 = split(rg)
     du_all[:, :third] = d3(r2, (ah_ref[...], al_ref[...]), NN)
     du_all[:, third:] = d3(r2, (bh_ref[...], bl_ref[...]), NN)
@@ -781,7 +778,7 @@
             to[here, third + at : third + at + lanes] = total
             if g < 2:
                 for j in range(taps):
-                    dkern_ref[j : j + 1, s] += jnp.sum(
+                    dkern[j : j + 1, s] += jnp.sum(
                         dshift * moved[j][:, s], axis=0, keepdims=True
                     )
 
@@ -792,7 +789,7 @@
     incoming = incoming + d3(right, (qbh_ref[...], qbl_ref[...]), NT)
     back, gain_grad, xhat = norm_back(x, gains_ref[0:1, :], incoming)
     ig_ref[0] = rg + back
-    gg_ref[...] += gain_grad
+    gg[...] += gain_grad
     n = split(xhat * gains_ref[0:1, :])
     joint = tuple(
         jnp.concatenate([p[:, i * third : i * third + own] for i in range(3)], axis=1) for p in left
@@ -800,9 +797,14 @@
     wg[:, : 3 * own] += d3(n, joint, TN)
     wg[:, 3 * own :] += d3(r2, split(mixed_ref[:, :own]), TN)
 
+    @pl.when(tile // 2 != (me_ref[0] & 1))
+    def _():
+        theirs_ref[...] = ig_ref[0]
+
     @pl.when(step == steps - 1)
     def _():
-        store_blocks(me_ref[0], wg, keep_ref, send_ref, 0)
+        few = (gg[...], g2[...], dkern[:, :own])
+        store_blocks(me_ref[0], wg, few, keep_ref, send_ref)
 
 
 def run_mixer_back(
@@ -813,7 +815,7 @@
     own = third // 2
     chunks = TILE // BLOCK
     last = tokens // TILE - 1
-    blocks = (1, 4, model // 8, 4 * own)
+    blocks = (1, 4, model // 8 + 8, 4 * own)
 
     def prior(c):
         return jnp.maximum((last - c) * (TILE // 8) - 1, 0)
@@ -823,6 +825,12 @@
     before = pl.BlockSpec((8, third), lambda c, m: (prior(c), 1))
     state = pl.BlockSpec((chunks, LANES, third), lambda c, m: (last - c, 0, 0))
     halves = pl.BlockSpec((1, TILE, model), lambda c, m: ((last - c) // 2, (last - c) % 2, 0))
+
+    def for_other(c, m):
+        core, tile = m[0] & 1, last - c
+        return (jnp.where(tile // 2 == 1 - core, tile % 2, core), 0)
+
+    theirs = pl.BlockSpec((TILE, model), for_other)
     return pl.pallas_call(
         partial(mixer_back_kernel, taps),
         grid_spec=pltpu.PrefetchScalarGridSpec(
@@ -842,9 +850,11 @@
             ]
             + [whole(a[0].shape)] * 4
             + [whole(qa[0].shape)] * 4,
-            out_specs=[halves, whole((1, model)), whole((1, model)), whole((taps, model))]
-            + [whole(blocks), whole(blocks)],
+            out_specs=[theirs, halves, whole(blocks), whole(blocks)],
             scratch_shapes=[
+                pltpu.VMEM((1, model), f32),
+                pltpu.VMEM((1, model), f32),
+                pltpu.VMEM((taps, model), f32),
                 pltpu.VMEM((LANES, model), f32),
                 pltpu.VMEM((taps - 1, 8, model), f32),
             ]
@@ -853,8 +863,8 @@
             + [pltpu.VMEM((TILE, 3 * third), f32)] * 2
             + [pltpu.VMEM((model, 4 * own), f32)],
         ),
-        out_shape=[shaped((2, tokens // 2, model)), shaped((1, model)), shaped((1, model))]
-        + [shaped((taps, model)), shaped(blocks), shaped(blocks)],
+        out_shape=[shaped((tokens // 2, model)), shaped((2, tokens // 2, model))]
+        + [shaped(blocks), shaped(blocks)],
         compiler_params=params(),
         cost_estimate=cost(1e11, 60 * 2**20),
         name="mixer_back",
@@ -872,48 +882,66 @@
     return act, back * slope
 
 
-def store_blocks(me, g, keep_ref, send_ref, i):
+def store_blocks(me, g, few, keep_ref, send_ref):
     rows = g.shape[0] // 8
     for b in range(8):
         r = me ^ b
-        part = g[b * rows : (b + 1) * rows]
         where = r // 2
+        short = [f[:, b * (f.shape[1] // 8) : (b + 1) * (f.shape[1] // 8)] for f in few]
+
+        def put(ref):
+            ref[0, where, 0:rows, :] = g[b * rows : (b + 1) * rows]
+            ref[0, where, rows:, :] = jnp.zeros((ref.shape[2] - rows, ref.shape[3]), f32)
+            at = rows
+            for part in short:
+                ref[0, where, at : at + part.shape[0], 0 : part.shape[1]] = part
+                at = at + part.shape[0]
 
         @pl.when((r & 1) == 0)
         def _():
-            keep_ref[i, where] = part
+            put(keep_ref)
 
         @pl.when((r & 1) == 1)
         def _():
-            send_ref[i, where] = part
-
-
-def feed_kernel(own, final, me_ref, nh_ref, nl_ref, ct_ref, cr_ref, out_in, fng_in, w_in, *refs):
+            put(send_ref)
+
+
+def feed_kernel(own, slots, final, me_ref, nh_ref, nl_ref, ct_ref, cr_ref, out_in, fng_in, w_in, *refs):
     if own:
         out_ref, fng_ref, wg, w = refs[-4:]
     else:
         out_ref, fng_ref, w = refs[-3:]
     step = pl.program_id(0)
-    hidden = w.shape[2] // 2
+    hidden = w.shape[2] // (2 * slots)
 
     @pl.when(step == 0)
     def _():
-        w[0], w[1] = split(w_in[...].reshape(w.shape[1:]))
+        w[0], w[1] = split(w_in[...])
         if own:
             wg[...] = jnp.zeros_like(wg)
 
     tile = theirs_first(step, me_ref)
     n = (nh_ref[...], nl_ref[...])
     ct = split(sequence_tile(tile, me_ref, ct_ref, cr_ref))
-    u, d = (w[0, :, :hidden], w[1, :, :hidden]), (w[0, :, hidden:], w[1, :, hidden:])
-    act, grad = gelu_parts(d3(n, u, NN), d3(ct, d, NN))
-    act, grad = split(act), split(grad)
-    out_ref[...] = (out_in[...] + d3(act, d, NT)).reshape(out_ref.shape)
-    more = d3(grad, u, NT)
-    fng_ref[...] = more if own else fng_in[...] + more
+    out, fng = out_in[...], None if own else fng_in[...]
+    for t in range(slots):
+        a, b = (slice((2 * t + i) * hidden, (2 * t + i + 1) * hidden) for i in range(2))
+        u, d = (w[0, :, a], w[1, :, a]), (w[0, :, b], w[1, :, b])
+        act, grad = gelu_parts(d3(n, u, NN), d3(ct, d, NN))
+        act, grad = split(act), split(grad)
+        out = out + d3(act, d, NT)
+        more = d3(grad, u, NT)
+        fng = more if fng is None else fng + more
+    out_ref[...] = out.reshape(out_ref.shape)
+    fng_ref[...] = fng
     if own:
         wg[:, :hidden] += d3(n, grad, TN)
         wg[:, hidden:] += d3(ct, act, TN)
+    if final:
+
+        @pl.when(step < 2)
+        def _():
+            refs[0][...] = out_ref[0]
 
 
 def theirs_first(step, me):
@@ -921,35 +949,34 @@
     return jnp.where(step < 2, 1 - core, core) * 2 + (step & 1)
 
 
-def run_feed(me, n, ct, out, fng, w, slot, slots, own, final=False, ties=()):
+def run_feed(me, n, ct, out, fng, w, slots, own, final=False):
     tokens, model = n[0].shape
-    wide = w.shape[1] // slots
-    part = pl.BlockSpec(
-        (model, wide), lambda *_: (0, slot), pipeline_mode=pl.Buffered(buffer_count=1)
-    )
+    wide = w.shape[1]
     row = pl.BlockSpec((TILE, model), lambda i, m: (theirs_first(i, m), 0))
-    tie_specs, tie_args = tied(ties)
     full = shaped((tokens, model))
     last = pl.BlockSpec((1, TILE, model), lambda i, m: (theirs_first(i, m) // 2, i % 2, 0))
+    theirs = pl.BlockSpec((TILE, model), lambda i, m: (jnp.minimum(i, 1), 0))
     return pl.pallas_call(
-        partial(feed_kernel, own, final),
+        partial(feed_kernel, own, slots, final),
         grid_spec=pltpu.PrefetchScalarGridSpec(
             num_scalar_prefetch=1,
             grid=(tokens // TILE,),
             in_specs=[row] * 2
             + sequence_specs(model, theirs_first)
             + [row] * 2
-            + [part]
-            + tie_specs,
-            out_specs=[last if final else row, row] + ([whole((model, wide))] if own else []),
+            + [whole(w.shape)],
+            out_specs=[theirs] * final
+            + [last if final else row, row]
+            + ([whole((model, wide))] if own else []),
             scratch_shapes=[pltpu.VMEM((2, model, wide), bf16)],
         ),
-        out_shape=[shaped((2, tokens // 2, model)) if final else full, full]
+        out_shape=[shaped((tokens // 2, model))] * final
+        + [shaped((2, tokens // 2, model)) if final else full, full]
         + ([shaped((model, wide))] if own else []),
         compiler_params=params(),
         cost_estimate=cost((6 if own else 4) * 3 * tokens * model * wide, 30 * 2**20),
         name="feed_own" if own else "feed",
-    )(me, *n, *ct, out, fng, w, *tie_args)
+    )(me, *n, *ct, out, fng, w)
 
 
 def norm_back(v, gain, incoming):
@@ -1043,15 +1070,10 @@
     return own + exchange(to_x, "dp", 1) + exchange(to_y, "dp", 2)
 
 
-def other_half(block):
-    theirs = lax.dynamic_index_in_dim(block, 1 - lax.axis_index("ctx"), 0, keepdims=False)
-    return exchange(theirs, "ctx", 1)
-
-
 def swap_in(block):
     me = lax.axis_index("ctx")
     mine = lax.dynamic_index_in_dim(block, me, 0, keepdims=False)
-    came = other_half(block)
+    came = lax.dynamic_index_in_dim(exchange(block, "ctx", 1), me, 0, keepdims=False)
     return jnp.where(
         me == 0, jnp.concatenate([mine, came], axis=0), jnp.concatenate([came, mine], axis=0)
     )
@@ -1077,7 +1099,8 @@
     a1 = exchange(a0, "tensor", 1)
     near0 = sides(a0)
     f0 = run_pack_feed(*after((up_weight, down_weight), a0))
-    x_came = other_half(after((layer_input,), a0)[0])
+    x_came = exchange(after((layer_input,), a0)[0], "ctx", 1)
+    seg = swap_in(segment_ids).astype(f32)
 
     b0, b1, near0 = after((a0, a1, near0), f0)
     a2 = exchange(b0, "tensor", 2)
@@ -1087,7 +1110,7 @@
     other0 = across_cores(*inner[:2], far0)
     other1 = exchange(inner[2], "ctx", 1)
 
-    b0, b2, near1 = after((a0, a2, near1), far0, other0, x_came)
+    b0, b2, near1, seg = after((a0, a2, near1, seg), far0, other0, x_came)
     a3 = exchange(b0, "tensor", 3)
     far1 = far(*near1)
     near2 = exchange(b2, "dp", 1), exchange(b2, "dp", 2)
@@ -1095,7 +1118,6 @@
     near1 = (*near1, other1)
     other1 = across_cores(*inner[:2], far1)
     other2 = exchange(inner[2], "ctx", 1)
-    seg = swap_in(segment_ids).astype(f32)
 
     g0, b3, near2 = after((f0, a3, near2), far1, other1)
     w0 = gathered(g0)
@@ -1114,7 +1136,7 @@
 
     near3, late = after((near3, cotangent), far2, proj_a)
     far3 = far(*near3)
-    ct = (cotangent, other_half(late))
+    ct = (cotangent, exchange(late, "ctx", 1))
     segrow = jnp.tile(seg.reshape(-1, 1, BLOCK), (1, 1, PAIR))
     seg = seg[:, None]
     states_a, mixed_a = run_mixer(me, proj_a, seg, segrow, wa[5], taps)
@@ -1133,15 +1155,14 @@
     more = (x, mixed_a, gains, wa[2:4], wb[2:4])
     states_b, resid, nh, nl = run_mixer(me, proj_b, seg, segrow, wb[5], taps, more)
     n = (nh, nl)
-    out, fng, feed_g = run_feed(me, n, ct, resid, resid, w0, 0, 1, True)
+    out, fng, feed_g = run_feed(me, n, ct, resid, resid, w0, 1, True)
     (f3,) = after((f3,), fng)
     w3 = gathered(f3)
-    out, fng = run_feed(me, n, ct, out, fng, w12, 0, 2, False)
-    out, fng = run_feed(me, n, ct, out, fng, w12, 1, 2, False)
-    out_halves, fng = run_feed(me, n, ct, out, fng, w3, 0, 1, False, True)
+    out, fng = run_feed(me, n, ct, out, fng, w12, 2, False)
+    theirs, out_halves, fng = run_feed(me, n, ct, out, fng, w3, 1, False, True)
     feed_g = lax.psum_scatter(feed_g, plane, scatter_dimension=0, tiled=True)
-    came = other_half(out_halves)
-    halves, mixer_gain_g, feed_gain_g, kern_g, keep, send = run_mixer_back(
+    came = exchange(theirs, "ctx", 1)
+    theirs, halves, keep, send = run_mixer_back(
         me, fng, resid, x, ct, projs, (states_a, states_b), mixed_a, seg, segrow, smalls, gains,
         wa[2:4], wb[2:4], wa[:2], wb[:2], taps,
     )
@@ -1150,32 +1171,26 @@
     came_send = exchange(send, "ctx", 1)
     diagonal = keep[:, 3] + came_send[:, 3]
     keep, came_send = after((keep, came_send), diagonal)
-    kern_g = kern_g[:, :own].reshape(taps, 8, few).transpose(1, 0, 2).reshape(8, taps * few)
-    gains_g = [g.reshape(8, rows) for g in (mixer_gain_g, feed_gain_g)]
-    tiny = jnp.concatenate(gains_g + [kern_g], axis=1)
     diagonal = corner(diagonal)
-    tiny = tiny + exchange(tiny, "ctx", 1)
-    came = other_half(halves)
+    came = exchange(theirs, "ctx", 1)
     to_own, to_x, to_y = (keep[:, i] + came_send[:, i] for i in range(3))
-    diagonal, to_own, to_x, to_y, tiny, came = after((diagonal, to_own, to_x, to_y, tiny, came))
+    diagonal, to_own, to_x, to_y, came = after((diagonal, to_own, to_x, to_y, came))
     came_x = exchange(jnp.where(core == 0, to_x + diagonal, to_x), "dp", 1)
     came_y = exchange(jnp.where(core == 0, to_y, to_y + diagonal), "dp", 2)
-    tiny = tiny + exchange(tiny, "dp", 1)
     input_grad = run_leave(me, halves, came)
-    tiny = tiny + exchange(tiny, "dp", 2)
     mixer_g = (to_own + came_x + came_y)[0]
-    tiny = lax.dynamic_index_in_dim(tiny, position, 0, keepdims=False)
+    few_g, mixer_g = mixer_g[rows:], mixer_g[:rows]
     hidden = up_weight.shape[1]
     return (
         layer_output,
         input_grad,
-        tiny[:rows],
+        few_g[0, :rows],
         mixer_g[:, :own],
         mixer_g[:, own : 2 * own],
         mixer_g[:, 2 * own : 3 * own],
-        tiny[2 * rows :].reshape(taps, few),
+        few_g[2 : 2 + taps, :few],
         mixer_g[:, 3 * own :].T,
-        tiny[rows : 2 * rows],
+        few_g[1, :rows],
         feed_g[:, :hidden],
         feed_g[:, hidden:].T,
     )

time: 340 us -> 333 us (0.979)
  waiting for transfers between devices: 31.7 us -> 39.6 us
  local copies, waits for them, and re-layouts: 19.1 us -> 13.8 us
  starting transfers between devices: 43 us -> 38.4 us
  Pallas kernels: 218 us -> 214 us
    ppermute x41 -> x38, waiting for transfers between devices: 23.5 us -> 29.1 us  [exchange(): return lax.ppermute(value, axis, [(i, i ^ flip) for i in range(count)])]
    pallas_call x4 -> x3, Pallas kernels: 97.6 us -> 92.9 us  [run_feed(): pl.pallas_call(partial(feed_kernel, own, slots, final), grid_spec=pltpu.P...]
    ppermute x41 -> x38, starting transfers between devices: 37.7 us -> 33.1 us  [exchange(): return lax.ppermute(value, axis, [(i, i ^ flip) for i in range(count)])]
    squeeze x4 -> x1, local copies, waits for them, and re-layouts: 4.9 us -> 0.52 us  [by_sequence(): few_g[1, :rows]]
    unnamed x75 -> x73, local copies, waits for them, and re-layouts: 7.23 us -> 6.42 us
  transfers between devices with their start and end apart: 50 -> 47, of which waited for: 17 -> 20; matrix products, arithmetic and copies ran while one was open for 5% -> 3% of each run, Pallas kernels for 65% -> 65%
where the time goes in v4:
time: 333 us; the launch traced here: 326 us
  Pallas kernels  214 us (64%)
  waiting for transfers between devices  39.6 us (12%)
  starting transfers between devices  38.4 us (12%)
  between operations  14.3 us (4%)
  local copies, waits for them, and re-layouts  13.8 us (4%)
  other arithmetic  6.34 us (2%)
    pallas_call x3, Pallas kernels, run_feed(): pl.pallas_call(partial(feed_kernel, own, slots, final), grid_spec=pltpu.P...  92.9 us
    pallas_call x1, Pallas kernels, run_mixer_back(): pl.pallas_call(partial(mixer_back_kernel, taps), grid_spec=pltpu.Prefetch...  60 us
    ppermute x38, starting transfers between devices, exchange(): return lax.ppermute(value, axis, [(i, i ^ flip) for i in range(count)])  33.1 us
    ppermute x38, waiting for transfers between devices, exchange(): return lax.ppermute(value, axis, [(i, i ^ flip) for i in range(count)])  29.1 us
    pallas_call x2, Pallas kernels, run_mixer(): pl.pallas_call(partial(mixer_kernel, taps, bool(more)), grid_spec=pltpu.P...  26.7 us
    pallas_call x2, Pallas kernels, run_project(): pl.pallas_call(project_kernel, grid_spec=pltpu.PrefetchScalarGridSpec(num...  25.7 us
    ppermute x5, waiting for transfers between devices, corner(): return lax.ppermute(value, ('dp', 'ctx'), pairs)  9.96 us
  transfers between devices with their start and end apart: 47, of which 20 were waited for; matrix products, arithmetic and copies ran while one was open for 3% of the time, Pallas kernels for 65%

profile of v4, /device:TPU:0, one launch (start us, length us, event | category | flops | bytes accessed | tf_op | source)
XLA Modules:
  0.0 326.5 jit_solution(5311533381368767309)
XLA Ops:
  7.2 2.1 pack_mixer.1.refs_0_
  9.8 2.9 collective-permute-start.3
  12.8 1.5 collective-permute-start.2
  14.3 1.6 collective-permute-start.1
  15.9 1.9 copy.28.down_ref
  17.7 2.1 pack_feed.1
  19.8 0.9 collective-permute-done.3.refs_4_
  20.7 1.5 collective-permute-done.2.refs_2_
  22.2 1.2 collective-permute-done.1.refs_8_
  24.0 2.6 collective-permute-start.5
  26.6 1.6 collective-permute-start.7
  28.2 5.6 %collective-permute-done.9.refs_6_ = f32[104,768]{1,0:T(8,128)} collective-permute-done((f32[104,768]{1,0:T(8,128)S(1)}, f32[104,768]{1,0:T(8,128)}, u32[]{:S(2)}, u32[]{:S(2)}) %collective-permute-start.9) | collective-permute-done | bytes 319520 | tf_op jit(solution)/shard_map/ppermute | solution.py:1028
  33.8 5.8 %collective-permute-done.5.refs_0_ = f32[104,768]{1,0:T(8,128)S(1)} collective-permute-done((f32[104,768]{1,0:T(8,128)S(1)}, f32[104,768]{1,0:T(8,128)S(1)}, u32[]{:S(2)}, u32[]{:S(2)}) %collective-permute-start.5) | collective-permute-done | bytes 319520 | tf_op jit(solution)/shard_map/ppermute | solution.py:1020
  43.5 3.5 %collective-permute-start.15 = (f32[104,768]{1,0:T(8,128)S(1)}, f32[104,768]{1,0:T(8,128)S(1)}, u32[]{:S(2)}, u32[]{:S(2)}) collective-permute-start(f32[104,768]{1,0:T(8,128)S(1)} %copy-done.5), channel_id=1, source_target_pairs={{0,3},{1,2},{2,1},{3,0},{4,7},{5,6},{6,5},{7,4},{8,11},{9,10},{10,... | collective-permute-start | bytes 958472 | tf_op jit(solution)/shard_map/ppermute | solution.py:1020
  47.0 1.4 collective-permute-start.17
  48.4 1.4 collective-permute-start.16
  50.4 5.1 %collective-permute-done.15.refs_8_ = f32[104,768]{1,0:T(8,128)S(1)} collective-permute-done((f32[104,768]{1,0:T(8,128)S(1)}, f32[104,768]{1,0:T(8,128)S(1)}, u32[]{:S(2)}, u32[]{:S(2)}) %collective-permute-start.15) | collective-permute-done | bytes 319520 | tf_op jit(solution)/shard_map/ppermute | solution.py:1020
  55.5 1.5 collective-permute-done.17.refs_4_
  58.8 1.0 copy.29.seg_ref.segb_ref
  59.8 1.6 collective-permute-start.24
  62.0 3.4 %collective-permute-start.30 = (f32[96,1536]{1,0:T(8,128)S(1)}, f32[96,1536]{1,0:T(8,128)S(1)}, u32[]{:S(2)}, u32[]{:S(2)}) collective-permute-start(f32[96,1536]{1,0:T(8,128)S(1)} %copy-done), channel_id=1, source_target_pairs={{0,2},{1,3},{2,0},{3,1},{4,6},{5,7},{6,4},{7,5},{8,10},{9,11},{10,... | collective-permute-start | bytes 1769480 | tf_op jit(solution)/shard_map/ppermute | solution.py:1020
  66.6 1.5 collective-permute-start.21
  68.1 12.8 %project.2 = (f32[1024,1152]{1,0:T(8,128)}, bf16[768,1152]{1,0:T(8,128)(2,1)}, bf16[768,1152]{1,0:T(8,128)(2,1)}, bf16[768,384]{1,0:T(8,128)(2,1)}, bf16[768,384...) custom-call(s32[1]{0:T(128)} %bitcast.me_ref, f32[2,512,768]{2,1,0:T(8,128)} %x_ref.5, ...), custom_call_target="tpu_custom_call" | custom-call | flops 5435817984 | bytes 20971520 | tf_op jit(solution)/shard_map/project/pallas_call | solution.py:493
  83.0 8.4 %mixer.1 = (f32[8,128,384]{2,1,0:T(8,128)}, f32[1024,384]{1,0:T(8,128)}) custom-call(s32[1]{0:T(128)} %bitcast.me_ref, f32[1024,1152]{1,0:T(8,128)} %get-tuple-element.108.proj_ref.pa_ref.ba_ref, f32[1024,1]{1,0:T(8,128)} %copy.29.seg_ref.segb_ref, f32[8,1,256]{2,1,0:T(1,128)} %bitcast.32, f32[8,384]{1,0:T(8,128)} %get-tuple-element.117.small_ref.sa_ref), custom_call_target="tpu_custom_call" | custom-call | flops 6000000000 | bytes 10485760 | tf_op jit(solution)/shard_map/mixer/pallas_call | solution.py:661
  92.2 1.1 pad_maximum_fusion
  94.8 3.3 %collective-permute-done.14.refs_1_ = f32[104,768]{1,0:T(8,128)S(1)} collective-permute-done((f32[104,768]{1,0:T(8,128)S(1)}, f32[104,768]{1,0:T(8,128)S(1)}, u32[]{:S(2)}, u32[]{:S(2)}) %collective-permute-start.14) | collective-permute-done | bytes 319520 | tf_op jit(solution)/shard_map/ppermute | solution.py:1020
  100.5 1.4 collective-permute-done.28.refs_9_
  102.7 1.7 collective-permute-done.34.refs_15_
  104.5 12.9 %project.3 = (f32[1024,1152]{1,0:T(8,128)}, bf16[768,1152]{1,0:T(8,128)(2,1)}, bf16[768,1152]{1,0:T(8,128)(2,1)}, bf16[768,384]{1,0:T(8,128)(2,1)}, bf16[768,384...) custom-call(s32[1]{0:T(128)} %bitcast.me_ref, f32[2,512,768]{2,1,0:T(8,128)} %x_ref.5, ...), custom_call_target="tpu_custom_call" | custom-call | flops 5435817984 | bytes 20971520 | tf_op jit(solution)/shard_map/project/pallas_call | solution.py:493
  117.4 18.2 %mixer_out.1 = (f32[8,128,384]{2,1,0:T(8,128)}, f32[1024,768]{1,0:T(8,128)}, bf16[1024,768]{1,0:T(8,128)(2,1)}, bf16[1024,768]{1,0:T(8,128)(2,1)}) custom-call(s32[1]{0:T(128)} %bitcast.me_ref, f32[1024,1152]{1,0:T(8,128)} %get-tuple-element.122.proj_ref.pb_ref.bb_ref, f32[1024,1]{1,0:T(8,128)} %copy.29.seg_ref.segb_ref, f32[8,1,256]{2,1,0:T(1,128)} %bitcast.33, ...), custom_call_target="tpu_custom_call" | custom-call | flops 12999999488 | bytes 10485760 | tf_op jit(solution)/shard_map/mixer_out/pallas_call | solution.py:661
  135.6 3.2 collective-permute-start.36
  138.8 30.4 %feed_own.1 = (f32[1024,768]{1,0:T(8,128)}, f32[1024,768]{1,0:T(8,128)}, f32[768,1536]{1,0:T(8,128)}) custom-call(s32[1]{0:T(128)} %bitcast.me_ref, bf16[1024,768]{1,0:T(8,128)(2,1)} %get-tuple-element.129.nh_ref, bf16[1024,768]{1,0:T(8,128)(2,1)} %get-tuple-element.130.nl_ref, f32[2,512,768]{2,1,0:T(8,128)} %ct_ref.7, ...), custom_call_target="tpu_custom_call" | custom-call | flops 21743271936 | bytes 31457280 | tf_op jit(solution)/shard_map/feed_own/pallas_call | solution.py:959
  170.6 39.9 %feed.2 = (f32[1024,768]{1,0:T(8,128)}, f32[1024,768]{1,0:T(8,128)}) custom-call(s32[1]{0:T(128)} %bitcast.me_ref, bf16[1024,768]{1,0:T(8,128)(2,1)} %get-tuple-element.129.nh_ref, bf16[1024,768]{1,0:T(8,128)(2,1)} %get-tuple-element.130.nl_ref, f32[2,512,768]{2,1,0:T(8,128)} %ct_ref.7, f32[2,512,768]{2,1,0:T(8,128)} %collective-permute-done.35.cr_ref, ...), custom_call_target="tpu_custom_call" | custom-call | flops 28991029248 | bytes 31457280 | tf_op jit(solution)/shard_map/feed/pallas_call | solution.py:959
  210.5 22.6 %feed.3 = (f32[512,768]{1,0:T(8,128)}, f32[2,512,768]{2,1,0:T(8,128)}, f32[1024,768]{1,0:T(8,128)}) custom-call(s32[1]{0:T(128)} %bitcast.me_ref, bf16[1024,768]{1,0:T(8,128)(2,1)} %get-tuple-element.129.nh_ref, bf16[1024,768]{1,0:T(8,128)(2,1)} %get-tuple-element.130.nl_ref, f32[2,512,768]{2,1,0:T(8,128)} %ct_ref.7, ...), custom_call_target="tpu_custom_call" | custom-call | flops 14495514624 | bytes 31457280 | tf_op jit(solution)/shard_map/feed/pallas_call | solution.py:959
  233.1 60.0 %mixer_back.1 = (f32[512,768]{1,0:T(8,128)}, f32[2,512,768]{2,1,0:T(8,128)}, f32[1,4,104,768]{3,2,1,0:T(8,128)}, f32[1,4,104,768]{3,2,1,0:T(8,128)}) custom-call(s32[1]{0:T(128)} %bitcast.me_ref, f32[1024,768]{1,0:T(8,128)} %get-tuple-element.144.fng_ref, f32[1024,768]{1,0:T(8,128)} %get-tuple-element.132.out_in.fng_in.resid_ref, f32[2,512,768]{2,1,0:T(8,128)} %x_ref.5, ...), custom_call_target="tpu_custom_call" | custom-call | flops 99999997952 | bytes 62914560 | tf_op jit(solution)/shard_map/mixer_back/pallas_call | solution.py:834
  293.8 2.6 collective-permute-done.38
  296.5 1.0 fusion
  297.5 1.5 collective-permute-start.39
  298.9 1.3 add_bitcast_fusion
  300.2 4.3 %collective-permute-done.39 = f32[1,104,768]{2,1,0:T(8,128)S(1)} collective-permute-done((f32[1,104,768]{2,1,0:T(8,128)S(1)}, f32[1,104,768]{2,1,0:T(8,128)S(1)}, u32[]{:S(2)}, u32[]{:S(2)}) %collective-permute-start.39) | collective-permute-done | bytes 319520 | tf_op jit(solution)/shard_map/ppermute | solution.py:1028
  304.5 0.9 add_select_fusion.1
  305.4 1.1 collective-permute-start.41
  306.6 1.7 collective-permute-start.42
  308.2 1.9 slice_bitcast_fusion
  310.2 1.2 copy-done.2
  311.3 2.3 leave.2
  313.6 2.3 leave.3
  316.0 1.1 add_add_fusion
  (156 shorter events, 21.3 us)
Async XLA Ops:
  7.2 131.6 %all-gather.4.cloned.1.call-start = ((), (), s32[]{:S(2)}) async-start(), calls=%async_computation.1 | async-start | bytes 5308416 | tf_op jit(solution)/shard_map/all_gather | solution.py:1093
  9.3 33.4 %collective-permute-start = (f32[2,512,768]{2,1,0:T(8,128)}, f32[2,512,768]{2,1,0:T(8,128)}, u32[]{:S(2)}, u32[]{:S(2)}) collective-permute-start(f32[2,512,768]{2,1,0:T(8,128)} %x_ref.5), channel_id=1, source_target_pairs={{0,4},{4,0},{1,5},{5,1},{2,6},{6,2},{3,7},{7,3},{8,12},{12,8},{9,1... | collective-permute-start | bytes 9437192 | tf_op jit(solution)/shard_map/ppermute | solution.py:1020
  9.7 10.1 %collective-permute-start.4 = (f32[104,768]{1,0:T(8,128)}, f32[104,768]{1,0:T(8,128)S(1)}, u32[]{:S(2)}, u32[]{:S(2)}) collective-permute-start(f32[104,768]{1,0:T(8,128)} %pack_mixer.1.refs_0_), channel_id=1, source_target_pairs={{0,4},{4,0},{1,5},{5,1},{2,6},{6,2},{3,7},{7,3},{8,12},{12,8},{9,1... | collective-permute-start | bytes 958472 | tf_op jit(solution)/shard_map/ppermute | solution.py:1020
  9.8 10.9 %collective-permute-start.3 = (f32[104,768]{1,0:T(8,128)}, f32[104,768]{1,0:T(8,128)S(1)}, u32[]{:S(2)}, u32[]{:S(2)}) collective-permute-start(f32[104,768]{1,0:T(8,128)} %pack_mixer.1.refs_0_), channel_id=1, source_target_pairs={{0,16},{8,24},{16,0},{24,8},{1,17},{9,25},{17,1},{25,9},{2,18},{10... | collective-permute-start | bytes 958472 | tf_op jit(solution)/shard_map/ppermute | solution.py:1020
  12.8 9.4 %collective-permute-start.2 = (f32[104,768]{1,0:T(8,128)}, f32[104,768]{1,0:T(8,128)S(1)}, u32[]{:S(2)}, u32[]{:S(2)}) collective-permute-start(f32[104,768]{1,0:T(8,128)} %pack_mixer.1.refs_0_), channel_id=1, source_target_pairs={{0,8},{8,0},{16,24},{24,16},{1,9},{9,1},{17,25},{25,17},{2,10},{10... | collective-permute-start | bytes 958472 | tf_op jit(solution)/shard_map/ppermute | solution.py:1020
  14.3 9.2 %collective-permute-start.1 = (f32[104,768]{1,0:T(8,128)}, f32[104,768]{1,0:T(8,128)S(1)}, u32[]{:S(2)}, u32[]{:S(2)}) collective-permute-start(f32[104,768]{1,0:T(8,128)} %pack_mixer.1.refs_0_), channel_id=1, source_target_pairs={{0,1},{1,0},{2,3},{3,2},{4,5},{5,4},{6,7},{7,6},{8,9},{9,8},{10,11... | collective-permute-start | bytes 958472 | tf_op jit(solution)/shard_map/ppermute | solution.py:1020
  20.7 45.8 %copy-start.7 = (f32[104,768]{1,0:T(8,128)}, f32[104,768]{1,0:T(8,128)S(1)}, u32[]{:S(2)}) copy-start(f32[104,768]{1,0:T(8,128)S(1)} %collective-permute-done.3.refs_4_) | copy-start | bytes 958468
  23.5 10.3 %collective-permute-start.9 = (f32[104,768]{1,0:T(8,128)S(1)}, f32[104,768]{1,0:T(8,128)}, u32[]{:S(2)}, u32[]{:S(2)}) collective-permute-start(f32[104,768]{1,0:T(8,128)S(1)} %broadcast_select_fusion.3), channel_id=1, source_target_pairs={{0,16},{4,12},{8,24},{12,4},{16,0},{20,28},{24,8},{28,20},{1,17},{... | collective-permute-start | bytes 958472 | tf_op jit(solution)/shard_map/ppermute | solution.py:1028
  24.0 15.6 %collective-permute-start.5 = (f32[104,768]{1,0:T(8,128)S(1)}, f32[104,768]{1,0:T(8,128)S(1)}, u32[]{:S(2)}, u32[]{:S(2)}) collective-permute-start(f32[104,768]{1,0:T(8,128)S(1)} %copy-done.5), channel_id=1, source_target_pairs={{0,2},{1,3},{2,0},{3,1},{4,6},{5,7},{6,4},{7,5},{8,10},{9,11},{10,... | collective-permute-start | bytes 958472 | tf_op jit(solution)/shard_map/ppermute | solution.py:1020
  26.6 13.1 %collective-permute-start.7 = (f32[104,768]{1,0:T(8,128)S(1)}, f32[104,768]{1,0:T(8,128)S(1)}, u32[]{:S(2)}, u32[]{:S(2)}) collective-permute-start(f32[104,768]{1,0:T(8,128)S(1)} %collective-permute-done.1.refs_8_), channel_id=1, source_target_pairs={{0,16},{8,24},{16,0},{24,8},{1,17},{9,25},{17,1},{25,9},{2,18},{10... | collective-permute-start | bytes 958472 | tf_op jit(solution)/shard_map/ppermute | solution.py:1020
  28.2 5.6 %collective-permute-start.8 = (s32[2,512]{1,0:T(2,128)S(1)}, s32[2,512]{1,0:T(2,128)S(1)}, u32[]{:S(2)}, u32[]{:S(2)}) collective-permute-start(s32[2,512]{1,0:T(2,128)S(1)} %copy-done.14), channel_id=1, source_target_pairs={{0,4},{4,0},{1,5},{5,1},{2,6},{6,2},{3,7},{7,3},{8,12},{12,8},{9,1... | collective-permute-start | bytes 12296 | tf_op jit(solution)/shard_map/ppermute | solution.py:1020
  33.8 7.0 %collective-permute-start.6 = (f32[104,768]{1,0:T(8,128)S(1)}, f32[104,768]{1,0:T(8,128)S(1)}, u32[]{:S(2)}, u32[]{:S(2)}) collective-permute-start(f32[104,768]{1,0:T(8,128)S(1)} %collective-permute-done.1.refs_8_), channel_id=1, source_target_pairs={{0,8},{8,0},{16,24},{24,16},{1,9},{9,1},{17,25},{25,17},{2,10},{10... | collective-permute-start | bytes 958472 | tf_op jit(solution)/shard_map/ppermute | solution.py:1020
  33.8 7.0 %collective-permute-start.10 = (f32[104,768]{1,0:T(8,128)S(1)}, f32[104,768]{1,0:T(8,128)S(1)}, u32[]{:S(2)}, u32[]{:S(2)}) collective-permute-start(f32[104,768]{1,0:T(8,128)S(1)} %collective-permute-done.2.refs_2_), channel_id=1, source_target_pairs={{0,4},{4,0},{1,5},{5,1},{2,6},{6,2},{3,7},{7,3},{8,12},{12,8},{9,1... | collective-permute-start | bytes 958472 | tf_op jit(solution)/shard_map/ppermute | solution.py:1020
  39.7 1.6 collective-permute-start.11
  39.7 2.3 collective-permute-start.12
  42.8 7.1 %collective-permute-start.13 = (f32[104,768]{1,0:T(8,128)S(1)}, f32[104,768]{1,0:T(8,128)S(1)}, u32[]{:S(2)}, u32[]{:S(2)}) collective-permute-start(f32[104,768]{1,0:T(8,128)S(1)} %broadcast_select_fusion.2), channel_id=1, source_target_pairs={{0,16},{4,12},{8,24},{12,4},{16,0},{20,28},{24,8},{28,20},{1,17},{... | collective-permute-start | bytes 958472 | tf_op jit(solution)/shard_map/ppermute | solution.py:1028
  43.5 12.0 %collective-permute-start.15 = (f32[104,768]{1,0:T(8,128)S(1)}, f32[104,768]{1,0:T(8,128)S(1)}, u32[]{:S(2)}, u32[]{:S(2)}) collective-permute-start(f32[104,768]{1,0:T(8,128)S(1)} %copy-done.5), channel_id=1, source_target_pairs={{0,3},{1,2},{2,1},{3,0},{4,7},{5,6},{6,5},{7,4},{8,11},{9,10},{10,... | collective-permute-start | bytes 958472 | tf_op jit(solution)/shard_map/ppermute | solution.py:1020
  47.0 10.0 %collective-permute-start.17 = (f32[104,768]{1,0:T(8,128)}, f32[104,768]{1,0:T(8,128)S(1)}, u32[]{:S(2)}, u32[]{:S(2)}) collective-permute-start(f32[104,768]{1,0:T(8,128)} %copy-done.15), channel_id=1, source_target_pairs={{0,16},{8,24},{16,0},{24,8},{1,17},{9,25},{17,1},{25,9},{2,18},{10... | collective-permute-start | bytes 958472 | tf_op jit(solution)/shard_map/ppermute | solution.py:1020
  48.4 8.8 %collective-permute-start.16 = (f32[104,768]{1,0:T(8,128)}, f32[104,768]{1,0:T(8,128)S(1)}, u32[]{:S(2)}, u32[]{:S(2)}) collective-permute-start(f32[104,768]{1,0:T(8,128)} %copy-done.15), channel_id=1, source_target_pairs={{0,8},{8,0},{16,24},{24,16},{1,9},{9,1},{17,25},{25,17},{2,10},{10... | collective-permute-start | bytes 958472 | tf_op jit(solution)/shard_map/ppermute | solution.py:1020
  49.9 7.3 %collective-permute-start.18 = (f32[104,768]{1,0:T(8,128)S(1)}, f32[104,768]{1,0:T(8,128)S(1)}, u32[]{:S(2)}, u32[]{:S(2)}) collective-permute-start(f32[104,768]{1,0:T(8,128)S(1)} %collective-permute-done.6.refs_10_), channel_id=1, source_target_pairs={{0,4},{4,0},{1,5},{5,1},{2,6},{6,2},{3,7},{7,3},{8,12},{12,8},{9,1... | collective-permute-start | bytes 958472 | tf_op jit(solution)/shard_map/ppermute | solution.py:1020
  49.9 7.3 %collective-permute-start.19 = (f32[104,768]{1,0:T(8,128)S(1)}, f32[104,768]{1,0:T(8,128)S(1)}, u32[]{:S(2)}, u32[]{:S(2)}) collective-permute-start(f32[104,768]{1,0:T(8,128)S(1)} %collective-permute-done.7.refs_12_), channel_id=1, source_target_pairs={{0,4},{4,0},{1,5},{5,1},{2,6},{6,2},{3,7},{7,3},{8,12},{12,8},{9,1... | collective-permute-start | bytes 958472 | tf_op jit(solution)/shard_map/ppermute | solution.py:1020
  55.5 2.6 collective-permute-start.20
  58.1 112.5 %all-gather.6.cloned.1.call-start = ((), (), s32[]{:S(2)}) async-start(), calls=%async_computation.2 | async-start | bytes 10616832 | tf_op jit(solution)/shard_map/all_gather | solution.py:1093
  58.1 8.4 %collective-permute-start.22 = (f32[104,768]{1,0:T(8,128)}, f32[104,768]{1,0:T(8,128)}, u32[]{:S(2)}, u32[]{:S(2)}) collective-permute-start(f32[104,768]{1,0:T(8,128)} %copy-done.19), channel_id=1, source_target_pairs={{0,4},{4,0},{1,5},{5,1},{2,6},{6,2},{3,7},{7,3},{8,12},{12,8},{9,1... | collective-permute-start | bytes 958472 | tf_op jit(solution)/shard_map/ppermute | solution.py:1020
  59.8 21.1 %collective-permute-start.24 = (f32[104,768]{1,0:T(8,128)}, f32[104,768]{1,0:T(8,128)S(1)}, u32[]{:S(2)}, u32[]{:S(2)}) collective-permute-start(f32[104,768]{1,0:T(8,128)} %copy-done.17), channel_id=1, source_target_pairs={{0,16},{8,24},{16,0},{24,8},{1,17},{9,25},{17,1},{25,9},{2,18},{10... | collective-permute-start | bytes 958472 | tf_op jit(solution)/shard_map/ppermute | solution.py:1020
  61.4 19.5 %collective-permute-start.23 = (f32[104,768]{1,0:T(8,128)}, f32[104,768]{1,0:T(8,128)S(1)}, u32[]{:S(2)}, u32[]{:S(2)}) collective-permute-start(f32[104,768]{1,0:T(8,128)} %copy-done.17), channel_id=1, source_target_pairs={{0,8},{8,0},{16,24},{24,16},{1,9},{9,1},{17,25},{25,17},{2,10},{10... | collective-permute-start | bytes 958472 | tf_op jit(solution)/shard_map/ppermute | solution.py:1020
  62.0 29.4 %collective-permute-start.30 = (f32[96,1536]{1,0:T(8,128)S(1)}, f32[96,1536]{1,0:T(8,128)S(1)}, u32[]{:S(2)}, u32[]{:S(2)}) collective-permute-start(f32[96,1536]{1,0:T(8,128)S(1)} %copy-done), channel_id=1, source_target_pairs={{0,2},{1,3},{2,0},{3,1},{4,6},{5,7},{6,4},{7,5},{8,10},{9,11},{10,... | collective-permute-start | bytes 1769480 | tf_op jit(solution)/shard_map/ppermute | solution.py:1020
  65.4 26.0 %collective-permute-start.29 = (f32[96,1536]{1,0:T(8,128)S(1)}, f32[96,1536]{1,0:T(8,128)S(1)}, u32[]{:S(2)}, u32[]{:S(2)}) collective-permute-start(f32[96,1536]{1,0:T(8,128)S(1)} %copy-done), channel_id=1, source_target_pairs={{0,1},{1,0},{2,3},{3,2},{4,5},{5,4},{6,7},{7,6},{8,9},{9,8},{10,11... | collective-permute-start | bytes 1769480 | tf_op jit(solution)/shard_map/ppermute | solution.py:1020
  66.6 14.3 %collective-permute-start.21 = (f32[104,768]{1,0:T(8,128)}, f32[104,768]{1,0:T(8,128)S(1)}, u32[]{:S(2)}, u32[]{:S(2)}) collective-permute-start(f32[104,768]{1,0:T(8,128)} %broadcast_select_fusion.1), channel_id=1, source_target_pairs={{0,16},{4,12},{8,24},{12,4},{16,0},{20,28},{24,8},{28,20},{1,17},{... | collective-permute-start | bytes 958472 | tf_op jit(solution)/shard_map/ppermute | solution.py:1028
  81.6 9.8 %collective-permute-start.31 = (f32[104,768]{1,0:T(8,128)S(1)}, f32[104,768]{1,0:T(8,128)S(1)}, u32[]{:S(2)}, u32[]{:S(2)}) collective-permute-start(f32[104,768]{1,0:T(8,128)S(1)} %broadcast_select_fusion), channel_id=1, source_target_pairs={{0,16},{4,12},{8,24},{12,4},{16,0},{20,28},{24,8},{28,20},{1,17},{... | collective-permute-start | bytes 958472 | tf_op jit(solution)/shard_map/ppermute | solution.py:1028
  93.4 117.2 %all-gather.8.cloned.1.call-start = ((), (), s32[]{:S(2)}) async-start(), calls=%async_computation.3 | async-start | bytes 5308416 | tf_op jit(solution)/shard_map/all_gather | solution.py:1093
  93.6 42.0 %collective-permute-start.35 = (f32[2,512,768]{2,1,0:T(8,128)}, f32[2,512,768]{2,1,0:T(8,128)}, u32[]{:S(2)}, u32[]{:S(2)}) collective-permute-start(f32[2,512,768]{2,1,0:T(8,128)} %ct_ref.7), channel_id=1, source_target_pairs={{0,4},{4,0},{1,5},{5,1},{2,6},{6,2},{3,7},{7,3},{8,12},{12,8},{9,1... | collective-permute-start | bytes 9437192 | tf_op jit(solution)/shard_map/ppermute | solution.py:1020
  93.7 4.4 %collective-permute-start.14 = (f32[104,768]{1,0:T(8,128)S(1)}, f32[104,768]{1,0:T(8,128)S(1)}, u32[]{:S(2)}, u32[]{:S(2)}) collective-permute-start(f32[104,768]{1,0:T(8,128)S(1)} %copy-done.16), channel_id=1, source_target_pairs={{0,4},{4,0},{1,5},{5,1},{2,6},{6,2},{3,7},{7,3},{8,12},{12,8},{9,1... | collective-permute-start | bytes 958472 | tf_op jit(solution)/shard_map/ppermute | solution.py:1020
  94.2 4.9 %collective-permute-start.25 = (f32[104,768]{1,0:T(8,128)S(1)}, f32[104,768]{1,0:T(8,128)S(1)}, u32[]{:S(2)}, u32[]{:S(2)}) collective-permute-start(f32[104,768]{1,0:T(8,128)S(1)} %collective-permute-done.16.refs_2_), channel_id=1, source_target_pairs={{0,4},{4,0},{1,5},{5,1},{2,6},{6,2},{3,7},{7,3},{8,12},{12,8},{9,1... | collective-permute-start | bytes 958472 | tf_op jit(solution)/shard_map/ppermute | solution.py:1020
  94.3 5.7 %collective-permute-start.26 = (f32[104,768]{1,0:T(8,128)S(1)}, f32[104,768]{1,0:T(8,128)S(1)}, u32[]{:S(2)}, u32[]{:S(2)}) collective-permute-start(f32[104,768]{1,0:T(8,128)S(1)} %collective-permute-done.17.refs_4_), channel_id=1, source_target_pairs={{0,4},{4,0},{1,5},{5,1},{2,6},{6,2},{3,7},{7,3},{8,12},{12,8},{9,1... | collective-permute-start | bytes 958472 | tf_op jit(solution)/shard_map/ppermute | solution.py:1020
  94.7 5.6 %collective-permute-start.27 = (f32[104,768]{1,0:T(8,128)}, f32[104,768]{1,0:T(8,128)S(1)}, u32[]{:S(2)}, u32[]{:S(2)}) collective-permute-start(f32[104,768]{1,0:T(8,128)} %copy-done.20), channel_id=1, source_target_pairs={{0,4},{4,0},{1,5},{5,1},{2,6},{6,2},{3,7},{7,3},{8,12},{12,8},{9,1... | collective-permute-start | bytes 958472 | tf_op jit(solution)/shard_map/ppermute | solution.py:1020
  98.1 3.8 %collective-permute-start.28 = (f32[104,768]{1,0:T(8,128)}, f32[104,768]{1,0:T(8,128)S(1)}, u32[]{:S(2)}, u32[]{:S(2)}) collective-permute-start(f32[104,768]{1,0:T(8,128)} %copy-done.17), channel_id=1, source_target_pairs={{0,4},{4,0},{1,5},{5,1},{2,6},{6,2},{3,7},{7,3},{8,12},{12,8},{9,1... | collective-permute-start | bytes 958472 | tf_op jit(solution)/shard_map/ppermute | solution.py:1020
  99.0 2.8 collective-permute-start.32
  100.0 2.8 collective-permute-start.33
  100.3 4.1 %collective-permute-start.34 = (f32[104,768]{1,0:T(8,128)}, f32[104,768]{1,0:T(8,128)}, u32[]{:S(2)}, u32[]{:S(2)}) collective-permute-start(f32[104,768]{1,0:T(8,128)} %copy-done.24), channel_id=1, source_target_pairs={{0,4},{4,0},{1,5},{5,1},{2,6},{6,2},{3,7},{7,3},{8,12},{12,8},{9,1... | collective-permute-start | bytes 958472 | tf_op jit(solution)/shard_map/ppermute | solution.py:1020
  135.6 33.5 %collective-permute-start.36 = (f32[96,1536]{1,0:T(8,128)S(1)}, f32[96,1536]{1,0:T(8,128)S(1)}, u32[]{:S(2)}, u32[]{:S(2)}) collective-permute-start(f32[96,1536]{1,0:T(8,128)S(1)} %copy-done), channel_id=1, source_target_pairs={{0,3},{1,2},{2,1},{3,0},{4,7},{5,6},{6,5},{7,4},{8,11},{9,10},{10,... | collective-permute-start | bytes 1769480 | tf_op jit(solution)/shard_map/ppermute | solution.py:1020
  170.0 138.2 %reduce-scatter.2.cloned.1.call-start = ((), (), s32[]{:S(2)}) async-start(), calls=%async_computation.4 | async-start | bytes 5308416 | tf_op jit(solution)/shard_map/reduce_scatter | solution.py:1163
  293.2 3.3 collective-permute-start.38
  293.3 7.0 %collective-permute-start.40 = (f32[512,768]{1,0:T(8,128)}, f32[512,768]{1,0:T(8,128)S(1)}, u32[]{:S(2)}, u32[]{:S(2)}) collective-permute-start(f32[512,768]{1,0:T(8,128)} %get-tuple-element.155), channel_id=1, source_target_pairs={{0,4},{4,0},{1,5},{5,1},{2,6},{6,2},{3,7},{7,3},{8,12},{12,8},{9,1... | collective-permute-start | bytes 4718600 | tf_op jit(solution)/shard_map/ppermute | solution.py:1020
  293.8 16.4 %collective-permute-start.37 = (f32[512,768]{1,0:T(8,128)}, f32[512,768]{1,0:T(8,128)S(1)}, u32[]{:S(2)}, u32[]{:S(2)}) collective-permute-start(f32[512,768]{1,0:T(8,128)} %get-tuple-element.142), channel_id=1, source_target_pairs={{0,4},{4,0},{1,5},{5,1},{2,6},{6,2},{3,7},{7,3},{8,12},{12,8},{9,1... | collective-permute-start | bytes 4718600 | tf_op jit(solution)/shard_map/ppermute | solution.py:1020
  297.5 7.1 %collective-permute-start.39 = (f32[1,104,768]{2,1,0:T(8,128)S(1)}, f32[1,104,768]{2,1,0:T(8,128)S(1)}, u32[]{:S(2)}, u32[]{:S(2)}) collective-permute-start(f32[1,104,768]{2,1,0:T(8,128)S(1)} %fusion), channel_id=1, source_target_pairs={{0,16},{4,12},{8,24},{12,4},{16,0},{20,28},{24,8},{28,20},{1,17},{... | collective-permute-start | bytes 958472 | tf_op jit(solution)/shard_map/ppermute | solution.py:1028
  305.4 10.5 %collective-permute-start.41 = (f32[1,104,768]{2,1,0:T(8,128)}, f32[1,104,768]{2,1,0:T(8,128)}, u32[]{:S(2)}, u32[]{:S(2)}) collective-permute-start(f32[1,104,768]{2,1,0:T(8,128)} %get-tuple-element.190), channel_id=1, source_target_pairs={{0,8},{8,0},{16,24},{24,16},{1,9},{9,1},{17,25},{25,17},{2,10},{10... | collective-permute-start | bytes 958472 | tf_op jit(solution)/shard_map/ppermute | solution.py:1020
  306.6 9.4 %collective-permute-start.42 = (f32[1,104,768]{2,1,0:T(8,128)}, f32[1,104,768]{2,1,0:T(8,128)}, u32[]{:S(2)}, u32[]{:S(2)}) collective-permute-start(f32[1,104,768]{2,1,0:T(8,128)} %get-tuple-element.191), channel_id=1, source_target_pairs={{0,16},{8,24},{16,0},{24,8},{1,17},{9,25},{17,1},{25,9},{2,18},{10... | collective-permute-start | bytes 958472 | tf_op jit(solution)/shard_map/ppermute | solution.py:1020
  (35 other events, 363.3 us)
Sparse Core Ops, SparseCore 0:
  58.2 45.8 all-gather.3
  106.0 59.1 all-gather.5
  170.1 38.8 all-gather.7
  212.3 53.8 reduce-scatter.1
